TPU v7x, 512 devices: a whole 4x4x16 slice. The times are simulated.
512 devices in a mesh: section: 16 (over y, x), expert: 32 (over z, core).
Axes of the slice: x: 4, y: 4, z: 16, core: 2. Of those that a mesh axis runs over, the one named last changes fastest.
Arguments:
- activations: bfloat16 [2, 32768, 4096], P(None, ('section', 'expert')), may hold values from -6 to 6
- expert_ids: int32 [2, 2, 32768, 8], P(None, None, ('section', 'expert')), may hold values from 0 to 127, all different within a row; in each aligned block of 64 rows (0 to 63, 64 to 127, ..., all dimensions but the last counted through in order) at most 6 rows name the same one
- gate_values: float32 [2, 2, 32768, 8], P(None, None, ('section', 'expert')), may hold values from 0.1 to 1
- w_gate: bfloat16 [16, 4096, 4096], P('section', None, 'expert'), may hold values from -0.09375 to 0.09375
- w_up: bfloat16 [16, 4096, 4096], P('section', None, 'expert'), may hold values from -0.09375 to 0.09375
- w_down: bfloat16 [16, 4096, 4096], P('section', 'expert'), may hold values from -0.75 to 0.75
Outputs:
- carried: bfloat16 [2, 32768, 4096], P(None, ('section', 'expert'))
Inputs may be any that keep to these rules, and one draw needn't show every extreme that they name: `expert_ids`: each token's 8 ids are different experts. In each aligned block of 64 rows (one device's tokens of one direction at one step) no expert is named by more than 6 rows, a bound that some block reaches.
All inputs are finite; a program needn't handle non-finite values.
Results may differ from a plain program's by a relative error of at most 0.012.
Values may be sent and summed in bfloat16 or wider, within the bound.
No kernel may reach another device: no remote copies, remote signals or barrier semaphores. Data moves between devices by JAX's collectives and lax.ppermute only.
A program may use at most 64 MiB of HBM per device.

v0:
```python
import jax
import jax.numpy as jnp
from jax import lax
from jax.sharding import PartitionSpec as P

HE = 1024
MOST = 6
STEPS = 2


def shifted(value, axis, steps):
    count = lax.axis_size(axis)
    pairs = [(source, (source + steps) % count) for source in range(count)]
    return lax.ppermute(value, axis, pairs)


def route_tables(ids, gates, expert_window, most):
    norm = gates / jnp.sum(gates, axis=-1, keepdims=True)
    picks = ids[..., None] == jnp.arange(expert_window, dtype=jnp.int32)
    member = jnp.any(picks, axis=-2).astype(jnp.int32)
    weight_matrix = jnp.sum(jnp.where(picks, norm[..., None], 0.0), axis=-2)
    rank = jnp.cumsum(member, axis=-2) - member
    placement_slot = (rank[..., None] == jnp.arange(most, dtype=jnp.int32)) & (
        member[..., None] > 0
    )
    return (placement_slot.astype(jnp.float32), weight_matrix)


def body(activations, expert_ids, gate_values, w_gate, w_up, w_down):
    width = activations.shape[2]
    split = HE // w_gate.shape[2]
    expert_window = lax.axis_size("expert") // split
    wg = w_gate[0]
    wu = w_up[0]
    wd = w_down[0]
    carry_state = activations
    for step in range(STEPS):
        placement_slot, weight_matrix = route_tables(
            expert_ids[step], gate_values[step], expert_window, MOST
        )
        listed = jnp.einsum(
            "inxv,inb->xivb",
            placement_slot.astype(jnp.bfloat16),
            carry_state,
            preferred_element_type=jnp.float32,
        ).astype(jnp.bfloat16)
        copies = jnp.repeat(listed, split, axis=0)
        received = lax.all_to_all(copies, "expert", split_axis=0, concat_axis=0, tiled=True)
        flat = received.reshape(-1, width)
        gate_part = jnp.dot(flat, wg, preferred_element_type=jnp.float32)
        up_projection = jnp.dot(flat, wu, preferred_element_type=jnp.float32)
        hidden = (jax.nn.silu(gate_part) * up_projection).astype(jnp.bfloat16)
        partial_value = jnp.dot(hidden, wd, preferred_element_type=jnp.float32).astype(jnp.bfloat16)
        done = partial_value.reshape(received.shape)
        back = lax.all_to_all(done, "expert", split_axis=0, concat_axis=0, tiled=True)
        output_rows = jnp.sum(
            back.astype(jnp.float32).reshape(expert_window, split, 2, MOST, width), axis=1
        )
        mixture_weights = placement_slot * weight_matrix[..., None]
        mixture_of_experts = jnp.einsum(
            "ghjz,jgzi->ghi", mixture_weights, output_rows, precision=lax.Precision.HIGHEST
        )
        updated = (carry_state.astype(jnp.float32) + mixture_of_experts).astype(jnp.bfloat16)
        ahead = shifted(updated[0], "section", 1)
        behind = shifted(updated[1], "section", -1)
        carry_state = jnp.stack([ahead, behind])
    return carry_state


def solution(mesh):
    placed = (
        P(None, ("section", "expert"), None),
        P(None, None, ("section", "expert"), None),
        P(None, None, ("section", "expert"), None),
        P("section", None, "expert"),
        P("section", None, "expert"),
        P("section", "expert", None),
    )
    return jax.shard_map(
        body,
        mesh=mesh,
        in_specs=placed,
        out_specs=P(None, ("section", "expert"), None),
        check_vma=False,
    )
```

profile of v0, /device:TPU:62, one launch (start us, length us, event | category | flops | bytes accessed | tf_op | source)
XLA Modules:
  0.0 750.4 jit_solution(697645252773429722)
XLA Ops:
  0.0 0.8 slice_bitcast_fusion.4
  0.8 0.1 copy.45
  1.0 0.1 copy.47
  1.1 0.1 reduce_window_sum.17
  1.2 0.1 copy.46
  1.3 1.5 fusion.2
  2.8 0.4 copy.48
  3.2 3.2 broadcast_in_dim.40
  6.4 159.4 %all_to_all.20 = bf16[32,2,6,4096]{3,1,2,0:T(2,128)(2,1)S(1)} all-to-all(bf16[32,2,6,4096]{3,1,2,0:T(2,128)(2,1)S(1)} %bitcast.75), channel_id=1, replica_groups=mesh['section'=16,'expert'=32] {'expert'}, dimensions={0} | all-to-all | bytes 6291456 | tf_op jit(solution)/shard_map/all_to_all | solution.py:48
  165.8 4.4 copy.49
  170.2 5.8 reshape.79
  176.0 3.0 fusion.20
  179.0 7.0 convolution_convert_fusion.1
  186.0 5.6 reshape.80
  191.6 7.2 copy.50
  198.8 7.4 all-to-all-start.1
  206.2 145.1 %all-to-all-done.1 = bf16[32,2,6,4096]{3,1,2,0:T(2,128)(2,1)} async-done(((bf16[32,2,6,4096]{3,1,2,0:T(2,128)(2,1)}), bf16[32,2,6,4096]{3,1,2,0:T(2,128)(2,1)}, u32[]{:S(2)}, u32[]{:S(2)}) %all-to-all-start.1) | async-done | bytes 3145760 | tf_op jit(solution)/shard_map/all_to_all | solution.py:55
  351.3 5.8 convert_reduce_fusion.1
  357.2 2.4 fusion.1
  359.6 1.1 slice_bitcast_fusion.3
  360.7 2.0 collective-permute-start
  362.7 3.8 collective-permute-start.1
  366.5 0.1 copy.53
  366.7 0.1 copy.55
  366.8 0.1 reduce_window_sum.18
  366.9 0.1 copy.54
  367.0 9.4 %collective-permute-done = bf16[64,4096]{1,0:T(8,128)(2,1)} collective-permute-done((bf16[64,4096]{1,0:T(8,128)(2,1)}, bf16[64,4096]{1,0:T(8,128)(2,1)}, u32[]{:S(2)}, u32[]{:S(2)}) %collective-permute-start) | collective-permute-done | bytes 524320 | tf_op jit(solution)/shard_map/ppermute | solution.py:14
  376.3 5.2 collective-permute-done.1
  381.6 1.5 fusion.3
  383.1 0.4 copy.56
  383.5 3.2 broadcast_in_dim.42
  386.7 147.6 %all_to_all.21 = bf16[32,2,6,4096]{3,1,2,0:T(2,128)(2,1)S(1)} all-to-all(bf16[32,2,6,4096]{3,1,2,0:T(2,128)(2,1)S(1)} %bitcast.76), channel_id=1, replica_groups=mesh['section'=16,'expert'=32] {'expert'}, dimensions={0} | all-to-all | bytes 6291456 | tf_op jit(solution)/shard_map/all_to_all | solution.py:48
  534.3 4.3 copy.57
  538.6 5.7 reshape.84
  544.3 2.9 fusion.18
  547.2 7.0 convolution_convert_fusion
  554.2 5.7 reshape.85
  559.8 7.1 copy.58
  567.0 6.9 all-to-all-start.3
  573.9 145.1 %all-to-all-done.3 = bf16[32,2,6,4096]{3,1,2,0:T(2,128)(2,1)} async-done(((bf16[32,2,6,4096]{3,1,2,0:T(2,128)(2,1)}), bf16[32,2,6,4096]{3,1,2,0:T(2,128)(2,1)}, u32[]{:S(2)}, u32[]{:S(2)}) %all-to-all-start.3) | async-done | bytes 3145760 | tf_op jit(solution)/shard_map/all_to_all | solution.py:55
  719.1 5.7 convert_reduce_fusion
  724.8 3.6 add_convert_fusion
  728.4 0.1 slice_bitcast_fusion.1
  728.5 1.9 collective-permute-start.2
  730.4 3.9 collective-permute-start.3
  734.4 9.5 %collective-permute-done.2 = bf16[64,4096]{1,0:T(8,128)(2,1)S(1)} collective-permute-done((bf16[64,4096]{1,0:T(8,128)(2,1)S(1)}, bf16[64,4096]{1,0:T(8,128)(2,1)S(1)}, u32[]{:S(2)}, u32[]{:S(2)}) %collective-permute-start.2) | collective-permute-done | bytes 524320 | tf_op jit(solution)/shard_map/ppermute | solution.py:14
  743.9 5.2 collective-permute-done.3
  749.1 1.1 pad_maximum_fusion.1
  (19 shorter events, 0.2 us)
Async XLA Ops:
  0.0 179.0 %copy-start = (bf16[1,128,4096]{2,1,0:T(8,128)(2,1)S(1)}, bf16[1,128,4096]{2,1,0:T(8,128)(2,1)}, u32[]{:S(2)}) copy-start(bf16[1,128,4096]{2,1,0:T(8,128)(2,1)} %param.11) | copy-start | bytes 3145732
  170.2 5.8 copy-start.1
  176.0 3.0 copy-start.2
  198.8 7.4 copy-start.4
  198.8 152.5 %all-to-all-start.1 = ((bf16[32,2,6,4096]{3,1,2,0:T(2,128)(2,1)}), bf16[32,2,6,4096]{3,1,2,0:T(2,128)(2,1)}, u32[]{:S(2)}, u32[]{:S(2)}) async-start(bf16[32,2,6,4096]{3,1,2,0:T(2,128)(2,1)} %copy.50), calls=%async_computation.1 | async-start | bytes 6291456 | tf_op jit(solution)/shard_map/all_to_all | solution.py:55
  351.3 5.8 copy-start.3
  360.7 15.7 %collective-permute-start = (bf16[64,4096]{1,0:T(8,128)(2,1)}, bf16[64,4096]{1,0:T(8,128)(2,1)}, u32[]{:S(2)}, u32[]{:S(2)}) collective-permute-start(bf16[64,4096]{1,0:T(8,128)(2,1)} %get-tuple-element.9), channel_id=1, source_target_pairs={{0,32},{32,64},{64,96},{96,128},{128,160},{160,192},{192,224},{224... | collective-permute-start | bytes 1572872 | tf_op jit(solution)/shard_map/ppermute | solution.py:14
  362.7 18.9 %collective-permute-start.1 = (bf16[64,4096]{1,0:T(8,128)(2,1)}, bf16[64,4096]{1,0:T(8,128)(2,1)}, u32[]{:S(2)}, u32[]{:S(2)}) collective-permute-start(bf16[64,4096]{1,0:T(8,128)(2,1)} %get-tuple-element.10), channel_id=1, source_target_pairs={{0,480},{32,0},{64,32},{96,64},{128,96},{160,128},{192,160},{224,1... | collective-permute-start | bytes 1572872 | tf_op jit(solution)/shard_map/ppermute | solution.py:14
  567.0 152.1 %all-to-all-start.3 = ((bf16[32,2,6,4096]{3,1,2,0:T(2,128)(2,1)}), bf16[32,2,6,4096]{3,1,2,0:T(2,128)(2,1)}, u32[]{:S(2)}, u32[]{:S(2)}) async-start(bf16[32,2,6,4096]{3,1,2,0:T(2,128)(2,1)} %copy.58), calls=%async_computation.3 | async-start | bytes 6291456 | tf_op jit(solution)/shard_map/all_to_all | solution.py:55
  728.5 15.4 %collective-permute-start.2 = (bf16[64,4096]{1,0:T(8,128)(2,1)S(1)}, bf16[64,4096]{1,0:T(8,128)(2,1)S(1)}, u32[]{:S(2)}, u32[]{:S(2)}) collective-permute-start(bf16[64,4096]{1,0:T(8,128)(2,1)S(1)} %get-tuple-element.7), channel_id=1, source_target_pairs={{0,32},{32,64},{64,96},{96,128},{128,160},{160,192},{192,224},{224... | collective-permute-start | bytes 1572872 | tf_op jit(solution)/shard_map/ppermute | solution.py:14
  730.4 18.7 %collective-permute-start.3 = (bf16[64,4096]{1,0:T(8,128)(2,1)S(1)}, bf16[64,4096]{1,0:T(8,128)(2,1)S(1)}, u32[]{:S(2)}, u32[]{:S(2)}) collective-permute-start(bf16[64,4096]{1,0:T(8,128)(2,1)S(1)} %get-tuple-element.8), channel_id=1, source_target_pairs={{0,480},{32,0},{64,32},{96,64},{128,96},{160,128},{192,160},{224,1... | collective-permute-start | bytes 1572872 | tf_op jit(solution)/shard_map/ppermute | solution.py:14
where the time goes:
time: 754 us; the launch traced here: 750 us
  waiting for transfers between devices  320 us (42%)
  blocking collectives  307 us (41%)
  local copies, waits for them, and re-layouts  55.5 us (7%)
  matrix products  28.8 us (4%)
  starting transfers between devices  26 us (3%)
  other arithmetic  13 us (2%)
    all_to_all x2, blocking collectives, body(): lax.all_to_all(copies, 'expert', split_axis=0, concat_axis=0, tiled=True)  307 us
    all_to_all x2, waiting for transfers between devices, body(): lax.all_to_all(done, 'expert', split_axis=0, concat_axis=0, tiled=True)  290 us
    ppermute x4, waiting for transfers between devices, shifted(): return lax.ppermute(value, axis, pairs)  29.4 us
    reshape x4, local copies, waits for them, and re-layouts, body(): done = partial_value.reshape(received.shape)  25.6 us
  transfers between devices with their start and end apart: 6, of which 6 were waited for; matrix products, arithmetic and copies ran while one was open for 0% of the time, Pallas kernels for 0%

commit v1 on v0

v1 whole, which is shorter than its diff:
```python
import functools

import jax
import jax.numpy as jnp
from jax import lax
from jax.experimental import pallas as pl
from jax.experimental.pallas import tpu as pltpu
from jax.sharding import PartitionSpec as P

MOST = 6
STEPS = 2
ROWS = 64
DIRS = 2
GROUPS = 4
CHIPS = 4
CORES = 2
FOLD = 2
PART = FOLD * DIRS * MOST
PARAMS = pltpu.CompilerParams(vmem_limit_bytes=48 * 1024 * 1024)


def device_at(g, m, c):
    return (g * CHIPS + m) * CORES + c


def pairs_of(place):
    pairs = []
    for g in range(GROUPS):
        for m in range(CHIPS):
            for c in range(CORES):
                pairs.append((device_at(g, m, c), device_at(*place(g, m, c))))
    return pairs


def group_shift(value, k):
    return lax.ppermute(value, "expert", pairs_of(lambda g, m, c: ((g + k) % GROUPS, m, c)))


def chip_shift(value, k):
    return lax.ppermute(value, "expert", pairs_of(lambda g, m, c: (g, (m + k) % CHIPS, c)))


def core_swap(value):
    return lax.ppermute(value, "expert", pairs_of(lambda g, m, c: (g, m, 1 - c)))


def section_shift(value, steps):
    count = lax.axis_size("section")
    return lax.ppermute(value, "section", [(s, (s + steps) % count) for s in range(count)])


def route_tables(ids, gates, group):
    norm = gates / jnp.sum(gates, axis=-1, keepdims=True)
    names = (group + jnp.arange(GROUPS, dtype=jnp.int32)) % GROUPS
    picks = ids[..., None] == names
    member = jnp.any(picks, axis=-2).astype(jnp.int32)
    weight = jnp.sum(jnp.where(picks, norm[..., None], 0.0), axis=-2)
    rank = jnp.cumsum(member, axis=-2) - member
    slot = (rank[..., None] == jnp.arange(MOST, dtype=jnp.int32)) & (member[..., None] > 0)
    slot = slot.astype(jnp.float32)
    fold = jnp.eye(FOLD, dtype=jnp.float32)
    way = jnp.eye(DIRS, dtype=jnp.float32)
    listing = jnp.einsum("dtks,qp,de->kqdspet", slot, fold, way, precision=lax.Precision.HIGHEST)
    mixing = jnp.einsum(
        "dtks,qp,de->qdtkpes", slot * weight[..., None], fold, way, precision=lax.Precision.HIGHEST
    )
    listing = listing.reshape(GROUPS * PART, FOLD * DIRS * ROWS).astype(jnp.bfloat16)
    mixing = mixing.reshape(FOLD * DIRS * ROWS, GROUPS * PART)
    high = mixing.astype(jnp.bfloat16)
    low = (mixing - high.astype(jnp.float32)).astype(jnp.bfloat16)
    return listing, jnp.concatenate([high, low], axis=1)


def stacked(states, width):
    return jnp.concatenate(
        [state[:, q * width : (q + 1) * width] for q in range(FOLD) for state in states], axis=0
    )


def list_kernel(listing_ref, *refs):
    states = [ref[...] for ref in refs[:DIRS]]
    outs = refs[DIRS:]
    width = outs[0].shape[1]
    rows = jnp.dot(listing_ref[...], stacked(states, width), preferred_element_type=jnp.float32)
    for k, out in enumerate(outs):
        out[...] = rows[k * PART : (k + 1) * PART].astype(jnp.bfloat16)


def list_rows(listing, states):
    width = states[0].shape[1] // FOLD
    return pl.pallas_call(
        list_kernel,
        out_shape=[jax.ShapeDtypeStruct((PART, width), jnp.bfloat16)] * GROUPS,
        compiler_params=PARAMS,
    )(listing, *states)


def expert_kernel(gate_up_ref, down_ref, *refs):
    ins, outs = refs[:CHIPS], refs[CHIPS:]
    rows_each, width = ins[0].shape
    hidden_units = down_ref.shape[0]
    total = rows_each * CHIPS
    rows = jnp.concatenate([ref[...] for ref in ins], axis=0)
    place = lax.broadcasted_iota(jnp.int32, (total, 1), 0)
    piece = (place % PART) // (PART // FOLD)
    sums = jnp.zeros((total, 2 * hidden_units), jnp.float32)
    for q in range(FOLD):
        part = jnp.dot(
            rows, gate_up_ref[q * width : (q + 1) * width], preferred_element_type=jnp.float32
        )
        sums = sums + jnp.where(piece == q, part, 0.0)
    one = lax.broadcasted_iota(jnp.int32, (rows_each, rows_each), 0)
    two = lax.broadcasted_iota(jnp.int32, (rows_each, rows_each), 1)
    step = PART // FOLD
    same = ((one // PART) == (two // PART)) & ((one % step) == (two % step))
    same = same.astype(jnp.float32)
    hidden = []
    for n in range(CHIPS):
        both = jnp.dot(
            same,
            sums[n * rows_each : (n + 1) * rows_each],
            precision=lax.Precision.HIGHEST,
            preferred_element_type=jnp.float32,
        )
        gate, up = both[:, :hidden_units], both[:, hidden_units:]
        hidden.append(jax.nn.silu(gate) * up)
    hidden = jnp.concatenate(hidden, axis=0)
    result = jnp.zeros((total, width), jnp.float32)
    for q in range(FOLD):
        chosen = jnp.where(piece == q, hidden, 0.0).astype(jnp.bfloat16)
        result = result + jnp.dot(
            chosen, down_ref[:, q * width : (q + 1) * width], preferred_element_type=jnp.float32
        )
    for n, out in enumerate(outs):
        out[...] = result[n * rows_each : (n + 1) * rows_each].astype(jnp.bfloat16)


def expert_rows(gate_up, down, rows):
    return pl.pallas_call(
        expert_kernel,
        out_shape=[jax.ShapeDtypeStruct(rows[0].shape, jnp.bfloat16)] * CHIPS,
        compiler_params=PARAMS,
    )(gate_up, down, *rows)


def sum_kernel(*refs):
    ins, outs = refs[:CHIPS], refs[CHIPS:]
    total = ins[0][...].astype(jnp.float32)
    for ref in ins[1:]:
        total = total + ref[...].astype(jnp.float32)
    for k, out in enumerate(outs):
        out[...] = total[k * PART : (k + 1) * PART].astype(jnp.bfloat16)


def sum_rows(parts):
    width = parts[0].shape[1]
    return pl.pallas_call(
        sum_kernel,
        out_shape=[jax.ShapeDtypeStruct((PART, width), jnp.bfloat16)] * GROUPS,
        compiler_params=PARAMS,
    )(*parts)


def mix_kernel(mixing_ref, *refs):
    states = [ref[...] for ref in refs[:DIRS]]
    rows = [ref[...].astype(jnp.float32) for ref in refs[DIRS : DIRS + GROUPS]]
    outs = refs[DIRS + GROUPS :]
    width = rows[0].shape[1]
    rows = jnp.concatenate(rows, axis=0).astype(jnp.bfloat16)
    half = GROUPS * PART
    mixed = jnp.dot(mixing_ref[:, :half], rows, preferred_element_type=jnp.float32)
    mixed = mixed + jnp.dot(mixing_ref[:, half:], rows, preferred_element_type=jnp.float32)
    for q in range(FOLD):
        for d, out in enumerate(outs):
            start = (q * DIRS + d) * ROWS
            old = states[d][:, q * width : (q + 1) * width].astype(jnp.float32)
            out[:, q * width : (q + 1) * width] = (old + mixed[start : start + ROWS]).astype(
                jnp.bfloat16
            )


def mix_rows(mixing, states, rows):
    return pl.pallas_call(
        mix_kernel,
        out_shape=[jax.ShapeDtypeStruct(states[0].shape, jnp.bfloat16)] * DIRS,
        compiler_params=PARAMS,
    )(mixing, *states, *rows)


def body(activations, expert_ids, gate_values, w_gate, w_up, w_down):
    group = lax.axis_index("expert") // (CHIPS * CORES)
    tables = [route_tables(expert_ids[s], gate_values[s], group) for s in range(STEPS)]
    gate_up = jnp.concatenate([w_gate[0], core_swap(w_gate[0]), w_up[0], core_swap(w_up[0])], axis=1)
    down = jnp.concatenate([w_down[0], core_swap(w_down[0])], axis=0)
    states = [activations[d] for d in range(DIRS)]
    for step in range(STEPS):
        listing, mixing = tables[step]
        sent = list_rows(listing, states)
        held = jnp.concatenate(
            [group_shift(sent[k], k) if k else sent[0] for k in range(GROUPS)], axis=0
        )
        rows = [chip_shift(held, k) if k else held for k in range(CHIPS)]
        done = expert_rows(gate_up, down, rows)
        parts = [chip_shift(done[k], -k) if k else done[0] for k in range(CHIPS)]
        summed = sum_rows(parts)
        back = [group_shift(summed[k], -k) if k else summed[0] for k in range(GROUPS)]
        updated = mix_rows(mixing, states, back)
        states = [section_shift(updated[0], 1), section_shift(updated[1], -1)]
    return jnp.stack(states)


def solution(mesh):
    placed = (
        P(None, ("section", "expert"), None),
        P(None, None, ("section", "expert"), None),
        P(None, None, ("section", "expert"), None),
        P("section", None, "expert"),
        P("section", None, "expert"),
        P("section", "expert", None),
    )
    return jax.shard_map(
        body,
        mesh=mesh,
        in_specs=placed,
        out_specs=P(None, ("section", "expert"), None),
        check_vma=False,
    )
```

time: 754 us -> 358 us (0.47)
  the two profiles are of different devices: /device:TPU:62 before, /device:TPU:64 now
where the time goes in v1:
time: 358 us; the launch traced here: 357 us
  waiting for transfers between devices  168 us (47%)
  starting transfers between devices  147 us (41%)
  Pallas kernels  17.9 us (5%)
  other arithmetic  12.6 us (4%)
  local copies, waits for them, and re-layouts  10.3 us (3%)
    ppermute x12, waiting for transfers between devices, chip_shift(): lax.ppermute(value, 'expert', pairs_of(lambda g, m, c: (g, (m + k) % CHIP...  100 us
    ppermute x12, starting transfers between devices, group_shift(): lax.ppermute(value, 'expert', pairs_of(lambda g, m, c: ((g + k) % GROUPS,...  82.3 us
    ppermute x12, waiting for transfers between devices, group_shift(): lax.ppermute(value, 'expert', pairs_of(lambda g, m, c: ((g + k) % GROUPS,...  43.4 us
    ppermute x12, starting transfers between devices, chip_shift(): lax.ppermute(value, 'expert', pairs_of(lambda g, m, c: (g, (m + k) % CHIP...  39.9 us
    ppermute x4, waiting for transfers between devices, section_shift(): lax.ppermute(value, 'section', [(s, (s + steps) % count) for s in range(c...  24.4 us
    ppermute x4, starting transfers between devices, section_shift(): lax.ppermute(value, 'section', [(s, (s + steps) % count) for s in range(c...  18.7 us
    pallas_call x2, Pallas kernels, expert_rows(): pl.pallas_call(expert_kernel, out_shape=[jax.ShapeDtypeStruct(rows[0].sha...  13.2 us
  transfers between devices with their start and end apart: 31, of which 20 were waited for; matrix products, arithmetic and copies ran while one was open for 6% of the time, Pallas kernels for 0%

profile of v1, /device:TPU:64, one launch (start us, length us, event | category | flops | bytes accessed | tf_op | source)
XLA Modules:
  0.0 356.8 jit_solution(12995587012225838716)
XLA Ops:
  0.0 2.0 collective-permute-start.1
  2.1 2.4 collective-permute-start
  4.5 1.9 collective-permute-start.2
  12.8 9.1 %collective-permute-start.3 = (bf16[24,2048]{1,0:T(8,128)(2,1)S(1)}, bf16[24,2048]{1,0:T(8,128)(2,1)S(1)}, u32[]{:S(2)}, u32[]{:S(2)}) collective-permute-start(bf16[24,2048]{1,0:T(8,128)(2,1)S(1)} %get-tuple-element.34), channel_id=1, source_target_pairs={{0,8},{1,9},{2,10},{3,11},{4,12},{5,13},{6,14},{7,15},{8,16},{9,17... | collective-permute-start | bytes 294920 | tf_op jit(solution)/shard_map/ppermute | solution.py:36
  21.9 9.1 %collective-permute-start.4 = (bf16[24,2048]{1,0:T(8,128)(2,1)S(1)}, bf16[24,2048]{1,0:T(8,128)(2,1)S(1)}, u32[]{:S(2)}, u32[]{:S(2)}) collective-permute-start(bf16[24,2048]{1,0:T(8,128)(2,1)S(1)} %get-tuple-element.35), channel_id=1, source_target_pairs={{0,16},{1,17},{2,18},{3,19},{4,20},{5,21},{6,22},{7,23},{8,24},{9,... | collective-permute-start | bytes 294920 | tf_op jit(solution)/shard_map/ppermute | solution.py:36
  32.0 8.5 %collective-permute-start.5 = (bf16[24,2048]{1,0:T(8,128)(2,1)S(1)}, bf16[24,2048]{1,0:T(8,128)(2,1)S(1)}, u32[]{:S(2)}, u32[]{:S(2)}) collective-permute-start(bf16[24,2048]{1,0:T(8,128)(2,1)S(1)} %get-tuple-element.36), channel_id=1, source_target_pairs={{0,24},{1,25},{2,26},{3,27},{4,28},{5,29},{6,30},{7,31},{8,0},{9,1... | collective-permute-start | bytes 294920 | tf_op jit(solution)/shard_map/ppermute | solution.py:36
  40.5 3.6 %collective-permute-done.4 = bf16[24,2048]{1,0:T(8,128)(2,1)S(1)} collective-permute-done((bf16[24,2048]{1,0:T(8,128)(2,1)S(1)}, bf16[24,2048]{1,0:T(8,128)(2,1)S(1)}, u32[]{:S(2)}, u32[]{:S(2)}) %collective-permute-start.4) | collective-permute-done | bytes 98336 | tf_op jit(solution)/shard_map/ppermute | solution.py:36
  44.1 4.6 %collective-permute-done.5 = bf16[24,2048]{1,0:T(8,128)(2,1)S(1)} collective-permute-done((bf16[24,2048]{1,0:T(8,128)(2,1)S(1)}, bf16[24,2048]{1,0:T(8,128)(2,1)S(1)}, u32[]{:S(2)}, u32[]{:S(2)}) %collective-permute-start.5) | collective-permute-done | bytes 98336 | tf_op jit(solution)/shard_map/ppermute | solution.py:36
  48.8 2.7 collective-permute-start.6
  51.4 1.9 collective-permute-start.7
  53.4 4.4 %collective-permute-start.8 = (bf16[96,2048]{1,0:T(8,128)(2,1)S(1)}, bf16[96,2048]{1,0:T(8,128)(2,1)S(1)}, u32[]{:S(2)}, u32[]{:S(2)}) collective-permute-start(bf16[96,2048]{1,0:T(8,128)(2,1)S(1)} %constant_dynamic-update-slice_fusion.refs_0_), channel_id=1, source_target_pairs={{0,6},{1,7},{2,0},{3,1},{4,2},{5,3},{6,4},{7,5},{8,14},{9,15},{10,... | collective-permute-start | bytes 1179656 | tf_op jit(solution)/shard_map/ppermute | solution.py:40
  57.8 3.5 pad_maximum_fusion.gate_up_ref
  62.7 17.0 %collective-permute-done.6.refs_1_ = bf16[96,2048]{1,0:T(8,128)(2,1)S(1)} collective-permute-done((bf16[96,2048]{1,0:T(8,128)(2,1)S(1)}, bf16[96,2048]{1,0:T(8,128)(2,1)S(1)}, u32[]{:S(2)}, u32[]{:S(2)}) %collective-permute-start.6) | collective-permute-done | bytes 393248 | tf_op jit(solution)/shard_map/ppermute | solution.py:40
  79.7 6.0 %collective-permute-done.8.refs_3_ = bf16[96,2048]{1,0:T(8,128)(2,1)S(1)} collective-permute-done((bf16[96,2048]{1,0:T(8,128)(2,1)S(1)}, bf16[96,2048]{1,0:T(8,128)(2,1)S(1)}, u32[]{:S(2)}, u32[]{:S(2)}) %collective-permute-start.8) | collective-permute-done | bytes 393248 | tf_op jit(solution)/shard_map/ppermute | solution.py:40
  85.7 6.6 %shard_map.65 = (bf16[96,2048]{1,0:T(8,128)(2,1)S(1)}, bf16[96,2048]{1,0:T(8,128)(2,1)}, bf16[96,2048]{1,0:T(8,128)(2,1)}, bf16[96,2048]{1,0:T(8,128)(2,1)}) custom-call(bf16[4096,512]{1,0:T(8,128)(2,1)} %pad_maximum_fusion.gate_up_ref, bf16[256,4096]{1,0:T(8,128)(2,1)S(1)} %pad_maximum_fusion.1.down_ref, ...), custom_call_target="tpu_custom_call" | custom-call | tf_op jit(solution)/shard_map/pallas_call | solution.py:139
  92.3 4.4 %collective-permute-start.9 = (bf16[96,2048]{1,0:T(8,128)(2,1)}, bf16[96,2048]{1,0:T(8,128)(2,1)}, u32[]{:S(2)}, u32[]{:S(2)}) collective-permute-start(bf16[96,2048]{1,0:T(8,128)(2,1)} %get-tuple-element.38), channel_id=1, source_target_pairs={{0,6},{1,7},{2,0},{3,1},{4,2},{5,3},{6,4},{7,5},{8,14},{9,15},{10,... | collective-permute-start | bytes 1179656 | tf_op jit(solution)/shard_map/ppermute | solution.py:40
  96.7 4.1 %collective-permute-start.10 = (bf16[96,2048]{1,0:T(8,128)(2,1)}, bf16[96,2048]{1,0:T(8,128)(2,1)}, u32[]{:S(2)}, u32[]{:S(2)}) collective-permute-start(bf16[96,2048]{1,0:T(8,128)(2,1)} %get-tuple-element.39), channel_id=1, source_target_pairs={{0,4},{1,5},{2,6},{3,7},{4,0},{5,1},{6,2},{7,3},{8,12},{9,13},{10,... | collective-permute-start | bytes 1179656 | tf_op jit(solution)/shard_map/ppermute | solution.py:40
  100.8 1.9 collective-permute-start.11
  110.1 13.2 %collective-permute-done.9.refs_1_ = bf16[96,2048]{1,0:T(8,128)(2,1)} collective-permute-done((bf16[96,2048]{1,0:T(8,128)(2,1)}, bf16[96,2048]{1,0:T(8,128)(2,1)}, u32[]{:S(2)}, u32[]{:S(2)}) %collective-permute-start.9) | collective-permute-done | bytes 393248 | tf_op jit(solution)/shard_map/ppermute | solution.py:40
  123.3 8.6 %collective-permute-done.10.refs_2_ = bf16[96,2048]{1,0:T(8,128)(2,1)} collective-permute-done((bf16[96,2048]{1,0:T(8,128)(2,1)}, bf16[96,2048]{1,0:T(8,128)(2,1)}, u32[]{:S(2)}, u32[]{:S(2)}) %collective-permute-start.10) | collective-permute-done | bytes 393248 | tf_op jit(solution)/shard_map/ppermute | solution.py:40
  133.4 8.6 %collective-permute-start.12 = (bf16[24,2048]{1,0:T(8,128)(2,1)S(1)}, bf16[24,2048]{1,0:T(8,128)(2,1)S(1)}, u32[]{:S(2)}, u32[]{:S(2)}) collective-permute-start(bf16[24,2048]{1,0:T(8,128)(2,1)S(1)} %get-tuple-element.42), channel_id=1, source_target_pairs={{0,24},{1,25},{2,26},{3,27},{4,28},{5,29},{6,30},{7,31},{8,0},{9,1... | collective-permute-start | bytes 294920 | tf_op jit(solution)/shard_map/ppermute | solution.py:36
  142.0 7.3 %collective-permute-start.13 = (bf16[24,2048]{1,0:T(8,128)(2,1)S(1)}, bf16[24,2048]{1,0:T(8,128)(2,1)S(1)}, u32[]{:S(2)}, u32[]{:S(2)}) collective-permute-start(bf16[24,2048]{1,0:T(8,128)(2,1)S(1)} %get-tuple-element.43), channel_id=1, source_target_pairs={{0,16},{1,17},{2,18},{3,19},{4,20},{5,21},{6,22},{7,23},{8,24},{9,... | collective-permute-start | bytes 294920 | tf_op jit(solution)/shard_map/ppermute | solution.py:36
  149.3 4.1 %collective-permute-start.14 = (bf16[24,2048]{1,0:T(8,128)(2,1)S(1)}, bf16[24,2048]{1,0:T(8,128)(2,1)S(1)}, u32[]{:S(2)}, u32[]{:S(2)}) collective-permute-start(bf16[24,2048]{1,0:T(8,128)(2,1)S(1)} %get-tuple-element.44), channel_id=1, source_target_pairs={{0,8},{1,9},{2,10},{3,11},{4,12},{5,13},{6,14},{7,15},{8,16},{9,17... | collective-permute-start | bytes 294920 | tf_op jit(solution)/shard_map/ppermute | solution.py:36
  154.4 12.7 %collective-permute-done.13.refs_4_ = bf16[24,2048]{1,0:T(8,128)(2,1)S(1)} collective-permute-done((bf16[24,2048]{1,0:T(8,128)(2,1)S(1)}, bf16[24,2048]{1,0:T(8,128)(2,1)S(1)}, u32[]{:S(2)}, u32[]{:S(2)}) %collective-permute-start.13) | collective-permute-done | bytes 98336 | tf_op jit(solution)/shard_map/ppermute | solution.py:36
  168.9 3.4 collective-permute-start.15
  172.2 5.8 %collective-permute-start.16 = (bf16[64,4096]{1,0:T(8,128)(2,1)}, bf16[64,4096]{1,0:T(8,128)(2,1)S(1)}, u32[]{:S(2)}, u32[]{:S(2)}) collective-permute-start(bf16[64,4096]{1,0:T(8,128)(2,1)} %get-tuple-element.46), channel_id=1, source_target_pairs={{0,480},{32,0},{64,32},{96,64},{128,96},{160,128},{192,160},{224,1... | collective-permute-start | bytes 1572872 | tf_op jit(solution)/shard_map/ppermute | solution.py:49
  179.1 6.3 %collective-permute-done.15.refs_0_ = bf16[64,4096]{1,0:T(8,128)(2,1)S(1)} collective-permute-done((bf16[64,4096]{1,0:T(8,128)(2,1)}, bf16[64,4096]{1,0:T(8,128)(2,1)S(1)}, u32[]{:S(2)}, u32[]{:S(2)}) %collective-permute-start.15) | collective-permute-done | bytes 524320 | tf_op jit(solution)/shard_map/ppermute | solution.py:49
  187.0 8.6 %collective-permute-start.17 = (bf16[24,2048]{1,0:T(8,128)(2,1)S(1)}, bf16[24,2048]{1,0:T(8,128)(2,1)S(1)}, u32[]{:S(2)}, u32[]{:S(2)}) collective-permute-start(bf16[24,2048]{1,0:T(8,128)(2,1)S(1)} %get-tuple-element.48), channel_id=1, source_target_pairs={{0,8},{1,9},{2,10},{3,11},{4,12},{5,13},{6,14},{7,15},{8,16},{9,17... | collective-permute-start | bytes 294920 | tf_op jit(solution)/shard_map/ppermute | solution.py:36
  195.6 4.3 %collective-permute-start.18 = (bf16[24,2048]{1,0:T(8,128)(2,1)S(1)}, bf16[24,2048]{1,0:T(8,128)(2,1)S(1)}, u32[]{:S(2)}, u32[]{:S(2)}) collective-permute-start(bf16[24,2048]{1,0:T(8,128)(2,1)S(1)} %get-tuple-element.49), channel_id=1, source_target_pairs={{0,16},{1,17},{2,18},{3,19},{4,20},{5,21},{6,22},{7,23},{8,24},{9,... | collective-permute-start | bytes 294920 | tf_op jit(solution)/shard_map/ppermute | solution.py:36
  199.9 6.9 %collective-permute-start.19 = (bf16[24,2048]{1,0:T(8,128)(2,1)S(1)}, bf16[24,2048]{1,0:T(8,128)(2,1)S(1)}, u32[]{:S(2)}, u32[]{:S(2)}) collective-permute-start(bf16[24,2048]{1,0:T(8,128)(2,1)S(1)} %get-tuple-element.50), channel_id=1, source_target_pairs={{0,24},{1,25},{2,26},{3,27},{4,28},{5,29},{6,30},{7,31},{8,0},{9,1... | collective-permute-start | bytes 294920 | tf_op jit(solution)/shard_map/ppermute | solution.py:36
  206.8 6.6 %collective-permute-done.18 = bf16[24,2048]{1,0:T(8,128)(2,1)S(1)} collective-permute-done((bf16[24,2048]{1,0:T(8,128)(2,1)S(1)}, bf16[24,2048]{1,0:T(8,128)(2,1)S(1)}, u32[]{:S(2)}, u32[]{:S(2)}) %collective-permute-start.18) | collective-permute-done | bytes 98336 | tf_op jit(solution)/shard_map/ppermute | solution.py:36
  217.3 4.6 %collective-permute-start.22 = (bf16[96,2048]{1,0:T(8,128)(2,1)S(1)}, bf16[96,2048]{1,0:T(8,128)(2,1)S(1)}, u32[]{:S(2)}, u32[]{:S(2)}) collective-permute-start(bf16[96,2048]{1,0:T(8,128)(2,1)S(1)} %constant_dynamic-update-slice_fusion.4.refs_0_), channel_id=1, source_target_pairs={{0,6},{1,7},{2,0},{3,1},{4,2},{5,3},{6,4},{7,5},{8,14},{9,15},{10,... | collective-permute-start | bytes 1179656 | tf_op jit(solution)/shard_map/ppermute | solution.py:40
  221.9 22.3 %collective-permute-done.20.refs_1_ = bf16[96,2048]{1,0:T(8,128)(2,1)S(1)} collective-permute-done((bf16[96,2048]{1,0:T(8,128)(2,1)S(1)}, bf16[96,2048]{1,0:T(8,128)(2,1)S(1)}, u32[]{:S(2)}, u32[]{:S(2)}) %collective-permute-start.20) | collective-permute-done | bytes 393248 | tf_op jit(solution)/shard_map/ppermute | solution.py:40
  244.2 4.9 %collective-permute-done.22.refs_3_ = bf16[96,2048]{1,0:T(8,128)(2,1)S(1)} collective-permute-done((bf16[96,2048]{1,0:T(8,128)(2,1)S(1)}, bf16[96,2048]{1,0:T(8,128)(2,1)S(1)}, u32[]{:S(2)}, u32[]{:S(2)}) %collective-permute-start.22) | collective-permute-done | bytes 393248 | tf_op jit(solution)/shard_map/ppermute | solution.py:40
  249.1 6.6 %shard_map.69 = (bf16[96,2048]{1,0:T(8,128)(2,1)S(1)}, bf16[96,2048]{1,0:T(8,128)(2,1)}, bf16[96,2048]{1,0:T(8,128)(2,1)}, bf16[96,2048]{1,0:T(8,128)(2,1)}) custom-call(bf16[4096,512]{1,0:T(8,128)(2,1)} %pad_maximum_fusion.gate_up_ref, bf16[256,4096]{1,0:T(8,128)(2,1)S(1)} %pad_maximum_fusion.1.down_ref, ...), custom_call_target="tpu_custom_call" | custom-call | tf_op jit(solution)/shard_map/pallas_call | solution.py:139
  255.7 4.4 %collective-permute-start.23 = (bf16[96,2048]{1,0:T(8,128)(2,1)}, bf16[96,2048]{1,0:T(8,128)(2,1)S(1)}, u32[]{:S(2)}, u32[]{:S(2)}) collective-permute-start(bf16[96,2048]{1,0:T(8,128)(2,1)} %get-tuple-element.52), channel_id=1, source_target_pairs={{0,6},{1,7},{2,0},{3,1},{4,2},{5,3},{6,4},{7,5},{8,14},{9,15},{10,... | collective-permute-start | bytes 1179656 | tf_op jit(solution)/shard_map/ppermute | solution.py:40
  260.1 5.8 %collective-permute-start.24 = (bf16[96,2048]{1,0:T(8,128)(2,1)}, bf16[96,2048]{1,0:T(8,128)(2,1)S(1)}, u32[]{:S(2)}, u32[]{:S(2)}) collective-permute-start(bf16[96,2048]{1,0:T(8,128)(2,1)} %get-tuple-element.53), channel_id=1, source_target_pairs={{0,4},{1,5},{2,6},{3,7},{4,0},{5,1},{6,2},{7,3},{8,12},{9,13},{10,... | collective-permute-start | bytes 1179656 | tf_op jit(solution)/shard_map/ppermute | solution.py:40
  269.2 17.4 %collective-permute-done.23.refs_1_ = bf16[96,2048]{1,0:T(8,128)(2,1)S(1)} collective-permute-done((bf16[96,2048]{1,0:T(8,128)(2,1)}, bf16[96,2048]{1,0:T(8,128)(2,1)S(1)}, u32[]{:S(2)}, u32[]{:S(2)}) %collective-permute-start.23) | collective-permute-done | bytes 393248 | tf_op jit(solution)/shard_map/ppermute | solution.py:40
  286.6 7.7 %collective-permute-done.24.refs_2_ = bf16[96,2048]{1,0:T(8,128)(2,1)S(1)} collective-permute-done((bf16[96,2048]{1,0:T(8,128)(2,1)}, bf16[96,2048]{1,0:T(8,128)(2,1)S(1)}, u32[]{:S(2)}, u32[]{:S(2)}) %collective-permute-start.24) | collective-permute-done | bytes 393248 | tf_op jit(solution)/shard_map/ppermute | solution.py:40
  294.2 3.3 collective-permute-done.25.refs_3_
  297.8 6.1 %collective-permute-start.26 = (bf16[24,2048]{1,0:T(8,128)(2,1)S(1)}, bf16[24,2048]{1,0:T(8,128)(2,1)S(1)}, u32[]{:S(2)}, u32[]{:S(2)}) collective-permute-start(bf16[24,2048]{1,0:T(8,128)(2,1)S(1)} %get-tuple-element.56), channel_id=1, source_target_pairs={{0,24},{1,25},{2,26},{3,27},{4,28},{5,29},{6,30},{7,31},{8,0},{9,1... | collective-permute-start | bytes 294920 | tf_op jit(solution)/shard_map/ppermute | solution.py:36
  303.9 3.7 %collective-permute-start.27 = (bf16[24,2048]{1,0:T(8,128)(2,1)S(1)}, bf16[24,2048]{1,0:T(8,128)(2,1)S(1)}, u32[]{:S(2)}, u32[]{:S(2)}) collective-permute-start(bf16[24,2048]{1,0:T(8,128)(2,1)S(1)} %get-tuple-element.57), channel_id=1, source_target_pairs={{0,16},{1,17},{2,18},{3,19},{4,20},{5,21},{6,22},{7,23},{8,24},{9,... | collective-permute-start | bytes 294920 | tf_op jit(solution)/shard_map/ppermute | solution.py:36
  307.5 6.0 %collective-permute-start.28 = (bf16[24,2048]{1,0:T(8,128)(2,1)S(1)}, bf16[24,2048]{1,0:T(8,128)(2,1)S(1)}, u32[]{:S(2)}, u32[]{:S(2)}) collective-permute-start(bf16[24,2048]{1,0:T(8,128)(2,1)S(1)} %get-tuple-element.58), channel_id=1, source_target_pairs={{0,8},{1,9},{2,10},{3,11},{4,12},{5,13},{6,14},{7,15},{8,16},{9,17... | collective-permute-start | bytes 294920 | tf_op jit(solution)/shard_map/ppermute | solution.py:36
  313.7 12.5 %collective-permute-done.27.refs_4_ = bf16[24,2048]{1,0:T(8,128)(2,1)S(1)} collective-permute-done((bf16[24,2048]{1,0:T(8,128)(2,1)S(1)}, bf16[24,2048]{1,0:T(8,128)(2,1)S(1)}, u32[]{:S(2)}, u32[]{:S(2)}) %collective-permute-start.27) | collective-permute-done | bytes 98336 | tf_op jit(solution)/shard_map/ppermute | solution.py:36
  326.2 2.4 collective-permute-done.28.refs_5_
  329.3 7.6 %collective-permute-start.30 = (bf16[64,4096]{1,0:T(8,128)(2,1)S(1)}, bf16[64,4096]{1,0:T(8,128)(2,1)S(1)}, u32[]{:S(2)}, u32[]{:S(2)}) collective-permute-start(bf16[64,4096]{1,0:T(8,128)(2,1)S(1)} %get-tuple-element.60), channel_id=1, source_target_pairs={{0,480},{32,0},{64,32},{96,64},{128,96},{160,128},{192,160},{224,1... | collective-permute-start | bytes 1572872 | tf_op jit(solution)/shard_map/ppermute | solution.py:49
  338.9 9.4 %collective-permute-done.30 = bf16[64,4096]{1,0:T(8,128)(2,1)S(1)} collective-permute-done((bf16[64,4096]{1,0:T(8,128)(2,1)S(1)}, bf16[64,4096]{1,0:T(8,128)(2,1)S(1)}, u32[]{:S(2)}, u32[]{:S(2)}) %collective-permute-start.30) | collective-permute-done | bytes 524320 | tf_op jit(solution)/shard_map/ppermute | solution.py:49
  348.3 7.4 %collective-permute-done.29 = bf16[64,4096]{1,0:T(8,128)(2,1)S(1)} collective-permute-done((bf16[64,4096]{1,0:T(8,128)(2,1)S(1)}, bf16[64,4096]{1,0:T(8,128)(2,1)S(1)}, u32[]{:S(2)}, u32[]{:S(2)}) %collective-permute-start.29) | collective-permute-done | bytes 524320 | tf_op jit(solution)/shard_map/ppermute | solution.py:49
  (79 shorter events, 34.0 us)
Async XLA Ops:
  0.0 57.8 %copy-start.1 = (bf16[1,4096,128]{2,1,0:T(8,128)(2,1)S(1)}, bf16[1,4096,128]{2,1,0:T(8,128)(2,1)}, u32[]{:S(2)}) copy-start(bf16[1,4096,128]{2,1,0:T(8,128)(2,1)} %param.10) | copy-start | bytes 3145732
  0.0 53.4 %collective-permute-start.1 = (bf16[4096,128]{1,0:T(8,128)(2,1)}, bf16[4096,128]{1,0:T(8,128)(2,1)}, u32[]{:S(2)}, u32[]{:S(2)}) collective-permute-start(bf16[4096,128]{1,0:T(8,128)(2,1)} %bitcast.31), channel_id=1, source_target_pairs={{0,1},{1,0},{2,3},{3,2},{4,5},{5,4},{6,7},{7,6},{8,9},{9,8},{10,11... | collective-permute-start | bytes 3145736 | tf_op jit(solution)/shard_map/ppermute | solution.py:44
  2.1 55.7 %collective-permute-start = (bf16[4096,128]{1,0:T(8,128)(2,1)}, bf16[4096,128]{1,0:T(8,128)(2,1)}, u32[]{:S(2)}, u32[]{:S(2)}) collective-permute-start(bf16[4096,128]{1,0:T(8,128)(2,1)} %bitcast.33), channel_id=1, source_target_pairs={{0,1},{1,0},{2,3},{3,2},{4,5},{5,4},{6,7},{7,6},{8,9},{9,8},{10,11... | collective-permute-start | bytes 3145736 | tf_op jit(solution)/shard_map/ppermute | solution.py:44
  4.5 56.9 %collective-permute-start.2 = (bf16[128,4096]{1,0:T(8,128)(2,1)}, bf16[128,4096]{1,0:T(8,128)(2,1)}, u32[]{:S(2)}, u32[]{:S(2)}) collective-permute-start(bf16[128,4096]{1,0:T(8,128)(2,1)} %bitcast.29), channel_id=1, source_target_pairs={{0,1},{1,0},{2,3},{3,2},{4,5},{5,4},{6,7},{7,6},{8,9},{9,8},{10,11... | collective-permute-start | bytes 3145736 | tf_op jit(solution)/shard_map/ppermute | solution.py:44
  12.8 19.2 %collective-permute-start.3 = (bf16[24,2048]{1,0:T(8,128)(2,1)S(1)}, bf16[24,2048]{1,0:T(8,128)(2,1)S(1)}, u32[]{:S(2)}, u32[]{:S(2)}) collective-permute-start(bf16[24,2048]{1,0:T(8,128)(2,1)S(1)} %get-tuple-element.34), channel_id=1, source_target_pairs={{0,8},{1,9},{2,10},{3,11},{4,12},{5,13},{6,14},{7,15},{8,16},{9,17... | collective-permute-start | bytes 294920 | tf_op jit(solution)/shard_map/ppermute | solution.py:36
  21.9 22.2 %collective-permute-start.4 = (bf16[24,2048]{1,0:T(8,128)(2,1)S(1)}, bf16[24,2048]{1,0:T(8,128)(2,1)S(1)}, u32[]{:S(2)}, u32[]{:S(2)}) collective-permute-start(bf16[24,2048]{1,0:T(8,128)(2,1)S(1)} %get-tuple-element.35), channel_id=1, source_target_pairs={{0,16},{1,17},{2,18},{3,19},{4,20},{5,21},{6,22},{7,23},{8,24},{9,... | collective-permute-start | bytes 294920 | tf_op jit(solution)/shard_map/ppermute | solution.py:36
  32.0 16.8 %collective-permute-start.5 = (bf16[24,2048]{1,0:T(8,128)(2,1)S(1)}, bf16[24,2048]{1,0:T(8,128)(2,1)S(1)}, u32[]{:S(2)}, u32[]{:S(2)}) collective-permute-start(bf16[24,2048]{1,0:T(8,128)(2,1)S(1)} %get-tuple-element.36), channel_id=1, source_target_pairs={{0,24},{1,25},{2,26},{3,27},{4,28},{5,29},{6,30},{7,31},{8,0},{9,1... | collective-permute-start | bytes 294920 | tf_op jit(solution)/shard_map/ppermute | solution.py:36
  48.7 12.6 %copy-start = (bf16[1,128,4096]{2,1,0:T(8,128)(2,1)S(1)}, bf16[1,128,4096]{2,1,0:T(8,128)(2,1)}, u32[]{:S(2)}) copy-start(bf16[1,128,4096]{2,1,0:T(8,128)(2,1)} %param.11) | copy-start | bytes 3145732
  48.8 30.9 %collective-permute-start.6 = (bf16[96,2048]{1,0:T(8,128)(2,1)S(1)}, bf16[96,2048]{1,0:T(8,128)(2,1)S(1)}, u32[]{:S(2)}, u32[]{:S(2)}) collective-permute-start(bf16[96,2048]{1,0:T(8,128)(2,1)S(1)} %constant_dynamic-update-slice_fusion.refs_0_), channel_id=1, source_target_pairs={{0,2},{1,3},{2,4},{3,5},{4,6},{5,7},{6,0},{7,1},{8,10},{9,11},{10,... | collective-permute-start | bytes 1179656 | tf_op jit(solution)/shard_map/ppermute | solution.py:40
  51.4 28.2 %collective-permute-start.7 = (bf16[96,2048]{1,0:T(8,128)(2,1)S(1)}, bf16[96,2048]{1,0:T(8,128)(2,1)S(1)}, u32[]{:S(2)}, u32[]{:S(2)}) collective-permute-start(bf16[96,2048]{1,0:T(8,128)(2,1)S(1)} %constant_dynamic-update-slice_fusion.refs_0_), channel_id=1, source_target_pairs={{0,4},{1,5},{2,6},{3,7},{4,0},{5,1},{6,2},{7,3},{8,12},{9,13},{10,... | collective-permute-start | bytes 1179656 | tf_op jit(solution)/shard_map/ppermute | solution.py:40
  53.4 32.3 %collective-permute-start.8 = (bf16[96,2048]{1,0:T(8,128)(2,1)S(1)}, bf16[96,2048]{1,0:T(8,128)(2,1)S(1)}, u32[]{:S(2)}, u32[]{:S(2)}) collective-permute-start(bf16[96,2048]{1,0:T(8,128)(2,1)S(1)} %constant_dynamic-update-slice_fusion.refs_0_), channel_id=1, source_target_pairs={{0,6},{1,7},{2,0},{3,1},{4,2},{5,3},{6,4},{7,5},{8,14},{9,15},{10,... | collective-permute-start | bytes 1179656 | tf_op jit(solution)/shard_map/ppermute | solution.py:40
  92.3 31.0 %collective-permute-start.9 = (bf16[96,2048]{1,0:T(8,128)(2,1)}, bf16[96,2048]{1,0:T(8,128)(2,1)}, u32[]{:S(2)}, u32[]{:S(2)}) collective-permute-start(bf16[96,2048]{1,0:T(8,128)(2,1)} %get-tuple-element.38), channel_id=1, source_target_pairs={{0,6},{1,7},{2,0},{3,1},{4,2},{5,3},{6,4},{7,5},{8,14},{9,15},{10,... | collective-permute-start | bytes 1179656 | tf_op jit(solution)/shard_map/ppermute | solution.py:40
  96.7 35.2 %collective-permute-start.10 = (bf16[96,2048]{1,0:T(8,128)(2,1)}, bf16[96,2048]{1,0:T(8,128)(2,1)}, u32[]{:S(2)}, u32[]{:S(2)}) collective-permute-start(bf16[96,2048]{1,0:T(8,128)(2,1)} %get-tuple-element.39), channel_id=1, source_target_pairs={{0,4},{1,5},{2,6},{3,7},{4,0},{5,1},{6,2},{7,3},{8,12},{9,13},{10,... | collective-permute-start | bytes 1179656 | tf_op jit(solution)/shard_map/ppermute | solution.py:40
  100.8 31.2 %collective-permute-start.11 = (bf16[96,2048]{1,0:T(8,128)(2,1)}, bf16[96,2048]{1,0:T(8,128)(2,1)}, u32[]{:S(2)}, u32[]{:S(2)}) collective-permute-start(bf16[96,2048]{1,0:T(8,128)(2,1)} %get-tuple-element.40), channel_id=1, source_target_pairs={{0,2},{1,3},{2,4},{3,5},{4,6},{5,7},{6,0},{7,1},{8,10},{9,11},{10,... | collective-permute-start | bytes 1179656 | tf_op jit(solution)/shard_map/ppermute | solution.py:40
  133.4 21.0 %collective-permute-start.12 = (bf16[24,2048]{1,0:T(8,128)(2,1)S(1)}, bf16[24,2048]{1,0:T(8,128)(2,1)S(1)}, u32[]{:S(2)}, u32[]{:S(2)}) collective-permute-start(bf16[24,2048]{1,0:T(8,128)(2,1)S(1)} %get-tuple-element.42), channel_id=1, source_target_pairs={{0,24},{1,25},{2,26},{3,27},{4,28},{5,29},{6,30},{7,31},{8,0},{9,1... | collective-permute-start | bytes 294920 | tf_op jit(solution)/shard_map/ppermute | solution.py:36
  142.0 25.1 %collective-permute-start.13 = (bf16[24,2048]{1,0:T(8,128)(2,1)S(1)}, bf16[24,2048]{1,0:T(8,128)(2,1)S(1)}, u32[]{:S(2)}, u32[]{:S(2)}) collective-permute-start(bf16[24,2048]{1,0:T(8,128)(2,1)S(1)} %get-tuple-element.43), channel_id=1, source_target_pairs={{0,16},{1,17},{2,18},{3,19},{4,20},{5,21},{6,22},{7,23},{8,24},{9,... | collective-permute-start | bytes 294920 | tf_op jit(solution)/shard_map/ppermute | solution.py:36
  149.3 17.8 %collective-permute-start.14 = (bf16[24,2048]{1,0:T(8,128)(2,1)S(1)}, bf16[24,2048]{1,0:T(8,128)(2,1)S(1)}, u32[]{:S(2)}, u32[]{:S(2)}) collective-permute-start(bf16[24,2048]{1,0:T(8,128)(2,1)S(1)} %get-tuple-element.44), channel_id=1, source_target_pairs={{0,8},{1,9},{2,10},{3,11},{4,12},{5,13},{6,14},{7,15},{8,16},{9,17... | collective-permute-start | bytes 294920 | tf_op jit(solution)/shard_map/ppermute | solution.py:36
  168.9 16.6 %collective-permute-start.15 = (bf16[64,4096]{1,0:T(8,128)(2,1)}, bf16[64,4096]{1,0:T(8,128)(2,1)S(1)}, u32[]{:S(2)}, u32[]{:S(2)}) collective-permute-start(bf16[64,4096]{1,0:T(8,128)(2,1)} %get-tuple-element.45), channel_id=1, source_target_pairs={{0,32},{32,64},{64,96},{96,128},{128,160},{160,192},{192,224},{224... | collective-permute-start | bytes 1572872 | tf_op jit(solution)/shard_map/ppermute | solution.py:49
  172.2 14.5 %collective-permute-start.16 = (bf16[64,4096]{1,0:T(8,128)(2,1)}, bf16[64,4096]{1,0:T(8,128)(2,1)S(1)}, u32[]{:S(2)}, u32[]{:S(2)}) collective-permute-start(bf16[64,4096]{1,0:T(8,128)(2,1)} %get-tuple-element.46), channel_id=1, source_target_pairs={{0,480},{32,0},{64,32},{96,64},{128,96},{160,128},{192,160},{224,1... | collective-permute-start | bytes 1572872 | tf_op jit(solution)/shard_map/ppermute | solution.py:49
  187.0 19.8 %collective-permute-start.17 = (bf16[24,2048]{1,0:T(8,128)(2,1)S(1)}, bf16[24,2048]{1,0:T(8,128)(2,1)S(1)}, u32[]{:S(2)}, u32[]{:S(2)}) collective-permute-start(bf16[24,2048]{1,0:T(8,128)(2,1)S(1)} %get-tuple-element.48), channel_id=1, source_target_pairs={{0,8},{1,9},{2,10},{3,11},{4,12},{5,13},{6,14},{7,15},{8,16},{9,17... | collective-permute-start | bytes 294920 | tf_op jit(solution)/shard_map/ppermute | solution.py:36
  195.6 17.8 %collective-permute-start.18 = (bf16[24,2048]{1,0:T(8,128)(2,1)S(1)}, bf16[24,2048]{1,0:T(8,128)(2,1)S(1)}, u32[]{:S(2)}, u32[]{:S(2)}) collective-permute-start(bf16[24,2048]{1,0:T(8,128)(2,1)S(1)} %get-tuple-element.49), channel_id=1, source_target_pairs={{0,16},{1,17},{2,18},{3,19},{4,20},{5,21},{6,22},{7,23},{8,24},{9,... | collective-permute-start | bytes 294920 | tf_op jit(solution)/shard_map/ppermute | solution.py:36
  199.9 13.5 %collective-permute-start.19 = (bf16[24,2048]{1,0:T(8,128)(2,1)S(1)}, bf16[24,2048]{1,0:T(8,128)(2,1)S(1)}, u32[]{:S(2)}, u32[]{:S(2)}) collective-permute-start(bf16[24,2048]{1,0:T(8,128)(2,1)S(1)} %get-tuple-element.50), channel_id=1, source_target_pairs={{0,24},{1,25},{2,26},{3,27},{4,28},{5,29},{6,30},{7,31},{8,0},{9,1... | collective-permute-start | bytes 294920 | tf_op jit(solution)/shard_map/ppermute | solution.py:36
  213.5 30.7 %collective-permute-start.20 = (bf16[96,2048]{1,0:T(8,128)(2,1)S(1)}, bf16[96,2048]{1,0:T(8,128)(2,1)S(1)}, u32[]{:S(2)}, u32[]{:S(2)}) collective-permute-start(bf16[96,2048]{1,0:T(8,128)(2,1)S(1)} %constant_dynamic-update-slice_fusion.4.refs_0_), channel_id=1, source_target_pairs={{0,2},{1,3},{2,4},{3,5},{4,6},{5,7},{6,0},{7,1},{8,10},{9,11},{10,... | collective-permute-start | bytes 1179656 | tf_op jit(solution)/shard_map/ppermute | solution.py:40
  215.4 28.8 %collective-permute-start.21 = (bf16[96,2048]{1,0:T(8,128)(2,1)S(1)}, bf16[96,2048]{1,0:T(8,128)(2,1)S(1)}, u32[]{:S(2)}, u32[]{:S(2)}) collective-permute-start(bf16[96,2048]{1,0:T(8,128)(2,1)S(1)} %constant_dynamic-update-slice_fusion.4.refs_0_), channel_id=1, source_target_pairs={{0,4},{1,5},{2,6},{3,7},{4,0},{5,1},{6,2},{7,3},{8,12},{9,13},{10,... | collective-permute-start | bytes 1179656 | tf_op jit(solution)/shard_map/ppermute | solution.py:40
  217.3 31.8 %collective-permute-start.22 = (bf16[96,2048]{1,0:T(8,128)(2,1)S(1)}, bf16[96,2048]{1,0:T(8,128)(2,1)S(1)}, u32[]{:S(2)}, u32[]{:S(2)}) collective-permute-start(bf16[96,2048]{1,0:T(8,128)(2,1)S(1)} %constant_dynamic-update-slice_fusion.4.refs_0_), channel_id=1, source_target_pairs={{0,6},{1,7},{2,0},{3,1},{4,2},{5,3},{6,4},{7,5},{8,14},{9,15},{10,... | collective-permute-start | bytes 1179656 | tf_op jit(solution)/shard_map/ppermute | solution.py:40
  255.7 30.9 %collective-permute-start.23 = (bf16[96,2048]{1,0:T(8,128)(2,1)}, bf16[96,2048]{1,0:T(8,128)(2,1)S(1)}, u32[]{:S(2)}, u32[]{:S(2)}) collective-permute-start(bf16[96,2048]{1,0:T(8,128)(2,1)} %get-tuple-element.52), channel_id=1, source_target_pairs={{0,6},{1,7},{2,0},{3,1},{4,2},{5,3},{6,4},{7,5},{8,14},{9,15},{10,... | collective-permute-start | bytes 1179656 | tf_op jit(solution)/shard_map/ppermute | solution.py:40
  260.1 34.2 %collective-permute-start.24 = (bf16[96,2048]{1,0:T(8,128)(2,1)}, bf16[96,2048]{1,0:T(8,128)(2,1)S(1)}, u32[]{:S(2)}, u32[]{:S(2)}) collective-permute-start(bf16[96,2048]{1,0:T(8,128)(2,1)} %get-tuple-element.53), channel_id=1, source_target_pairs={{0,4},{1,5},{2,6},{3,7},{4,0},{5,1},{6,2},{7,3},{8,12},{9,13},{10,... | collective-permute-start | bytes 1179656 | tf_op jit(solution)/shard_map/ppermute | solution.py:40
  265.9 31.7 %collective-permute-start.25 = (bf16[96,2048]{1,0:T(8,128)(2,1)}, bf16[96,2048]{1,0:T(8,128)(2,1)S(1)}, u32[]{:S(2)}, u32[]{:S(2)}) collective-permute-start(bf16[96,2048]{1,0:T(8,128)(2,1)} %get-tuple-element.54), channel_id=1, source_target_pairs={{0,2},{1,3},{2,4},{3,5},{4,6},{5,7},{6,0},{7,1},{8,10},{9,11},{10,... | collective-permute-start | bytes 1179656 | tf_op jit(solution)/shard_map/ppermute | solution.py:40
  297.8 15.9 %collective-permute-start.26 = (bf16[24,2048]{1,0:T(8,128)(2,1)S(1)}, bf16[24,2048]{1,0:T(8,128)(2,1)S(1)}, u32[]{:S(2)}, u32[]{:S(2)}) collective-permute-start(bf16[24,2048]{1,0:T(8,128)(2,1)S(1)} %get-tuple-element.56), channel_id=1, source_target_pairs={{0,24},{1,25},{2,26},{3,27},{4,28},{5,29},{6,30},{7,31},{8,0},{9,1... | collective-permute-start | bytes 294920 | tf_op jit(solution)/shard_map/ppermute | solution.py:36
  303.9 22.4 %collective-permute-start.27 = (bf16[24,2048]{1,0:T(8,128)(2,1)S(1)}, bf16[24,2048]{1,0:T(8,128)(2,1)S(1)}, u32[]{:S(2)}, u32[]{:S(2)}) collective-permute-start(bf16[24,2048]{1,0:T(8,128)(2,1)S(1)} %get-tuple-element.57), channel_id=1, source_target_pairs={{0,16},{1,17},{2,18},{3,19},{4,20},{5,21},{6,22},{7,23},{8,24},{9,... | collective-permute-start | bytes 294920 | tf_op jit(solution)/shard_map/ppermute | solution.py:36
  307.5 21.1 %collective-permute-start.28 = (bf16[24,2048]{1,0:T(8,128)(2,1)S(1)}, bf16[24,2048]{1,0:T(8,128)(2,1)S(1)}, u32[]{:S(2)}, u32[]{:S(2)}) collective-permute-start(bf16[24,2048]{1,0:T(8,128)(2,1)S(1)} %get-tuple-element.58), channel_id=1, source_target_pairs={{0,8},{1,9},{2,10},{3,11},{4,12},{5,13},{6,14},{7,15},{8,16},{9,17... | collective-permute-start | bytes 294920 | tf_op jit(solution)/shard_map/ppermute | solution.py:36
  329.3 19.0 %collective-permute-start.30 = (bf16[64,4096]{1,0:T(8,128)(2,1)S(1)}, bf16[64,4096]{1,0:T(8,128)(2,1)S(1)}, u32[]{:S(2)}, u32[]{:S(2)}) collective-permute-start(bf16[64,4096]{1,0:T(8,128)(2,1)S(1)} %get-tuple-element.60), channel_id=1, source_target_pairs={{0,480},{32,0},{64,32},{96,64},{128,96},{160,128},{192,160},{224,1... | collective-permute-start | bytes 1572872 | tf_op jit(solution)/shard_map/ppermute | solution.py:49
  337.0 18.8 %collective-permute-start.29 = (bf16[64,4096]{1,0:T(8,128)(2,1)S(1)}, bf16[64,4096]{1,0:T(8,128)(2,1)S(1)}, u32[]{:S(2)}, u32[]{:S(2)}) collective-permute-start(bf16[64,4096]{1,0:T(8,128)(2,1)S(1)} %get-tuple-element.59), channel_id=1, source_target_pairs={{0,32},{32,64},{64,96},{96,128},{128,160},{160,192},{192,224},{224... | collective-permute-start | bytes 1572872 | tf_op jit(solution)/shard_map/ppermute | solution.py:49

commit v2 on v0

v2 whole, which is shorter than its diff:
```python
import jax
import jax.numpy as jnp
from jax import lax
from jax.experimental import pallas as pl
from jax.experimental.pallas import tpu as pltpu
from jax.sharding import PartitionSpec as P

MOST = 6
STEPS = 2
ROWS = 64
GROUPS = 4
CHIPS = 4
CORES = 2
PIECES = 2
DIRS = 2
FOLD = 2
EACH = DIRS * MOST
PART = FOLD * EACH
LISTED = GROUPS * MOST
PARAMS = pltpu.CompilerParams(vmem_limit_bytes=52 * 1024 * 1024)


def device_at(g, m, c):
    return (g * CHIPS + m) * CORES + c


def pairs_of(place):
    pairs = []
    for g in range(GROUPS):
        for m in range(CHIPS):
            for c in range(CORES):
                pairs.append((device_at(g, m, c), device_at(*place(g, m, c))))
    return pairs


def group_exchange(value):
    groups = [
        [device_at(g, m, c) for g in range(GROUPS)] for m in range(CHIPS) for c in range(CORES)
    ]
    return lax.all_to_all(
        value, "expert", split_axis=0, concat_axis=0, axis_index_groups=groups, tiled=True
    )


def chip_swap(value, k):
    return lax.ppermute(value, "expert", pairs_of(lambda g, m, c: (g, m ^ k, c)))


def core_swap(value):
    return lax.ppermute(value, "expert", pairs_of(lambda g, m, c: (g, m, 1 - c)))


def section_shift(value, steps):
    count = lax.axis_size("section")
    return lax.ppermute(value, "section", [(s, (s + steps) % count) for s in range(count)])


def local_call(kernel, shapes, *operands):
    return pl.pallas_call(
        kernel,
        out_shape=[jax.ShapeDtypeStruct(shape, jnp.bfloat16) for shape in shapes],
        compiler_params=PARAMS,
    )(*operands)


def dot(a, b):
    return jnp.dot(a, b, preferred_element_type=jnp.float32)


def one_hot(mask):
    return mask.astype(jnp.float32).astype(jnp.bfloat16)


def listed_slots(ids):
    shape = (ROWS, GROUPS * PART)
    lane = lax.broadcasted_iota(jnp.int32, shape, 1)
    member = jnp.zeros(shape, jnp.float32)
    for e in range(GROUPS):
        named = jnp.max((ids == e).astype(jnp.float32), axis=1, keepdims=True)
        member = member + jnp.where(lane // PART == e, named, 0.0)
    later = lax.broadcasted_iota(jnp.int32, (ROWS, ROWS), 0)
    earlier = lax.broadcasted_iota(jnp.int32, (ROWS, ROWS), 1)
    rank = dot(one_hot(earlier < later), member.astype(jnp.bfloat16))
    slot = (lane % MOST).astype(jnp.float32)
    return jnp.where((rank == slot) & (member > 0.0), 1.0, 0.0)


def spread(tables):
    lane = lax.broadcasted_iota(jnp.int32, tables[0].shape, 1)
    block = (lane % PART) // MOST
    rows = [
        jnp.where(block == q * DIRS + d, tables[d], 0.0) for q in range(FOLD) for d in range(DIRS)
    ]
    return jnp.concatenate(rows, axis=0)


def fold_match(folded, plain, q, d):
    same_expert = (folded // PART) == (plain // MOST)
    same_slot = (folded % MOST) == (plain % MOST)
    this_block = ((folded % PART) // MOST) == q * DIRS + d
    return one_hot(same_expert & same_slot & this_block)


def list_kernel(ids_ref, *refs):
    states, out_ref = refs[:DIRS], refs[DIRS]
    width = out_ref.shape[1]
    table = spread([listed_slots(ids_ref[d]) for d in range(DIRS)]).astype(jnp.bfloat16)
    stack = [ref[:, q * width : (q + 1) * width] for q in range(FOLD) for ref in states]
    rows = lax.dot_general(
        table,
        jnp.concatenate(stack, axis=0),
        (((0,), (0,)), ((), ())),
        preferred_element_type=jnp.float32,
    )
    out_ref[...] = rows.astype(jnp.bfloat16)


def unfold_kernel(folded_ref, *outs):
    rows = folded_ref[...]
    width = rows.shape[1]
    shape = (LISTED, rows.shape[0])
    plain = lax.broadcasted_iota(jnp.int32, shape, 0)
    folded = lax.broadcasted_iota(jnp.int32, shape, 1)
    for d, out in enumerate(outs):
        for q in range(FOLD):
            part = dot(fold_match(folded, plain, q, d), rows)
            out[:, q * width : (q + 1) * width] = part.astype(jnp.bfloat16)


def pair_kernel(near_ref, far_ref, out_ref):
    rows = [ref[...].astype(jnp.float32) for ref in (near_ref, far_ref)]
    out_ref[...] = jnp.concatenate(rows, axis=0).astype(jnp.bfloat16)


def add_kernel(own_ref, got_ref, near_ref, far_ref):
    rows = near_ref.shape[0]
    total = own_ref[...].astype(jnp.float32) + got_ref[...].astype(jnp.float32)
    near_ref[...] = total[:rows].astype(jnp.bfloat16)
    far_ref[...] = total[rows:].astype(jnp.bfloat16)


def expert_kernel(*refs):
    pieces = refs[: 3 * PIECES]
    near_ref, far_ref, done_near_ref, done_far_ref = refs[3 * PIECES :]
    rows = jnp.concatenate([near_ref[...], far_ref[...]], axis=0)
    result = jnp.zeros(rows.shape, jnp.float32)
    for p in range(0, PIECES, 2):
        gates, ups, downs = ([ref[...] for ref in pieces[3 * p + n : 3 * p + 6 : 3]] for n in range(3))
        both = dot(rows, jnp.concatenate(gates + ups, axis=1))
        half = both.shape[1] // 2
        hidden = (jax.nn.silu(both[:, :half]) * both[:, half:]).astype(jnp.bfloat16)
        result = result + dot(hidden, jnp.concatenate(downs, axis=0))
    count = near_ref.shape[0]
    done_near_ref[...] = result[:count].astype(jnp.bfloat16)
    done_far_ref[...] = result[count:].astype(jnp.bfloat16)


def fold_kernel(*refs):
    owns, gots, out_ref = refs[:DIRS], refs[DIRS : 2 * DIRS], refs[2 * DIRS]
    width = out_ref.shape[1]
    shape = (out_ref.shape[0], LISTED)
    folded = lax.broadcasted_iota(jnp.int32, shape, 0)
    plain = lax.broadcasted_iota(jnp.int32, shape, 1)
    rows = jnp.zeros(out_ref.shape, jnp.float32)
    for d in range(DIRS):
        total = owns[d][...].astype(jnp.float32) + gots[d][...].astype(jnp.float32)
        total = total.astype(jnp.bfloat16)
        for q in range(FOLD):
            part = total[:, q * width : (q + 1) * width]
            rows = rows + dot(fold_match(folded, plain, q, d), part)
    out_ref[...] = rows.astype(jnp.bfloat16)


def weighted_slots(ids, gates):
    norm = gates / jnp.sum(gates, axis=1, keepdims=True)
    slots = listed_slots(ids)
    lane = lax.broadcasted_iota(jnp.int32, slots.shape, 1)
    weight = jnp.zeros(slots.shape, jnp.float32)
    for e in range(GROUPS):
        chosen = jnp.sum(jnp.where(ids == e, norm, 0.0), axis=1, keepdims=True)
        weight = weight + jnp.where(lane // PART == e, chosen, 0.0)
    return slots * weight


def mix_kernel(ids_ref, gates_ref, *refs):
    states, home_ref, outs = refs[:DIRS], refs[DIRS], refs[DIRS + 1 :]
    mixing = spread([weighted_slots(ids_ref[d], gates_ref[d]) for d in range(DIRS)])
    high = mixing.astype(jnp.bfloat16)
    low = (mixing - high.astype(jnp.float32)).astype(jnp.bfloat16)
    rows = home_ref[...]
    width = rows.shape[1]
    mixed = dot(high, rows) + dot(low, rows)
    for q in range(FOLD):
        for d in range(DIRS):
            at = (q * DIRS + d) * ROWS
            old = states[d][:, q * width : (q + 1) * width].astype(jnp.float32)
            outs[d][:, q * width : (q + 1) * width] = (old + mixed[at : at + ROWS]).astype(
                jnp.bfloat16
            )


def expert_step(states, ids, gates, weights):
    rows, model = states[0].shape
    width = model // FOLD
    (sent,) = local_call(list_kernel, [(GROUPS * PART, width)], ids, *states)
    held = group_exchange(sent)
    near = local_call(unfold_kernel, [(LISTED, model)] * DIRS, held)
    owns, gots = [], []
    for d in range(DIRS):
        far = chip_swap(near[d], 2)
        (pair,) = local_call(pair_kernel, [(2 * LISTED, model)], near[d], far)
        other = chip_swap(pair, 1)
        done, sent_back = local_call(
            expert_kernel, [(2 * LISTED, model)] * 2, *weights, pair, other
        )
        got = chip_swap(sent_back, 1)
        own, passed = local_call(add_kernel, [(LISTED, model)] * 2, done, got)
        owns.append(own)
        gots.append(chip_swap(passed, 2))
    (summed,) = local_call(fold_kernel, [(GROUPS * PART, width)], *owns, *gots)
    home = group_exchange(summed)
    return local_call(mix_kernel, [(rows, model)] * DIRS, ids, gates, *states, home)


def body(activations, expert_ids, gate_values, w_gate, w_up, w_down):
    own = [w_gate[0], w_up[0], w_down[0]]
    weights = own + [core_swap(value) for value in own]
    states = [activations[d] for d in range(DIRS)]
    for step in range(STEPS):
        updated = expert_step(states, expert_ids[step], gate_values[step], weights)
        states = [section_shift(updated[0], 1), section_shift(updated[1], -1)]
    return jnp.stack(states)


def solution(mesh):
    placed = (
        P(None, ("section", "expert"), None),
        P(None, None, ("section", "expert"), None),
        P(None, None, ("section", "expert"), None),
        P("section", None, "expert"),
        P("section", None, "expert"),
        P("section", "expert", None),
    )
    return jax.shard_map(
        body,
        mesh=mesh,
        in_specs=placed,
        out_specs=P(None, ("section", "expert"), None),
        check_vma=False,
    )
```

time: 754 us -> 313 us (0.42)
  the two profiles are of different devices: /device:TPU:62 before, /device:TPU:30 now
where the time goes in v2:
time: 313 us; the launch traced here: 312 us
  waiting for transfers between devices  165 us (53%)
  starting transfers between devices  88.3 us (28%)
  blocking collectives  28.4 us (9%)
  Pallas kernels  26.2 us (8%)
    ppermute x16, waiting for transfers between devices, chip_swap(): lax.ppermute(value, 'expert', pairs_of(lambda g, m, c: (g, m ^ k, c)))  80.5 us
    all_to_all x3, waiting for transfers between devices, group_exchange(): lax.all_to_all(value, 'expert', split_axis=0, concat_axis=0, axis_index_g...  58 us
    ppermute x16, starting transfers between devices, chip_swap(): lax.ppermute(value, 'expert', pairs_of(lambda g, m, c: (g, m ^ k, c)))  44.5 us
    all_to_all x1, blocking collectives, group_exchange(): lax.all_to_all(value, 'expert', split_axis=0, concat_axis=0, axis_index_g...  28.4 us
    ppermute x4, waiting for transfers between devices, section_shift(): lax.ppermute(value, 'section', [(s, (s + steps) % count) for s in range(c...  26.9 us
    pallas_call x20, Pallas kernels, local_call(): pl.pallas_call(kernel, out_shape=[jax.ShapeDtypeStruct(shape, jnp.bfloat1...  26.2 us
    all_to_all x3, starting transfers between devices, group_exchange(): lax.all_to_all(value, 'expert', split_axis=0, concat_axis=0, axis_index_g...  25.9 us
    ppermute x4, starting transfers between devices, section_shift(): lax.ppermute(value, 'section', [(s, (s + steps) % count) for s in range(c...  11.7 us
  transfers between devices with their start and end apart: 26, of which 23 were waited for; matrix products, arithmetic and copies ran while one was open for 0% of the time, Pallas kernels for 5%

profile of v2, /device:TPU:30, one launch (start us, length us, event | category | flops | bytes accessed | tf_op | source)
XLA Modules:
  0.0 311.7 jit_solution(15854751246317793281)
XLA Ops:
  2.8 15.1 %all-to-all-start = ((bf16[4,24,2048]{2,1,0:T(8,128)(2,1)}), bf16[4,24,2048]{2,1,0:T(8,128)(2,1)S(1)}, u32[]{:S(2)}, u32[]{:S(2)}) async-start(bf16[4,24,2048]{2,1,0:T(8,128)(2,1)} %bitcast.9), calls=%async_computation | async-start | bytes 786432 | tf_op jit(solution)/shard_map/all_to_all | solution.py:40
  19.8 2.4 collective-permute-start.1
  22.2 1.9 collective-permute-start.2
  24.2 14.7 %all-to-all-done = bf16[4,24,2048]{2,1,0:T(8,128)(2,1)S(1)} async-done(((bf16[4,24,2048]{2,1,0:T(8,128)(2,1)}), bf16[4,24,2048]{2,1,0:T(8,128)(2,1)S(1)}, u32[]{:S(2)}, u32[]{:S(2)}) %all-to-all-start) | async-done | bytes 393248 | tf_op jit(solution)/shard_map/all_to_all | solution.py:40
  39.2 8.3 %collective-permute-start.6 = (bf16[24,4096]{1,0:T(8,128)(2,1)S(1)}, bf16[24,4096]{1,0:T(8,128)(2,1)S(1)}, u32[]{:S(2)}, u32[]{:S(2)}) collective-permute-start(bf16[24,4096]{1,0:T(8,128)(2,1)S(1)} %get-tuple-element.33.near_ref), channel_id=1, source_target_pairs={{0,4},{1,5},{2,6},{3,7},{4,0},{5,1},{6,2},{7,3},{8,12},{9,13},{10,... | collective-permute-start | bytes 589832 | tf_op jit(solution)/shard_map/ppermute | solution.py:46
  49.5 11.9 %collective-permute-done.6.far_ref = bf16[24,4096]{1,0:T(8,128)(2,1)S(1)} collective-permute-done((bf16[24,4096]{1,0:T(8,128)(2,1)S(1)}, bf16[24,4096]{1,0:T(8,128)(2,1)S(1)}, u32[]{:S(2)}, u32[]{:S(2)}) %collective-permute-start.6) | collective-permute-done | bytes 196640 | tf_op jit(solution)/shard_map/ppermute | solution.py:46
  63.9 3.4 %collective-permute-start.4 = (bf16[48,4096]{1,0:T(8,128)(2,1)S(1)}, bf16[48,4096]{1,0:T(8,128)(2,1)S(1)}, u32[]{:S(2)}, u32[]{:S(2)}) collective-permute-start(bf16[48,4096]{1,0:T(8,128)(2,1)S(1)} %shard_map.66.refs_6_), channel_id=1, source_target_pairs={{0,2},{1,3},{2,0},{3,1},{4,6},{5,7},{6,4},{7,5},{8,10},{9,11},{10,... | collective-permute-start | bytes 1179656 | tf_op jit(solution)/shard_map/ppermute | solution.py:46
  67.3 8.0 %collective-permute-done.7.refs_7_ = bf16[48,4096]{1,0:T(8,128)(2,1)S(1)} collective-permute-done((bf16[48,4096]{1,0:T(8,128)(2,1)S(1)}, bf16[48,4096]{1,0:T(8,128)(2,1)S(1)}, u32[]{:S(2)}, u32[]{:S(2)}) %collective-permute-start.7) | collective-permute-done | bytes 393248 | tf_op jit(solution)/shard_map/ppermute | solution.py:46
  75.3 4.0 %shard_map.70 = (bf16[48,4096]{1,0:T(8,128)(2,1)S(1)}, bf16[48,4096]{1,0:T(8,128)(2,1)S(1)}) custom-call(bf16[4096,128]{1,0:T(8,128)(2,1)} %bitcast.32, bf16[4096,128]{1,0:T(8,128)(2,1)} %bitcast.37, bf16[128,4096]{1,0:T(8,128)(2,1)} %bitcast.43, bf16[4096,128]{1,0:T(8,128)(2,1)} %collective-permute-done.refs_3_, ...), custom_call_target="tpu_custom_call" | custom-call | tf_op jit(solution)/shard_map/pallas_call | solution.py:59
  81.3 2.2 collective-permute-done.4.refs_7_
  83.5 4.0 %shard_map.67 = (bf16[48,4096]{1,0:T(8,128)(2,1)S(1)}, bf16[48,4096]{1,0:T(8,128)(2,1)S(1)}) custom-call(bf16[4096,128]{1,0:T(8,128)(2,1)} %bitcast.33, bf16[4096,128]{1,0:T(8,128)(2,1)} %bitcast.38, bf16[128,4096]{1,0:T(8,128)(2,1)} %bitcast.44, bf16[4096,128]{1,0:T(8,128)(2,1)} %collective-permute-done.refs_3_, ...), custom_call_target="tpu_custom_call" | custom-call | tf_op jit(solution)/shard_map/pallas_call | solution.py:59
  87.5 1.9 collective-permute-start.5
  89.4 4.6 %collective-permute-done.8.got_ref = bf16[48,4096]{1,0:T(8,128)(2,1)S(1)} collective-permute-done((bf16[48,4096]{1,0:T(8,128)(2,1)S(1)}, bf16[48,4096]{1,0:T(8,128)(2,1)S(1)}, u32[]{:S(2)}, u32[]{:S(2)}) %collective-permute-start.8) | collective-permute-done | bytes 393248 | tf_op jit(solution)/shard_map/ppermute | solution.py:46
  96.0 3.5 %collective-permute-done.5.got_ref = bf16[48,4096]{1,0:T(8,128)(2,1)S(1)} collective-permute-done((bf16[48,4096]{1,0:T(8,128)(2,1)S(1)}, bf16[48,4096]{1,0:T(8,128)(2,1)S(1)}, u32[]{:S(2)}, u32[]{:S(2)}) %collective-permute-start.5) | collective-permute-done | bytes 393248 | tf_op jit(solution)/shard_map/ppermute | solution.py:46
  99.7 2.3 collective-permute-start.9
  102.0 7.9 %collective-permute-done.10.refs_3_ = bf16[24,4096]{1,0:T(8,128)(2,1)S(1)} collective-permute-done((bf16[24,4096]{1,0:T(8,128)(2,1)S(1)}, bf16[24,4096]{1,0:T(8,128)(2,1)S(1)}, u32[]{:S(2)}, u32[]{:S(2)}) %collective-permute-start.10) | collective-permute-done | bytes 196640 | tf_op jit(solution)/shard_map/ppermute | solution.py:46
  109.9 2.2 collective-permute-done.9.refs_2_
  113.5 4.8 %all-to-all-start.1 = ((bf16[4,24,2048]{2,1,0:T(8,128)(2,1)}), bf16[4,24,2048]{2,1,0:T(8,128)(2,1)S(1)}, u32[]{:S(2)}, u32[]{:S(2)}) async-start(bf16[4,24,2048]{2,1,0:T(8,128)(2,1)} %bitcast.11), calls=%async_computation.1 | async-start | bytes 786432 | tf_op jit(solution)/shard_map/all_to_all | solution.py:40
  118.4 20.8 %all-to-all-done.1 = bf16[4,24,2048]{2,1,0:T(8,128)(2,1)S(1)} async-done(((bf16[4,24,2048]{2,1,0:T(8,128)(2,1)}), bf16[4,24,2048]{2,1,0:T(8,128)(2,1)S(1)}, u32[]{:S(2)}, u32[]{:S(2)}) %all-to-all-start.1) | async-done | bytes 393248 | tf_op jit(solution)/shard_map/all_to_all | solution.py:40
  139.2 2.1 shard_map.73
  141.3 2.0 collective-permute-start.11
  143.3 3.8 %collective-permute-start.12 = (bf16[64,4096]{1,0:T(8,128)(2,1)S(1)}, bf16[64,4096]{1,0:T(8,128)(2,1)S(1)}, u32[]{:S(2)}, u32[]{:S(2)}) collective-permute-start(bf16[64,4096]{1,0:T(8,128)(2,1)S(1)} %get-tuple-element.40), channel_id=1, source_target_pairs={{0,480},{32,0},{64,32},{96,64},{128,96},{160,128},{192,160},{224,1... | collective-permute-start | bytes 1572872 | tf_op jit(solution)/shard_map/ppermute | solution.py:55
  147.3 7.1 %collective-permute-done.11.refs_0_ = bf16[64,4096]{1,0:T(8,128)(2,1)S(1)} collective-permute-done((bf16[64,4096]{1,0:T(8,128)(2,1)S(1)}, bf16[64,4096]{1,0:T(8,128)(2,1)S(1)}, u32[]{:S(2)}, u32[]{:S(2)}) %collective-permute-start.11) | collective-permute-done | bytes 524320 | tf_op jit(solution)/shard_map/ppermute | solution.py:55
  154.4 5.2 %collective-permute-done.12.refs_1_ = bf16[64,4096]{1,0:T(8,128)(2,1)S(1)} collective-permute-done((bf16[64,4096]{1,0:T(8,128)(2,1)S(1)}, bf16[64,4096]{1,0:T(8,128)(2,1)S(1)}, u32[]{:S(2)}, u32[]{:S(2)}) %collective-permute-start.12) | collective-permute-done | bytes 524320 | tf_op jit(solution)/shard_map/ppermute | solution.py:55
  160.4 28.4 %all_to_all.44 = bf16[4,24,2048]{2,1,0:T(8,128)(2,1)S(1)} all-to-all(bf16[4,24,2048]{2,1,0:T(8,128)(2,1)S(1)} %bitcast.25), channel_id=1, replica_groups={{0,8,16,24},{1,9,17,25},{2,10,18,26},{3,11,19,27},{4,12,20,28},{5,13,21..., dimensions={0} | all-to-all | bytes 786432 | tf_op jit(solution)/shard_map/all_to_all | solution.py:40
  189.2 5.7 %collective-permute-start.16 = (bf16[24,4096]{1,0:T(8,128)(2,1)S(1)}, bf16[24,4096]{1,0:T(8,128)(2,1)S(1)}, u32[]{:S(2)}, u32[]{:S(2)}) collective-permute-start(bf16[24,4096]{1,0:T(8,128)(2,1)S(1)} %get-tuple-element.45.near_ref), channel_id=1, source_target_pairs={{0,4},{1,5},{2,6},{3,7},{4,0},{5,1},{6,2},{7,3},{8,12},{9,13},{10,... | collective-permute-start | bytes 589832 | tf_op jit(solution)/shard_map/ppermute | solution.py:46
  194.9 1.9 collective-permute-start.13
  196.8 10.2 %collective-permute-done.16.far_ref = bf16[24,4096]{1,0:T(8,128)(2,1)S(1)} collective-permute-done((bf16[24,4096]{1,0:T(8,128)(2,1)S(1)}, bf16[24,4096]{1,0:T(8,128)(2,1)S(1)}, u32[]{:S(2)}, u32[]{:S(2)}) %collective-permute-start.16) | collective-permute-done | bytes 196640 | tf_op jit(solution)/shard_map/ppermute | solution.py:46
  207.1 1.9 collective-permute-start.17
  209.4 3.5 %collective-permute-start.14 = (bf16[48,4096]{1,0:T(8,128)(2,1)S(1)}, bf16[48,4096]{1,0:T(8,128)(2,1)S(1)}, u32[]{:S(2)}, u32[]{:S(2)}) collective-permute-start(bf16[48,4096]{1,0:T(8,128)(2,1)S(1)} %shard_map.76.refs_6_), channel_id=1, source_target_pairs={{0,2},{1,3},{2,0},{3,1},{4,6},{5,7},{6,4},{7,5},{8,10},{9,11},{10,... | collective-permute-start | bytes 1179656 | tf_op jit(solution)/shard_map/ppermute | solution.py:46
  213.0 8.0 %collective-permute-done.17.refs_7_ = bf16[48,4096]{1,0:T(8,128)(2,1)S(1)} collective-permute-done((bf16[48,4096]{1,0:T(8,128)(2,1)S(1)}, bf16[48,4096]{1,0:T(8,128)(2,1)S(1)}, u32[]{:S(2)}, u32[]{:S(2)}) %collective-permute-start.17) | collective-permute-done | bytes 393248 | tf_op jit(solution)/shard_map/ppermute | solution.py:46
  221.0 4.0 %shard_map.80 = (bf16[48,4096]{1,0:T(8,128)(2,1)S(1)}, bf16[48,4096]{1,0:T(8,128)(2,1)S(1)}) custom-call(bf16[4096,128]{1,0:T(8,128)(2,1)} %bitcast.34, bf16[4096,128]{1,0:T(8,128)(2,1)} %bitcast.39, bf16[128,4096]{1,0:T(8,128)(2,1)} %bitcast.45, bf16[4096,128]{1,0:T(8,128)(2,1)} %collective-permute-done.refs_3_, ...), custom_call_target="tpu_custom_call" | custom-call | tf_op jit(solution)/shard_map/pallas_call | solution.py:59
  227.0 2.2 collective-permute-done.14.refs_7_
  229.2 4.0 %shard_map.77 = (bf16[48,4096]{1,0:T(8,128)(2,1)S(1)}, bf16[48,4096]{1,0:T(8,128)(2,1)S(1)}) custom-call(bf16[4096,128]{1,0:T(8,128)(2,1)} %bitcast.35, bf16[4096,128]{1,0:T(8,128)(2,1)} %bitcast.40, bf16[128,4096]{1,0:T(8,128)(2,1)} %bitcast.46, bf16[4096,128]{1,0:T(8,128)(2,1)} %collective-permute-done.refs_3_, ...), custom_call_target="tpu_custom_call" | custom-call | tf_op jit(solution)/shard_map/pallas_call | solution.py:59
  233.2 1.9 collective-permute-start.15
  235.2 5.0 %collective-permute-done.18.got_ref = bf16[48,4096]{1,0:T(8,128)(2,1)S(1)} collective-permute-done((bf16[48,4096]{1,0:T(8,128)(2,1)S(1)}, bf16[48,4096]{1,0:T(8,128)(2,1)S(1)}, u32[]{:S(2)}, u32[]{:S(2)}) %collective-permute-start.18) | collective-permute-done | bytes 393248 | tf_op jit(solution)/shard_map/ppermute | solution.py:46
  240.2 1.9 collective-permute-start.20
  242.2 3.1 %collective-permute-done.15.got_ref = bf16[48,4096]{1,0:T(8,128)(2,1)S(1)} collective-permute-done((bf16[48,4096]{1,0:T(8,128)(2,1)S(1)}, bf16[48,4096]{1,0:T(8,128)(2,1)S(1)}, u32[]{:S(2)}, u32[]{:S(2)}) %collective-permute-start.15) | collective-permute-done | bytes 393248 | tf_op jit(solution)/shard_map/ppermute | solution.py:46
  245.4 2.0 collective-permute-start.19
  247.4 8.6 %collective-permute-done.20.refs_3_ = bf16[24,4096]{1,0:T(8,128)(2,1)S(1)} collective-permute-done((bf16[24,4096]{1,0:T(8,128)(2,1)S(1)}, bf16[24,4096]{1,0:T(8,128)(2,1)S(1)}, u32[]{:S(2)}, u32[]{:S(2)}) %collective-permute-start.20) | collective-permute-done | bytes 196640 | tf_op jit(solution)/shard_map/ppermute | solution.py:46
  256.0 2.2 collective-permute-done.19.refs_2_
  259.6 6.0 %all-to-all-start.3 = ((bf16[4,24,2048]{2,1,0:T(8,128)(2,1)}), bf16[4,24,2048]{2,1,0:T(8,128)(2,1)S(1)}, u32[]{:S(2)}, u32[]{:S(2)}) async-start(bf16[4,24,2048]{2,1,0:T(8,128)(2,1)} %bitcast.15), calls=%async_computation.3 | async-start | bytes 786432 | tf_op jit(solution)/shard_map/all_to_all | solution.py:40
  265.6 22.5 %all-to-all-done.3 = bf16[4,24,2048]{2,1,0:T(8,128)(2,1)S(1)} async-done(((bf16[4,24,2048]{2,1,0:T(8,128)(2,1)}), bf16[4,24,2048]{2,1,0:T(8,128)(2,1)S(1)}, u32[]{:S(2)}, u32[]{:S(2)}) %all-to-all-start.3) | async-done | bytes 393248 | tf_op jit(solution)/shard_map/all_to_all | solution.py:40
  288.1 2.1 shard_map.83
  290.2 1.9 collective-permute-start.21
  292.2 3.9 %collective-permute-start.22 = (bf16[64,4096]{1,0:T(8,128)(2,1)S(1)}, bf16[64,4096]{1,0:T(8,128)(2,1)S(1)}, u32[]{:S(2)}, u32[]{:S(2)}) collective-permute-start(bf16[64,4096]{1,0:T(8,128)(2,1)S(1)} %get-tuple-element.52), channel_id=1, source_target_pairs={{0,480},{32,0},{64,32},{96,64},{128,96},{160,128},{192,160},{224,1... | collective-permute-start | bytes 1572872 | tf_op jit(solution)/shard_map/ppermute | solution.py:55
  296.1 9.3 %collective-permute-done.21 = bf16[64,4096]{1,0:T(8,128)(2,1)S(1)} collective-permute-done((bf16[64,4096]{1,0:T(8,128)(2,1)S(1)}, bf16[64,4096]{1,0:T(8,128)(2,1)S(1)}, u32[]{:S(2)}, u32[]{:S(2)}) %collective-permute-start.21) | collective-permute-done | bytes 524320 | tf_op jit(solution)/shard_map/ppermute | solution.py:55
  305.4 5.2 %collective-permute-done.22 = bf16[64,4096]{1,0:T(8,128)(2,1)S(1)} collective-permute-done((bf16[64,4096]{1,0:T(8,128)(2,1)S(1)}, bf16[64,4096]{1,0:T(8,128)(2,1)S(1)}, u32[]{:S(2)}, u32[]{:S(2)}) %collective-permute-start.22) | collective-permute-done | bytes 524320 | tf_op jit(solution)/shard_map/ppermute | solution.py:55
  (49 shorter events, 21.2 us)
Async XLA Ops:
  0.0 1.3 copy-start.6
  1.3 1.5 copy-start
  1.3 1.5 copy-start.1
  1.4 16.5 %copy-start.4 = (bf16[1,4096,128]{2,1,0:T(8,128)(2,1)S(1)}, bf16[1,4096,128]{2,1,0:T(8,128)(2,1)}, u32[]{:S(2)}) copy-start(bf16[1,4096,128]{2,1,0:T(8,128)(2,1)} %param.9) | copy-start | bytes 3145732
  1.4 18.4 %copy-start.5 = (bf16[1,4096,128]{2,1,0:T(8,128)(2,1)S(1)}, bf16[1,4096,128]{2,1,0:T(8,128)(2,1)}, u32[]{:S(2)}) copy-start(bf16[1,4096,128]{2,1,0:T(8,128)(2,1)} %param.10) | copy-start | bytes 3145732
  2.8 36.1 %all-to-all-start = ((bf16[4,24,2048]{2,1,0:T(8,128)(2,1)}), bf16[4,24,2048]{2,1,0:T(8,128)(2,1)S(1)}, u32[]{:S(2)}, u32[]{:S(2)}) async-start(bf16[4,24,2048]{2,1,0:T(8,128)(2,1)} %bitcast.9), calls=%async_computation | async-start | bytes 786432 | tf_op jit(solution)/shard_map/all_to_all | solution.py:40
  17.9 49.4 %collective-permute-start = (bf16[4096,128]{1,0:T(8,128)(2,1)S(1)}, bf16[4096,128]{1,0:T(8,128)(2,1)}, u32[]{:S(2)}, u32[]{:S(2)}) collective-permute-start(bf16[4096,128]{1,0:T(8,128)(2,1)S(1)} %bitcast.36), channel_id=1, source_target_pairs={{0,1},{1,0},{2,3},{3,2},{4,5},{5,4},{6,7},{7,6},{8,9},{9,8},{10,11... | collective-permute-start | bytes 3145736 | tf_op jit(solution)/shard_map/ppermute | solution.py:50
  19.8 47.5 %collective-permute-start.1 = (bf16[4096,128]{1,0:T(8,128)(2,1)S(1)}, bf16[4096,128]{1,0:T(8,128)(2,1)}, u32[]{:S(2)}, u32[]{:S(2)}) collective-permute-start(bf16[4096,128]{1,0:T(8,128)(2,1)S(1)} %bitcast.41), channel_id=1, source_target_pairs={{0,1},{1,0},{2,3},{3,2},{4,5},{5,4},{6,7},{7,6},{8,9},{9,8},{10,11... | collective-permute-start | bytes 3145736 | tf_op jit(solution)/shard_map/ppermute | solution.py:50
  22.2 45.1 %collective-permute-start.2 = (bf16[128,4096]{1,0:T(8,128)(2,1)}, bf16[128,4096]{1,0:T(8,128)(2,1)}, u32[]{:S(2)}, u32[]{:S(2)}) collective-permute-start(bf16[128,4096]{1,0:T(8,128)(2,1)} %bitcast.42), channel_id=1, source_target_pairs={{0,1},{1,0},{2,3},{3,2},{4,5},{5,4},{6,7},{7,6},{8,9},{9,8},{10,11... | collective-permute-start | bytes 3145736 | tf_op jit(solution)/shard_map/ppermute | solution.py:50
  39.2 22.1 %collective-permute-start.6 = (bf16[24,4096]{1,0:T(8,128)(2,1)S(1)}, bf16[24,4096]{1,0:T(8,128)(2,1)S(1)}, u32[]{:S(2)}, u32[]{:S(2)}) collective-permute-start(bf16[24,4096]{1,0:T(8,128)(2,1)S(1)} %get-tuple-element.33.near_ref), channel_id=1, source_target_pairs={{0,4},{1,5},{2,6},{3,7},{4,0},{5,1},{6,2},{7,3},{8,12},{9,13},{10,... | collective-permute-start | bytes 589832 | tf_op jit(solution)/shard_map/ppermute | solution.py:46
  47.5 16.3 %collective-permute-start.3 = (bf16[24,4096]{1,0:T(8,128)(2,1)S(1)}, bf16[24,4096]{1,0:T(8,128)(2,1)S(1)}, u32[]{:S(2)}, u32[]{:S(2)}) collective-permute-start(bf16[24,4096]{1,0:T(8,128)(2,1)S(1)} %get-tuple-element.29.near_ref), channel_id=1, source_target_pairs={{0,4},{1,5},{2,6},{3,7},{4,0},{5,1},{6,2},{7,3},{8,12},{9,13},{10,... | collective-permute-start | bytes 589832 | tf_op jit(solution)/shard_map/ppermute | solution.py:46
  61.4 13.9 %collective-permute-start.7 = (bf16[48,4096]{1,0:T(8,128)(2,1)S(1)}, bf16[48,4096]{1,0:T(8,128)(2,1)S(1)}, u32[]{:S(2)}, u32[]{:S(2)}) collective-permute-start(bf16[48,4096]{1,0:T(8,128)(2,1)S(1)} %shard_map.69.refs_6_), channel_id=1, source_target_pairs={{0,2},{1,3},{2,0},{3,1},{4,6},{5,7},{6,4},{7,5},{8,10},{9,11},{10,... | collective-permute-start | bytes 1179656 | tf_op jit(solution)/shard_map/ppermute | solution.py:46
  63.9 19.6 %collective-permute-start.4 = (bf16[48,4096]{1,0:T(8,128)(2,1)S(1)}, bf16[48,4096]{1,0:T(8,128)(2,1)S(1)}, u32[]{:S(2)}, u32[]{:S(2)}) collective-permute-start(bf16[48,4096]{1,0:T(8,128)(2,1)S(1)} %shard_map.66.refs_6_), channel_id=1, source_target_pairs={{0,2},{1,3},{2,0},{3,1},{4,6},{5,7},{6,4},{7,5},{8,10},{9,11},{10,... | collective-permute-start | bytes 1179656 | tf_op jit(solution)/shard_map/ppermute | solution.py:46
  79.3 14.7 %collective-permute-start.8 = (bf16[48,4096]{1,0:T(8,128)(2,1)S(1)}, bf16[48,4096]{1,0:T(8,128)(2,1)S(1)}, u32[]{:S(2)}, u32[]{:S(2)}) collective-permute-start(bf16[48,4096]{1,0:T(8,128)(2,1)S(1)} %get-tuple-element.35), channel_id=1, source_target_pairs={{0,2},{1,3},{2,0},{3,1},{4,6},{5,7},{6,4},{7,5},{8,10},{9,11},{10,... | collective-permute-start | bytes 1179656 | tf_op jit(solution)/shard_map/ppermute | solution.py:46
  87.5 12.1 %collective-permute-start.5 = (bf16[48,4096]{1,0:T(8,128)(2,1)S(1)}, bf16[48,4096]{1,0:T(8,128)(2,1)S(1)}, u32[]{:S(2)}, u32[]{:S(2)}) collective-permute-start(bf16[48,4096]{1,0:T(8,128)(2,1)S(1)} %get-tuple-element.31), channel_id=1, source_target_pairs={{0,2},{1,3},{2,0},{3,1},{4,6},{5,7},{6,4},{7,5},{8,10},{9,11},{10,... | collective-permute-start | bytes 1179656 | tf_op jit(solution)/shard_map/ppermute | solution.py:46
  94.1 15.8 %collective-permute-start.10 = (bf16[24,4096]{1,0:T(8,128)(2,1)S(1)}, bf16[24,4096]{1,0:T(8,128)(2,1)S(1)}, u32[]{:S(2)}, u32[]{:S(2)}) collective-permute-start(bf16[24,4096]{1,0:T(8,128)(2,1)S(1)} %get-tuple-element.38), channel_id=1, source_target_pairs={{0,4},{1,5},{2,6},{3,7},{4,0},{5,1},{6,2},{7,3},{8,12},{9,13},{10,... | collective-permute-start | bytes 589832 | tf_op jit(solution)/shard_map/ppermute | solution.py:46
  99.7 12.4 %collective-permute-start.9 = (bf16[24,4096]{1,0:T(8,128)(2,1)S(1)}, bf16[24,4096]{1,0:T(8,128)(2,1)S(1)}, u32[]{:S(2)}, u32[]{:S(2)}) collective-permute-start(bf16[24,4096]{1,0:T(8,128)(2,1)S(1)} %get-tuple-element.37), channel_id=1, source_target_pairs={{0,4},{1,5},{2,6},{3,7},{4,0},{5,1},{6,2},{7,3},{8,12},{9,13},{10,... | collective-permute-start | bytes 589832 | tf_op jit(solution)/shard_map/ppermute | solution.py:46
  113.4 4.8 %copy-start.7 = (f32[2,2,64,8]{2,3,1,0:T(8,128)S(1)}, f32[2,2,64,8]{2,3,1,0:T(8,128)}, u32[]{:S(2)}) copy-start(f32[2,2,64,8]{2,3,1,0:T(8,128)} %param.8) | copy-start | bytes 24580
  113.5 25.7 %all-to-all-start.1 = ((bf16[4,24,2048]{2,1,0:T(8,128)(2,1)}), bf16[4,24,2048]{2,1,0:T(8,128)(2,1)S(1)}, u32[]{:S(2)}, u32[]{:S(2)}) async-start(bf16[4,24,2048]{2,1,0:T(8,128)(2,1)} %bitcast.11), calls=%async_computation.1 | async-start | bytes 786432 | tf_op jit(solution)/shard_map/all_to_all | solution.py:40
  141.3 13.1 %collective-permute-start.11 = (bf16[64,4096]{1,0:T(8,128)(2,1)S(1)}, bf16[64,4096]{1,0:T(8,128)(2,1)S(1)}, u32[]{:S(2)}, u32[]{:S(2)}) collective-permute-start(bf16[64,4096]{1,0:T(8,128)(2,1)S(1)} %get-tuple-element.39), channel_id=1, source_target_pairs={{0,32},{32,64},{64,96},{96,128},{128,160},{160,192},{192,224},{224... | collective-permute-start | bytes 1572872 | tf_op jit(solution)/shard_map/ppermute | solution.py:55
  143.3 16.3 %collective-permute-start.12 = (bf16[64,4096]{1,0:T(8,128)(2,1)S(1)}, bf16[64,4096]{1,0:T(8,128)(2,1)S(1)}, u32[]{:S(2)}, u32[]{:S(2)}) collective-permute-start(bf16[64,4096]{1,0:T(8,128)(2,1)S(1)} %get-tuple-element.40), channel_id=1, source_target_pairs={{0,480},{32,0},{64,32},{96,64},{128,96},{160,128},{192,160},{224,1... | collective-permute-start | bytes 1572872 | tf_op jit(solution)/shard_map/ppermute | solution.py:55
  154.4 5.8 %copy-start.2 = (bf16[64,4096]{1,0:T(8,128)(2,1)}, bf16[64,4096]{1,0:T(8,128)(2,1)S(1)}, u32[]{:S(2)}) copy-start(bf16[64,4096]{1,0:T(8,128)(2,1)S(1)} %collective-permute-done.11.refs_0_) | copy-start | bytes 1572868
  159.7 0.8 copy-start.3
  189.2 17.9 %collective-permute-start.16 = (bf16[24,4096]{1,0:T(8,128)(2,1)S(1)}, bf16[24,4096]{1,0:T(8,128)(2,1)S(1)}, u32[]{:S(2)}, u32[]{:S(2)}) collective-permute-start(bf16[24,4096]{1,0:T(8,128)(2,1)S(1)} %get-tuple-element.45.near_ref), channel_id=1, source_target_pairs={{0,4},{1,5},{2,6},{3,7},{4,0},{5,1},{6,2},{7,3},{8,12},{9,13},{10,... | collective-permute-start | bytes 589832 | tf_op jit(solution)/shard_map/ppermute | solution.py:46
  194.9 14.5 %collective-permute-start.13 = (bf16[24,4096]{1,0:T(8,128)(2,1)S(1)}, bf16[24,4096]{1,0:T(8,128)(2,1)S(1)}, u32[]{:S(2)}, u32[]{:S(2)}) collective-permute-start(bf16[24,4096]{1,0:T(8,128)(2,1)S(1)} %get-tuple-element.41.near_ref), channel_id=1, source_target_pairs={{0,4},{1,5},{2,6},{3,7},{4,0},{5,1},{6,2},{7,3},{8,12},{9,13},{10,... | collective-permute-start | bytes 589832 | tf_op jit(solution)/shard_map/ppermute | solution.py:46
  207.1 13.9 %collective-permute-start.17 = (bf16[48,4096]{1,0:T(8,128)(2,1)S(1)}, bf16[48,4096]{1,0:T(8,128)(2,1)S(1)}, u32[]{:S(2)}, u32[]{:S(2)}) collective-permute-start(bf16[48,4096]{1,0:T(8,128)(2,1)S(1)} %shard_map.79.refs_6_), channel_id=1, source_target_pairs={{0,2},{1,3},{2,0},{3,1},{4,6},{5,7},{6,4},{7,5},{8,10},{9,11},{10,... | collective-permute-start | bytes 1179656 | tf_op jit(solution)/shard_map/ppermute | solution.py:46
  209.4 19.7 %collective-permute-start.14 = (bf16[48,4096]{1,0:T(8,128)(2,1)S(1)}, bf16[48,4096]{1,0:T(8,128)(2,1)S(1)}, u32[]{:S(2)}, u32[]{:S(2)}) collective-permute-start(bf16[48,4096]{1,0:T(8,128)(2,1)S(1)} %shard_map.76.refs_6_), channel_id=1, source_target_pairs={{0,2},{1,3},{2,0},{3,1},{4,6},{5,7},{6,4},{7,5},{8,10},{9,11},{10,... | collective-permute-start | bytes 1179656 | tf_op jit(solution)/shard_map/ppermute | solution.py:46
  225.1 15.1 %collective-permute-start.18 = (bf16[48,4096]{1,0:T(8,128)(2,1)S(1)}, bf16[48,4096]{1,0:T(8,128)(2,1)S(1)}, u32[]{:S(2)}, u32[]{:S(2)}) collective-permute-start(bf16[48,4096]{1,0:T(8,128)(2,1)S(1)} %get-tuple-element.47), channel_id=1, source_target_pairs={{0,2},{1,3},{2,0},{3,1},{4,6},{5,7},{6,4},{7,5},{8,10},{9,11},{10,... | collective-permute-start | bytes 1179656 | tf_op jit(solution)/shard_map/ppermute | solution.py:46
  233.2 12.1 %collective-permute-start.15 = (bf16[48,4096]{1,0:T(8,128)(2,1)S(1)}, bf16[48,4096]{1,0:T(8,128)(2,1)S(1)}, u32[]{:S(2)}, u32[]{:S(2)}) collective-permute-start(bf16[48,4096]{1,0:T(8,128)(2,1)S(1)} %get-tuple-element.43), channel_id=1, source_target_pairs={{0,2},{1,3},{2,0},{3,1},{4,6},{5,7},{6,4},{7,5},{8,10},{9,11},{10,... | collective-permute-start | bytes 1179656 | tf_op jit(solution)/shard_map/ppermute | solution.py:46
  240.2 15.8 %collective-permute-start.20 = (bf16[24,4096]{1,0:T(8,128)(2,1)S(1)}, bf16[24,4096]{1,0:T(8,128)(2,1)S(1)}, u32[]{:S(2)}, u32[]{:S(2)}) collective-permute-start(bf16[24,4096]{1,0:T(8,128)(2,1)S(1)} %get-tuple-element.50), channel_id=1, source_target_pairs={{0,4},{1,5},{2,6},{3,7},{4,0},{5,1},{6,2},{7,3},{8,12},{9,13},{10,... | collective-permute-start | bytes 589832 | tf_op jit(solution)/shard_map/ppermute | solution.py:46
  245.4 12.8 %collective-permute-start.19 = (bf16[24,4096]{1,0:T(8,128)(2,1)S(1)}, bf16[24,4096]{1,0:T(8,128)(2,1)S(1)}, u32[]{:S(2)}, u32[]{:S(2)}) collective-permute-start(bf16[24,4096]{1,0:T(8,128)(2,1)S(1)} %get-tuple-element.49), channel_id=1, source_target_pairs={{0,4},{1,5},{2,6},{3,7},{4,0},{5,1},{6,2},{7,3},{8,12},{9,13},{10,... | collective-permute-start | bytes 589832 | tf_op jit(solution)/shard_map/ppermute | solution.py:46
  259.6 28.6 %all-to-all-start.3 = ((bf16[4,24,2048]{2,1,0:T(8,128)(2,1)}), bf16[4,24,2048]{2,1,0:T(8,128)(2,1)S(1)}, u32[]{:S(2)}, u32[]{:S(2)}) async-start(bf16[4,24,2048]{2,1,0:T(8,128)(2,1)} %bitcast.15), calls=%async_computation.3 | async-start | bytes 786432 | tf_op jit(solution)/shard_map/all_to_all | solution.py:40
  290.2 15.1 %collective-permute-start.21 = (bf16[64,4096]{1,0:T(8,128)(2,1)S(1)}, bf16[64,4096]{1,0:T(8,128)(2,1)S(1)}, u32[]{:S(2)}, u32[]{:S(2)}) collective-permute-start(bf16[64,4096]{1,0:T(8,128)(2,1)S(1)} %get-tuple-element.51), channel_id=1, source_target_pairs={{0,32},{32,64},{64,96},{96,128},{128,160},{160,192},{192,224},{224... | collective-permute-start | bytes 1572872 | tf_op jit(solution)/shard_map/ppermute | solution.py:55
  292.2 18.4 %collective-permute-start.22 = (bf16[64,4096]{1,0:T(8,128)(2,1)S(1)}, bf16[64,4096]{1,0:T(8,128)(2,1)S(1)}, u32[]{:S(2)}, u32[]{:S(2)}) collective-permute-start(bf16[64,4096]{1,0:T(8,128)(2,1)S(1)} %get-tuple-element.52), channel_id=1, source_target_pairs={{0,480},{32,0},{64,32},{96,64},{128,96},{160,128},{192,160},{224,1... | collective-permute-start | bytes 1572872 | tf_op jit(solution)/shard_map/ppermute | solution.py:55

commit v3 on v2

--- a/solution.py
+++ b/solution.py
@@ -17,7 +17,7 @@
 EACH = DIRS * MOST
 PART = FOLD * EACH
 LISTED = GROUPS * MOST
-PARAMS = pltpu.CompilerParams(vmem_limit_bytes=52 * 1024 * 1024)
+MIB = 1024 * 1024
 
 
 def device_at(g, m, c):
@@ -55,11 +55,11 @@
     return lax.ppermute(value, "section", [(s, (s + steps) % count) for s in range(count)])
 
 
-def local_call(kernel, shapes, *operands):
+def local_call(kernel, shapes, *operands, vmem=52):
     return pl.pallas_call(
         kernel,
         out_shape=[jax.ShapeDtypeStruct(shape, jnp.bfloat16) for shape in shapes],
-        compiler_params=PARAMS,
+        compiler_params=pltpu.CompilerParams(vmem_limit_bytes=vmem * MIB),
     )(*operands)
 
 
@@ -71,13 +71,13 @@
     return mask.astype(jnp.float32).astype(jnp.bfloat16)
 
 
-def listed_slots(ids):
-    shape = (ROWS, GROUPS * PART)
+def listed_slots(ids, part):
+    shape = (ROWS, GROUPS * part)
     lane = lax.broadcasted_iota(jnp.int32, shape, 1)
     member = jnp.zeros(shape, jnp.float32)
     for e in range(GROUPS):
         named = jnp.max((ids == e).astype(jnp.float32), axis=1, keepdims=True)
-        member = member + jnp.where(lane // PART == e, named, 0.0)
+        member = member + jnp.where(lane // part == e, named, 0.0)
     later = lax.broadcasted_iota(jnp.int32, (ROWS, ROWS), 0)
     earlier = lax.broadcasted_iota(jnp.int32, (ROWS, ROWS), 1)
     rank = dot(one_hot(earlier < later), member.astype(jnp.bfloat16))
@@ -104,7 +104,7 @@
 def list_kernel(ids_ref, *refs):
     states, out_ref = refs[:DIRS], refs[DIRS]
     width = out_ref.shape[1]
-    table = spread([listed_slots(ids_ref[d]) for d in range(DIRS)]).astype(jnp.bfloat16)
+    table = spread([listed_slots(ids_ref[d], PART) for d in range(DIRS)]).astype(jnp.bfloat16)
     stack = [ref[:, q * width : (q + 1) * width] for q in range(FOLD) for ref in states]
     rows = lax.dot_general(
         table,
@@ -171,47 +171,71 @@
     out_ref[...] = rows.astype(jnp.bfloat16)
 
 
-def weighted_slots(ids, gates):
+def split_kernel(home_ref, *outs):
+    rows = home_ref[...]
+    shape = (outs[0].shape[0], rows.shape[0])
+    to = lax.broadcasted_iota(jnp.int32, shape, 0)
+    at = lax.broadcasted_iota(jnp.int32, shape, 1)
+    for d, out in enumerate(outs):
+        same = (at // EACH == to // MOST) & (at % MOST == to % MOST) & ((at % EACH) // MOST == d)
+        out[...] = dot(one_hot(same), rows).astype(jnp.bfloat16)
+
+
+def weighted_slots(ids, gates, part):
     norm = gates / jnp.sum(gates, axis=1, keepdims=True)
-    slots = listed_slots(ids)
+    slots = listed_slots(ids, part)
     lane = lax.broadcasted_iota(jnp.int32, slots.shape, 1)
     weight = jnp.zeros(slots.shape, jnp.float32)
     for e in range(GROUPS):
         chosen = jnp.sum(jnp.where(ids == e, norm, 0.0), axis=1, keepdims=True)
-        weight = weight + jnp.where(lane // PART == e, chosen, 0.0)
+        weight = weight + jnp.where(lane // part == e, chosen, 0.0)
     return slots * weight
 
 
-def mix_kernel(ids_ref, gates_ref, *refs):
-    states, home_ref, outs = refs[:DIRS], refs[DIRS], refs[DIRS + 1 :]
-    mixing = spread([weighted_slots(ids_ref[d], gates_ref[d]) for d in range(DIRS)])
-    high = mixing.astype(jnp.bfloat16)
-    low = (mixing - high.astype(jnp.float32)).astype(jnp.bfloat16)
-    rows = home_ref[...]
-    width = rows.shape[1]
-    mixed = dot(high, rows) + dot(low, rows)
-    for q in range(FOLD):
+def mix_kernel(step, top):
+    def kernel(*refs):
+        routes, states, homes = refs[:DIRS], refs[DIRS : 2 * DIRS], refs[2 * DIRS : 3 * DIRS]
+        outs = refs[3 * DIRS :]
         for d in range(DIRS):
-            at = (q * DIRS + d) * ROWS
-            old = states[d][:, q * width : (q + 1) * width].astype(jnp.float32)
-            outs[d][:, q * width : (q + 1) * width] = (old + mixed[at : at + ROWS]).astype(
-                jnp.bfloat16
-            )
-
-
-def expert_step(states, ids, gates, weights):
-    rows, model = states[0].shape
+            route = routes[d][step]
+            table = weighted_slots(route[:, :top], route[:, top:], FOLD * MOST)
+            lane = lax.broadcasted_iota(jnp.int32, table.shape, 1)
+            fold = (lane % (FOLD * MOST)) // MOST
+            mixing = [jnp.where(fold == q, table, 0.0) for q in range(FOLD)]
+            mixing = jnp.concatenate(mixing, axis=0)
+            high = mixing.astype(jnp.bfloat16)
+            low = (mixing - high.astype(jnp.float32)).astype(jnp.bfloat16)
+            rows = homes[d][...]
+            width = rows.shape[1]
+            mixed = dot(high, rows) + dot(low, rows)
+            out = outs[0].at[d] if len(outs) == 1 else outs[d]
+            for q in range(FOLD):
+                old = states[d][:, q * width : (q + 1) * width].astype(jnp.float32)
+                new = old + mixed[q * ROWS : (q + 1) * ROWS]
+                out[:, q * width : (q + 1) * width] = new.astype(jnp.bfloat16)
+
+    return kernel
+
+
+def both_ways(values):
+    return [section_shift(value, 1 - 2 * d) for d, value in enumerate(values)]
+
+
+def expert_step(states, ids, weights, early):
+    model = states[0].shape[1]
     width = model // FOLD
     (sent,) = local_call(list_kernel, [(GROUPS * PART, width)], ids, *states)
-    held = group_exchange(sent)
+    held, early = lax.optimization_barrier((group_exchange(sent), early))
     near = local_call(unfold_kernel, [(LISTED, model)] * DIRS, held)
+    far = [chip_swap(near[d], 2) for d in range(DIRS)]
+    _, states = lax.optimization_barrier((far[1], states))
+    moved = both_ways(states)
     owns, gots = [], []
     for d in range(DIRS):
-        far = chip_swap(near[d], 2)
-        (pair,) = local_call(pair_kernel, [(2 * LISTED, model)], near[d], far)
+        (pair,) = local_call(pair_kernel, [(2 * LISTED, model)], near[d], far[d])
         other = chip_swap(pair, 1)
         done, sent_back = local_call(
-            expert_kernel, [(2 * LISTED, model)] * 2, *weights, pair, other
+            expert_kernel, [(2 * LISTED, model)] * 2, *weights, pair, other, vmem=32
         )
         got = chip_swap(sent_back, 1)
         own, passed = local_call(add_kernel, [(LISTED, model)] * 2, done, got)
@@ -219,17 +243,22 @@
         gots.append(chip_swap(passed, 2))
     (summed,) = local_call(fold_kernel, [(GROUPS * PART, width)], *owns, *gots)
     home = group_exchange(summed)
-    return local_call(mix_kernel, [(rows, model)] * DIRS, ids, gates, *states, home)
+    parts = local_call(split_kernel, [(GROUPS * PART // DIRS, width)] * DIRS, home)
+    return both_ways(parts), moved, early
 
 
 def body(activations, expert_ids, gate_values, w_gate, w_up, w_down):
     own = [w_gate[0], w_up[0], w_down[0]]
     weights = own + [core_swap(value) for value in own]
     states = [activations[d] for d in range(DIRS)]
+    shape, top = states[0].shape, expert_ids.shape[-1]
+    routes = jnp.concatenate([expert_ids.astype(jnp.float32), gate_values], axis=-1)
+    routes = both_ways([routes[:, d] for d in range(DIRS)])
     for step in range(STEPS):
-        updated = expert_step(states, expert_ids[step], gate_values[step], weights)
-        states = [section_shift(updated[0], 1), section_shift(updated[1], -1)]
-    return jnp.stack(states)
+        rows, moved, routes = expert_step(states, expert_ids[step], weights, routes)
+        outs = [shape] * DIRS if step < STEPS - 1 else [(DIRS, *shape)]
+        states = local_call(mix_kernel(step, top), outs, *routes, *moved, *rows)
+    return states[0]
 
 
 def solution(mesh):

time: 313 us -> 305 us (0.974)
  the two profiles are of different devices: /device:TPU:30 before, /device:TPU:14 now
where the time goes in v3:
time: 305 us; the launch traced here: 303 us
  waiting for transfers between devices  131 us (43%)
  starting transfers between devices  118 us (39%)
  Pallas kernels  23.3 us (8%)
  blocking collectives  22.4 us (7%)
  local copies, waits for them, and re-layouts  7.88 us (3%)
    ppermute x16, waiting for transfers between devices, chip_swap(): lax.ppermute(value, 'expert', pairs_of(lambda g, m, c: (g, m ^ k, c)))  81.3 us
    ppermute x16, starting transfers between devices, chip_swap(): lax.ppermute(value, 'expert', pairs_of(lambda g, m, c: (g, m ^ k, c)))  46.3 us
    ppermute x10, starting transfers between devices, section_shift(): lax.ppermute(value, 'section', [(s, (s + steps) % count) for s in range(c...  38.2 us
    all_to_all x3, waiting for transfers between devices, group_exchange(): lax.all_to_all(value, 'expert', split_axis=0, concat_axis=0, axis_index_g...  29.4 us
    all_to_all x3, starting transfers between devices, group_exchange(): lax.all_to_all(value, 'expert', split_axis=0, concat_axis=0, axis_index_g...  27.3 us
    pallas_call x22, Pallas kernels, local_call(): pl.pallas_call(kernel, out_shape=[jax.ShapeDtypeStruct(shape, jnp.bfloat1...  23.3 us
    all_to_all x1, blocking collectives, group_exchange(): lax.all_to_all(value, 'expert', split_axis=0, concat_axis=0, axis_index_g...  22.4 us
    ppermute x10, waiting for transfers between devices, section_shift(): lax.ppermute(value, 'section', [(s, (s + steps) % count) for s in range(c...  19.8 us
  transfers between devices with their start and end apart: 32, of which 24 were waited for; matrix products, arithmetic and copies ran while one was open for 1% of the time, Pallas kernels for 5%

profile of v3, /device:TPU:14, one launch (start us, length us, event | category | flops | bytes accessed | tf_op | source)
XLA Modules:
  0.0 303.4 jit_solution(2309656453097729496)
XLA Ops:
  4.5 15.2 %all-to-all-start = ((bf16[4,24,2048]{2,1,0:T(8,128)(2,1)}), bf16[4,24,2048]{2,1,0:T(8,128)(2,1)S(1)}, u32[]{:S(2)}, u32[]{:S(2)}) async-start(bf16[4,24,2048]{2,1,0:T(8,128)(2,1)} %bitcast.38), calls=%async_computation | async-start | bytes 786432 | tf_op jit(solution)/shard_map/all_to_all | solution.py:40
  21.7 2.4 collective-permute-start.6
  24.1 1.9 collective-permute-start.7
  28.1 3.4 %collective-permute-start = (f32[2,64,16]{2,1,0:T(8,128)}, f32[2,64,16]{2,1,0:T(8,128)}, u32[]{:S(2)}, u32[]{:S(2)}) collective-permute-start(f32[2,64,16]{2,1,0:T(8,128)} %bitcast.43), channel_id=1, source_target_pairs={{0,32},{32,64},{64,96},{96,128},{128,160},{160,192},{192,224},{224... | collective-permute-start | bytes 24584 | tf_op jit(solution)/shard_map/ppermute | solution.py:55
  32.2 2.4 collective-permute-start.1
  34.8 5.9 %collective-permute-done.1.refs_1_ = f32[2,64,16]{2,1,0:T(8,128)S(1)} collective-permute-done((f32[2,64,16]{2,1,0:T(8,128)}, f32[2,64,16]{2,1,0:T(8,128)S(1)}, u32[]{:S(2)}, u32[]{:S(2)}) %collective-permute-start.1) | collective-permute-done | bytes 8224 | tf_op jit(solution)/shard_map/ppermute | solution.py:55
  41.7 7.7 %collective-permute-start.8 = (bf16[24,4096]{1,0:T(8,128)(2,1)S(1)}, bf16[24,4096]{1,0:T(8,128)(2,1)S(1)}, u32[]{:S(2)}, u32[]{:S(2)}) collective-permute-start(bf16[24,4096]{1,0:T(8,128)(2,1)S(1)} %get-tuple-element.47.near_ref), channel_id=1, source_target_pairs={{0,4},{1,5},{2,6},{3,7},{4,0},{5,1},{6,2},{7,3},{8,12},{9,13},{10,... | collective-permute-start | bytes 589832 | tf_op jit(solution)/shard_map/ppermute | solution.py:46
  51.3 11.9 %collective-permute-done.8.far_ref = bf16[24,4096]{1,0:T(8,128)(2,1)S(1)} collective-permute-done((bf16[24,4096]{1,0:T(8,128)(2,1)S(1)}, bf16[24,4096]{1,0:T(8,128)(2,1)S(1)}, u32[]{:S(2)}, u32[]{:S(2)}) %collective-permute-start.8) | collective-permute-done | bytes 196640 | tf_op jit(solution)/shard_map/ppermute | solution.py:46
  63.2 1.9 collective-permute-start.9
  65.7 3.4 %collective-permute-start.11 = (bf16[48,4096]{1,0:T(8,128)(2,1)S(1)}, bf16[48,4096]{1,0:T(8,128)(2,1)S(1)}, u32[]{:S(2)}, u32[]{:S(2)}) collective-permute-start(bf16[48,4096]{1,0:T(8,128)(2,1)S(1)} %shard_map.69.refs_6_), channel_id=1, source_target_pairs={{0,2},{1,3},{2,0},{3,1},{4,6},{5,7},{6,4},{7,5},{8,10},{9,11},{10,... | collective-permute-start | bytes 1179656 | tf_op jit(solution)/shard_map/ppermute | solution.py:46
  69.2 8.0 %collective-permute-done.9.refs_7_ = bf16[48,4096]{1,0:T(8,128)(2,1)S(1)} collective-permute-done((bf16[48,4096]{1,0:T(8,128)(2,1)S(1)}, bf16[48,4096]{1,0:T(8,128)(2,1)S(1)}, u32[]{:S(2)}, u32[]{:S(2)}) %collective-permute-start.9) | collective-permute-done | bytes 393248 | tf_op jit(solution)/shard_map/ppermute | solution.py:46
  77.2 3.1 %shard_map.67 = (bf16[48,4096]{1,0:T(8,128)(2,1)S(1)}, bf16[48,4096]{1,0:T(8,128)(2,1)S(1)}) custom-call(bf16[4096,128]{1,0:T(8,128)(2,1)S(1)} %bitcast.20, bf16[4096,128]{1,0:T(8,128)(2,1)S(1)} %bitcast.25, bf16[128,4096]{1,0:T(8,128)(2,1)S(1)} %bitcast.30, bf16[4096,128]{1,0:T(8,128)(2,1)} %collective-permute-done.5.refs_3_, ...), custom_call_target="tpu_custom_call" | custom-call | tf_op jit(solution)/shard_map/pallas_call | solution.py:59
  82.2 3.4 %collective-permute-done.11.refs_7_ = bf16[48,4096]{1,0:T(8,128)(2,1)S(1)} collective-permute-done((bf16[48,4096]{1,0:T(8,128)(2,1)S(1)}, bf16[48,4096]{1,0:T(8,128)(2,1)S(1)}, u32[]{:S(2)}, u32[]{:S(2)}) %collective-permute-start.11) | collective-permute-done | bytes 393248 | tf_op jit(solution)/shard_map/ppermute | solution.py:46
  85.6 3.1 %shard_map.70 = (bf16[48,4096]{1,0:T(8,128)(2,1)S(1)}, bf16[48,4096]{1,0:T(8,128)(2,1)S(1)}) custom-call(bf16[4096,128]{1,0:T(8,128)(2,1)S(1)} %bitcast.21, bf16[4096,128]{1,0:T(8,128)(2,1)S(1)} %bitcast.26, bf16[128,4096]{1,0:T(8,128)(2,1)S(1)} %bitcast.31, bf16[4096,128]{1,0:T(8,128)(2,1)} %collective-permute-done.5.refs_3_, ...), custom_call_target="tpu_custom_call" | custom-call | tf_op jit(solution)/shard_map/pallas_call | solution.py:59
  90.6 5.5 %collective-permute-done.10.got_ref = bf16[48,4096]{1,0:T(8,128)(2,1)S(1)} collective-permute-done((bf16[48,4096]{1,0:T(8,128)(2,1)S(1)}, bf16[48,4096]{1,0:T(8,128)(2,1)S(1)}, u32[]{:S(2)}, u32[]{:S(2)}) %collective-permute-start.10) | collective-permute-done | bytes 393248 | tf_op jit(solution)/shard_map/ppermute | solution.py:46
  98.1 3.3 %collective-permute-done.12.got_ref = bf16[48,4096]{1,0:T(8,128)(2,1)S(1)} collective-permute-done((bf16[48,4096]{1,0:T(8,128)(2,1)S(1)}, bf16[48,4096]{1,0:T(8,128)(2,1)S(1)}, u32[]{:S(2)}, u32[]{:S(2)}) %collective-permute-start.12) | collective-permute-done | bytes 393248 | tf_op jit(solution)/shard_map/ppermute | solution.py:46
  101.5 1.9 collective-permute-start.14
  103.4 8.4 %collective-permute-done.13.refs_2_ = bf16[24,4096]{1,0:T(8,128)(2,1)S(1)} collective-permute-done((bf16[24,4096]{1,0:T(8,128)(2,1)S(1)}, bf16[24,4096]{1,0:T(8,128)(2,1)S(1)}, u32[]{:S(2)}, u32[]{:S(2)}) %collective-permute-start.13) | collective-permute-done | bytes 196640 | tf_op jit(solution)/shard_map/ppermute | solution.py:46
  111.8 2.2 collective-permute-done.14.refs_3_
  115.4 8.5 %all-to-all-start.1 = ((bf16[4,24,2048]{2,1,0:T(8,128)(2,1)}), bf16[4,24,2048]{2,1,0:T(8,128)(2,1)S(1)}, u32[]{:S(2)}, u32[]{:S(2)}) async-start(bf16[4,24,2048]{2,1,0:T(8,128)(2,1)} %bitcast.39), calls=%async_computation.1 | async-start | bytes 786432 | tf_op jit(solution)/shard_map/all_to_all | solution.py:40
  123.9 2.0 collective-permute-start.3
  125.8 3.9 %collective-permute-start.4 = (bf16[64,4096]{1,0:T(8,128)(2,1)}, bf16[64,4096]{1,0:T(8,128)(2,1)}, u32[]{:S(2)}, u32[]{:S(2)}) collective-permute-start(bf16[64,4096]{1,0:T(8,128)(2,1)} %copy-done.3), channel_id=1, source_target_pairs={{0,480},{32,0},{64,32},{96,64},{128,96},{160,128},{192,160},{224,1... | collective-permute-start | bytes 1572872 | tf_op jit(solution)/shard_map/ppermute | solution.py:55
  129.7 15.4 %all-to-all-done.1 = bf16[4,24,2048]{2,1,0:T(8,128)(2,1)S(1)} async-done(((bf16[4,24,2048]{2,1,0:T(8,128)(2,1)}), bf16[4,24,2048]{2,1,0:T(8,128)(2,1)S(1)}, u32[]{:S(2)}, u32[]{:S(2)}) %all-to-all-start.1) | async-done | bytes 393248 | tf_op jit(solution)/shard_map/all_to_all | solution.py:40
  146.0 2.1 collective-permute-start.15
  148.2 3.8 %collective-permute-start.16 = (bf16[48,2048]{1,0:T(8,128)(2,1)}, bf16[48,2048]{1,0:T(8,128)(2,1)}, u32[]{:S(2)}, u32[]{:S(2)}) collective-permute-start(bf16[48,2048]{1,0:T(8,128)(2,1)} %get-tuple-element.57), channel_id=1, source_target_pairs={{0,480},{32,0},{64,32},{96,64},{128,96},{160,128},{192,160},{224,1... | collective-permute-start | bytes 589832 | tf_op jit(solution)/shard_map/ppermute | solution.py:55
  153.9 4.2 %collective-permute-done.16.refs_5_ = bf16[48,2048]{1,0:T(8,128)(2,1)} collective-permute-done((bf16[48,2048]{1,0:T(8,128)(2,1)}, bf16[48,2048]{1,0:T(8,128)(2,1)}, u32[]{:S(2)}, u32[]{:S(2)}) %collective-permute-start.16) | collective-permute-done | bytes 196640 | tf_op jit(solution)/shard_map/ppermute | solution.py:55
  158.2 2.5 shard_map.74
  161.6 22.4 %all_to_all.46 = bf16[4,24,2048]{2,1,0:T(8,128)(2,1)S(1)} all-to-all(bf16[4,24,2048]{2,1,0:T(8,128)(2,1)S(1)} %bitcast.40), channel_id=1, replica_groups={{0,8,16,24},{1,9,17,25},{2,10,18,26},{3,11,19,27},{4,12,20,28},{5,13,21..., dimensions={0} | all-to-all | bytes 786432 | tf_op jit(solution)/shard_map/all_to_all | solution.py:40
  184.4 7.2 %collective-permute-start.20 = (bf16[24,4096]{1,0:T(8,128)(2,1)S(1)}, bf16[24,4096]{1,0:T(8,128)(2,1)S(1)}, u32[]{:S(2)}, u32[]{:S(2)}) collective-permute-start(bf16[24,4096]{1,0:T(8,128)(2,1)S(1)} %get-tuple-element.66.near_ref), channel_id=1, source_target_pairs={{0,4},{1,5},{2,6},{3,7},{4,0},{5,1},{6,2},{7,3},{8,12},{9,13},{10,... | collective-permute-start | bytes 589832 | tf_op jit(solution)/shard_map/ppermute | solution.py:46
  193.5 8.2 %collective-permute-done.20.far_ref = bf16[24,4096]{1,0:T(8,128)(2,1)S(1)} collective-permute-done((bf16[24,4096]{1,0:T(8,128)(2,1)S(1)}, bf16[24,4096]{1,0:T(8,128)(2,1)S(1)}, u32[]{:S(2)}, u32[]{:S(2)}) %collective-permute-start.20) | collective-permute-done | bytes 196640 | tf_op jit(solution)/shard_map/ppermute | solution.py:46
  204.3 3.3 %collective-permute-start.23 = (bf16[48,4096]{1,0:T(8,128)(2,1)S(1)}, bf16[48,4096]{1,0:T(8,128)(2,1)S(1)}, u32[]{:S(2)}, u32[]{:S(2)}) collective-permute-start(bf16[48,4096]{1,0:T(8,128)(2,1)S(1)} %shard_map.80.refs_6_), channel_id=1, source_target_pairs={{0,2},{1,3},{2,0},{3,1},{4,6},{5,7},{6,4},{7,5},{8,10},{9,11},{10,... | collective-permute-start | bytes 1179656 | tf_op jit(solution)/shard_map/ppermute | solution.py:46
  207.6 8.0 %collective-permute-done.21.refs_7_ = bf16[48,4096]{1,0:T(8,128)(2,1)S(1)} collective-permute-done((bf16[48,4096]{1,0:T(8,128)(2,1)S(1)}, bf16[48,4096]{1,0:T(8,128)(2,1)S(1)}, u32[]{:S(2)}, u32[]{:S(2)}) %collective-permute-start.21) | collective-permute-done | bytes 393248 | tf_op jit(solution)/shard_map/ppermute | solution.py:46
  215.6 3.1 %shard_map.78 = (bf16[48,4096]{1,0:T(8,128)(2,1)S(1)}, bf16[48,4096]{1,0:T(8,128)(2,1)S(1)}) custom-call(bf16[4096,128]{1,0:T(8,128)(2,1)S(1)} %bitcast.22, bf16[4096,128]{1,0:T(8,128)(2,1)S(1)} %bitcast.27, bf16[128,4096]{1,0:T(8,128)(2,1)S(1)} %bitcast.32, bf16[4096,128]{1,0:T(8,128)(2,1)} %collective-permute-done.5.refs_3_, ...), custom_call_target="tpu_custom_call" | custom-call | tf_op jit(solution)/shard_map/pallas_call | solution.py:59
  218.7 1.9 collective-permute-start.22
  220.7 3.4 %collective-permute-done.23.refs_7_ = bf16[48,4096]{1,0:T(8,128)(2,1)S(1)} collective-permute-done((bf16[48,4096]{1,0:T(8,128)(2,1)S(1)}, bf16[48,4096]{1,0:T(8,128)(2,1)S(1)}, u32[]{:S(2)}, u32[]{:S(2)}) %collective-permute-start.23) | collective-permute-done | bytes 393248 | tf_op jit(solution)/shard_map/ppermute | solution.py:46
  224.1 3.1 %shard_map.81 = (bf16[48,4096]{1,0:T(8,128)(2,1)S(1)}, bf16[48,4096]{1,0:T(8,128)(2,1)S(1)}) custom-call(bf16[4096,128]{1,0:T(8,128)(2,1)S(1)} %bitcast.23, bf16[4096,128]{1,0:T(8,128)(2,1)S(1)} %bitcast.28, bf16[128,4096]{1,0:T(8,128)(2,1)S(1)} %bitcast.33, bf16[4096,128]{1,0:T(8,128)(2,1)} %collective-permute-done.5.refs_3_, ...), custom_call_target="tpu_custom_call" | custom-call | tf_op jit(solution)/shard_map/pallas_call | solution.py:59
  227.2 1.9 collective-permute-start.24
  229.1 5.7 %collective-permute-done.22.got_ref = bf16[48,4096]{1,0:T(8,128)(2,1)S(1)} collective-permute-done((bf16[48,4096]{1,0:T(8,128)(2,1)S(1)}, bf16[48,4096]{1,0:T(8,128)(2,1)S(1)}, u32[]{:S(2)}, u32[]{:S(2)}) %collective-permute-start.22) | collective-permute-done | bytes 393248 | tf_op jit(solution)/shard_map/ppermute | solution.py:46
  236.8 3.2 %collective-permute-done.24.got_ref = bf16[48,4096]{1,0:T(8,128)(2,1)S(1)} collective-permute-done((bf16[48,4096]{1,0:T(8,128)(2,1)S(1)}, bf16[48,4096]{1,0:T(8,128)(2,1)S(1)}, u32[]{:S(2)}, u32[]{:S(2)}) %collective-permute-start.24) | collective-permute-done | bytes 393248 | tf_op jit(solution)/shard_map/ppermute | solution.py:46
  240.1 3.7 %collective-permute-start.26 = (bf16[24,4096]{1,0:T(8,128)(2,1)S(1)}, bf16[24,4096]{1,0:T(8,128)(2,1)S(1)}, u32[]{:S(2)}, u32[]{:S(2)}) collective-permute-start(bf16[24,4096]{1,0:T(8,128)(2,1)S(1)} %get-tuple-element.74), channel_id=1, source_target_pairs={{0,4},{1,5},{2,6},{3,7},{4,0},{5,1},{6,2},{7,3},{8,12},{9,13},{10,... | collective-permute-start | bytes 589832 | tf_op jit(solution)/shard_map/ppermute | solution.py:46
  243.8 6.6 %collective-permute-done.25.refs_2_ = bf16[24,4096]{1,0:T(8,128)(2,1)S(1)} collective-permute-done((bf16[24,4096]{1,0:T(8,128)(2,1)S(1)}, bf16[24,4096]{1,0:T(8,128)(2,1)S(1)}, u32[]{:S(2)}, u32[]{:S(2)}) %collective-permute-start.25) | collective-permute-done | bytes 196640 | tf_op jit(solution)/shard_map/ppermute | solution.py:46
  250.4 2.3 collective-permute-done.26.refs_3_
  254.1 3.6 %all-to-all-start.3 = ((bf16[4,24,2048]{2,1,0:T(8,128)(2,1)}), bf16[4,24,2048]{2,1,0:T(8,128)(2,1)S(1)}, u32[]{:S(2)}, u32[]{:S(2)}) async-start(bf16[4,24,2048]{2,1,0:T(8,128)(2,1)} %bitcast.15), calls=%async_computation.3 | async-start | bytes 786432 | tf_op jit(solution)/shard_map/all_to_all | solution.py:40
  257.7 7.8 %collective-permute-start.18 = (bf16[64,4096]{1,0:T(8,128)(2,1)S(1)}, bf16[64,4096]{1,0:T(8,128)(2,1)S(1)}, u32[]{:S(2)}, u32[]{:S(2)}) collective-permute-start(bf16[64,4096]{1,0:T(8,128)(2,1)S(1)} %copy-done.10), channel_id=1, source_target_pairs={{0,32},{32,64},{64,96},{96,128},{128,160},{160,192},{192,224},{224... | collective-permute-start | bytes 1572872 | tf_op jit(solution)/shard_map/ppermute | solution.py:55
  267.4 14.1 %all-to-all-done.3 = bf16[4,24,2048]{2,1,0:T(8,128)(2,1)S(1)} async-done(((bf16[4,24,2048]{2,1,0:T(8,128)(2,1)}), bf16[4,24,2048]{2,1,0:T(8,128)(2,1)S(1)}, u32[]{:S(2)}, u32[]{:S(2)}) %all-to-all-start.3) | async-done | bytes 393248 | tf_op jit(solution)/shard_map/all_to_all | solution.py:40
  281.8 9.0 %collective-permute-start.27 = (bf16[48,2048]{1,0:T(8,128)(2,1)S(1)}, bf16[48,2048]{1,0:T(8,128)(2,1)S(1)}, u32[]{:S(2)}, u32[]{:S(2)}) collective-permute-start(bf16[48,2048]{1,0:T(8,128)(2,1)S(1)} %get-tuple-element.75), channel_id=1, source_target_pairs={{0,32},{32,64},{64,96},{96,128},{128,160},{160,192},{192,224},{224... | collective-permute-start | bytes 589832 | tf_op jit(solution)/shard_map/ppermute | solution.py:55
  293.9 6.5 %collective-permute-done.28.refs_5_ = bf16[48,2048]{1,0:T(8,128)(2,1)S(1)} collective-permute-done((bf16[48,2048]{1,0:T(8,128)(2,1)S(1)}, bf16[48,2048]{1,0:T(8,128)(2,1)S(1)}, u32[]{:S(2)}, u32[]{:S(2)}) %collective-permute-start.28) | collective-permute-done | bytes 196640 | tf_op jit(solution)/shard_map/ppermute | solution.py:55
  300.4 3.0 shard_map.85
  (79 shorter events, 37.6 us)
Async XLA Ops:
  1.4 22.7 %copy-start.2 = (bf16[1,128,4096]{2,1,0:T(8,128)(2,1)S(1)}, bf16[1,128,4096]{2,1,0:T(8,128)(2,1)}, u32[]{:S(2)}) copy-start(bf16[1,128,4096]{2,1,0:T(8,128)(2,1)} %param.11) | copy-start | bytes 3145732
  2.8 0.8 copy-start.3
  2.8 1.0 copy-start.4
  2.8 16.9 %copy-start = (bf16[1,4096,128]{2,1,0:T(8,128)(2,1)S(1)}, bf16[1,4096,128]{2,1,0:T(8,128)(2,1)}, u32[]{:S(2)}) copy-start(bf16[1,4096,128]{2,1,0:T(8,128)(2,1)} %param.9) | copy-start | bytes 3145732
  2.8 18.8 %copy-start.1 = (bf16[1,4096,128]{2,1,0:T(8,128)(2,1)S(1)}, bf16[1,4096,128]{2,1,0:T(8,128)(2,1)}, u32[]{:S(2)}) copy-start(bf16[1,4096,128]{2,1,0:T(8,128)(2,1)} %param.10) | copy-start | bytes 3145732
  3.8 0.8 copy-start.5
  4.5 21.5 %copy-start.13 = (s32[2,2,64,8]{2,3,1,0:T(8,128)S(1)}, s32[2,2,64,8]{2,3,1,0:T(8,128)}, u32[]{:S(2)}) copy-start(s32[2,2,64,8]{2,3,1,0:T(8,128)} %param.7) | copy-start | bytes 24580
  4.5 36.8 %all-to-all-start = ((bf16[4,24,2048]{2,1,0:T(8,128)(2,1)}), bf16[4,24,2048]{2,1,0:T(8,128)(2,1)S(1)}, u32[]{:S(2)}, u32[]{:S(2)}) async-start(bf16[4,24,2048]{2,1,0:T(8,128)(2,1)} %bitcast.38), calls=%async_computation | async-start | bytes 786432 | tf_op jit(solution)/shard_map/all_to_all | solution.py:40
  19.7 49.4 %collective-permute-start.5 = (bf16[4096,128]{1,0:T(8,128)(2,1)S(1)}, bf16[4096,128]{1,0:T(8,128)(2,1)}, u32[]{:S(2)}, u32[]{:S(2)}) collective-permute-start(bf16[4096,128]{1,0:T(8,128)(2,1)S(1)} %bitcast.19), channel_id=1, source_target_pairs={{0,1},{1,0},{2,3},{3,2},{4,5},{5,4},{6,7},{7,6},{8,9},{9,8},{10,11... | collective-permute-start | bytes 3145736 | tf_op jit(solution)/shard_map/ppermute | solution.py:50
  21.7 47.5 %collective-permute-start.6 = (bf16[4096,128]{1,0:T(8,128)(2,1)S(1)}, bf16[4096,128]{1,0:T(8,128)(2,1)}, u32[]{:S(2)}, u32[]{:S(2)}) collective-permute-start(bf16[4096,128]{1,0:T(8,128)(2,1)S(1)} %bitcast.24), channel_id=1, source_target_pairs={{0,1},{1,0},{2,3},{3,2},{4,5},{5,4},{6,7},{7,6},{8,9},{9,8},{10,11... | collective-permute-start | bytes 3145736 | tf_op jit(solution)/shard_map/ppermute | solution.py:50
  24.1 2.0 copy-start.15
  24.1 45.0 %collective-permute-start.7 = (bf16[128,4096]{1,0:T(8,128)(2,1)S(1)}, bf16[128,4096]{1,0:T(8,128)(2,1)}, u32[]{:S(2)}, u32[]{:S(2)}) collective-permute-start(bf16[128,4096]{1,0:T(8,128)(2,1)S(1)} %bitcast.29), channel_id=1, source_target_pairs={{0,1},{1,0},{2,3},{3,2},{4,5},{5,4},{6,7},{7,6},{8,9},{9,8},{10,11... | collective-permute-start | bytes 3145736 | tf_op jit(solution)/shard_map/ppermute | solution.py:50
  28.1 6.7 %collective-permute-start = (f32[2,64,16]{2,1,0:T(8,128)}, f32[2,64,16]{2,1,0:T(8,128)}, u32[]{:S(2)}, u32[]{:S(2)}) collective-permute-start(f32[2,64,16]{2,1,0:T(8,128)} %bitcast.43), channel_id=1, source_target_pairs={{0,32},{32,64},{64,96},{96,128},{128,160},{160,192},{192,224},{224... | collective-permute-start | bytes 24584 | tf_op jit(solution)/shard_map/ppermute | solution.py:55
  32.2 8.5 %collective-permute-start.1 = (f32[2,64,16]{2,1,0:T(8,128)}, f32[2,64,16]{2,1,0:T(8,128)S(1)}, u32[]{:S(2)}, u32[]{:S(2)}) collective-permute-start(f32[2,64,16]{2,1,0:T(8,128)} %bitcast.44), channel_id=1, source_target_pairs={{0,480},{32,0},{64,32},{96,64},{128,96},{160,128},{192,160},{224,1... | collective-permute-start | bytes 24584 | tf_op jit(solution)/shard_map/ppermute | solution.py:55
  40.7 0.6 copy-start.11
  41.7 21.5 %collective-permute-start.8 = (bf16[24,4096]{1,0:T(8,128)(2,1)S(1)}, bf16[24,4096]{1,0:T(8,128)(2,1)S(1)}, u32[]{:S(2)}, u32[]{:S(2)}) collective-permute-start(bf16[24,4096]{1,0:T(8,128)(2,1)S(1)} %get-tuple-element.47.near_ref), channel_id=1, source_target_pairs={{0,4},{1,5},{2,6},{3,7},{4,0},{5,1},{6,2},{7,3},{8,12},{9,13},{10,... | collective-permute-start | bytes 589832 | tf_op jit(solution)/shard_map/ppermute | solution.py:46
  49.4 16.3 %collective-permute-start.2 = (bf16[24,4096]{1,0:T(8,128)(2,1)S(1)}, bf16[24,4096]{1,0:T(8,128)(2,1)S(1)}, u32[]{:S(2)}, u32[]{:S(2)}) collective-permute-start(bf16[24,4096]{1,0:T(8,128)(2,1)S(1)} %get-tuple-element.44.near_ref), channel_id=1, source_target_pairs={{0,4},{1,5},{2,6},{3,7},{4,0},{5,1},{6,2},{7,3},{8,12},{9,13},{10,... | collective-permute-start | bytes 589832 | tf_op jit(solution)/shard_map/ppermute | solution.py:46
  63.2 13.9 %collective-permute-start.9 = (bf16[48,4096]{1,0:T(8,128)(2,1)S(1)}, bf16[48,4096]{1,0:T(8,128)(2,1)S(1)}, u32[]{:S(2)}, u32[]{:S(2)}) collective-permute-start(bf16[48,4096]{1,0:T(8,128)(2,1)S(1)} %shard_map.66.refs_6_), channel_id=1, source_target_pairs={{0,2},{1,3},{2,0},{3,1},{4,6},{5,7},{6,4},{7,5},{8,10},{9,11},{10,... | collective-permute-start | bytes 1179656 | tf_op jit(solution)/shard_map/ppermute | solution.py:46
  65.7 19.9 %collective-permute-start.11 = (bf16[48,4096]{1,0:T(8,128)(2,1)S(1)}, bf16[48,4096]{1,0:T(8,128)(2,1)S(1)}, u32[]{:S(2)}, u32[]{:S(2)}) collective-permute-start(bf16[48,4096]{1,0:T(8,128)(2,1)S(1)} %shard_map.69.refs_6_), channel_id=1, source_target_pairs={{0,2},{1,3},{2,0},{3,1},{4,6},{5,7},{6,4},{7,5},{8,10},{9,11},{10,... | collective-permute-start | bytes 1179656 | tf_op jit(solution)/shard_map/ppermute | solution.py:46
  80.3 15.8 %collective-permute-start.10 = (bf16[48,4096]{1,0:T(8,128)(2,1)S(1)}, bf16[48,4096]{1,0:T(8,128)(2,1)S(1)}, u32[]{:S(2)}, u32[]{:S(2)}) collective-permute-start(bf16[48,4096]{1,0:T(8,128)(2,1)S(1)} %get-tuple-element.49), channel_id=1, source_target_pairs={{0,2},{1,3},{2,0},{3,1},{4,6},{5,7},{6,4},{7,5},{8,10},{9,11},{10,... | collective-permute-start | bytes 1179656 | tf_op jit(solution)/shard_map/ppermute | solution.py:46
  88.7 12.7 %collective-permute-start.12 = (bf16[48,4096]{1,0:T(8,128)(2,1)S(1)}, bf16[48,4096]{1,0:T(8,128)(2,1)S(1)}, u32[]{:S(2)}, u32[]{:S(2)}) collective-permute-start(bf16[48,4096]{1,0:T(8,128)(2,1)S(1)} %get-tuple-element.52), channel_id=1, source_target_pairs={{0,2},{1,3},{2,0},{3,1},{4,6},{5,7},{6,4},{7,5},{8,10},{9,11},{10,... | collective-permute-start | bytes 1179656 | tf_op jit(solution)/shard_map/ppermute | solution.py:46
  96.2 15.6 %collective-permute-start.13 = (bf16[24,4096]{1,0:T(8,128)(2,1)S(1)}, bf16[24,4096]{1,0:T(8,128)(2,1)S(1)}, u32[]{:S(2)}, u32[]{:S(2)}) collective-permute-start(bf16[24,4096]{1,0:T(8,128)(2,1)S(1)} %get-tuple-element.54), channel_id=1, source_target_pairs={{0,4},{1,5},{2,6},{3,7},{4,0},{5,1},{6,2},{7,3},{8,12},{9,13},{10,... | collective-permute-start | bytes 589832 | tf_op jit(solution)/shard_map/ppermute | solution.py:46
  101.5 12.5 %collective-permute-start.14 = (bf16[24,4096]{1,0:T(8,128)(2,1)S(1)}, bf16[24,4096]{1,0:T(8,128)(2,1)S(1)}, u32[]{:S(2)}, u32[]{:S(2)}) collective-permute-start(bf16[24,4096]{1,0:T(8,128)(2,1)S(1)} %get-tuple-element.55), channel_id=1, source_target_pairs={{0,4},{1,5},{2,6},{3,7},{4,0},{5,1},{6,2},{7,3},{8,12},{9,13},{10,... | collective-permute-start | bytes 589832 | tf_op jit(solution)/shard_map/ppermute | solution.py:46
  114.6 0.8 copy-start.6
  115.4 29.7 %all-to-all-start.1 = ((bf16[4,24,2048]{2,1,0:T(8,128)(2,1)}), bf16[4,24,2048]{2,1,0:T(8,128)(2,1)S(1)}, u32[]{:S(2)}, u32[]{:S(2)}) async-start(bf16[4,24,2048]{2,1,0:T(8,128)(2,1)} %bitcast.39), calls=%async_computation.1 | async-start | bytes 786432 | tf_op jit(solution)/shard_map/all_to_all | solution.py:40
  123.9 28.3 %collective-permute-start.3 = (bf16[64,4096]{1,0:T(8,128)(2,1)}, bf16[64,4096]{1,0:T(8,128)(2,1)}, u32[]{:S(2)}, u32[]{:S(2)}) collective-permute-start(bf16[64,4096]{1,0:T(8,128)(2,1)} %copy-done.4), channel_id=1, source_target_pairs={{0,32},{32,64},{64,96},{96,128},{128,160},{160,192},{192,224},{224... | collective-permute-start | bytes 1572872 | tf_op jit(solution)/shard_map/ppermute | solution.py:55
  125.8 26.3 %collective-permute-start.4 = (bf16[64,4096]{1,0:T(8,128)(2,1)}, bf16[64,4096]{1,0:T(8,128)(2,1)}, u32[]{:S(2)}, u32[]{:S(2)}) collective-permute-start(bf16[64,4096]{1,0:T(8,128)(2,1)} %copy-done.3), channel_id=1, source_target_pairs={{0,480},{32,0},{64,32},{96,64},{128,96},{160,128},{192,160},{224,1... | collective-permute-start | bytes 1572872 | tf_op jit(solution)/shard_map/ppermute | solution.py:55
  145.1 6.9 %copy-start.14 = (s32[1,2,64,8]{2,3,1,0:T(8,128)S(1)}, s32[1,2,64,8]{2,3,1,0:T(8,128)}, u32[]{:S(2)}) copy-start(s32[1,2,64,8]{2,3,1,0:T(8,128)} %get-tuple-element.82) | copy-start | bytes 12292
  146.0 12.1 %copy-start.12 = (f32[2,64,16]{2,1,0:T(8,128)S(1)}, f32[2,64,16]{2,1,0:T(8,128)}, u32[]{:S(2)}) copy-start(f32[2,64,16]{2,1,0:T(8,128)} %copy-done.11) | copy-start | bytes 24580
  146.0 7.9 %collective-permute-start.15 = (bf16[48,2048]{1,0:T(8,128)(2,1)}, bf16[48,2048]{1,0:T(8,128)(2,1)S(1)}, u32[]{:S(2)}, u32[]{:S(2)}) collective-permute-start(bf16[48,2048]{1,0:T(8,128)(2,1)} %get-tuple-element.56), channel_id=1, source_target_pairs={{0,32},{32,64},{64,96},{96,128},{128,160},{160,192},{192,224},{224... | collective-permute-start | bytes 589832 | tf_op jit(solution)/shard_map/ppermute | solution.py:55
  148.2 10.0 %collective-permute-start.16 = (bf16[48,2048]{1,0:T(8,128)(2,1)}, bf16[48,2048]{1,0:T(8,128)(2,1)}, u32[]{:S(2)}, u32[]{:S(2)}) collective-permute-start(bf16[48,2048]{1,0:T(8,128)(2,1)} %get-tuple-element.57), channel_id=1, source_target_pairs={{0,480},{32,0},{64,32},{96,64},{128,96},{160,128},{192,160},{224,1... | collective-permute-start | bytes 589832 | tf_op jit(solution)/shard_map/ppermute | solution.py:55
  160.6 0.8 copy-start.7
  160.6 1.0 copy-start.9
  184.4 17.3 %collective-permute-start.20 = (bf16[24,4096]{1,0:T(8,128)(2,1)S(1)}, bf16[24,4096]{1,0:T(8,128)(2,1)S(1)}, u32[]{:S(2)}, u32[]{:S(2)}) collective-permute-start(bf16[24,4096]{1,0:T(8,128)(2,1)S(1)} %get-tuple-element.66.near_ref), channel_id=1, source_target_pairs={{0,4},{1,5},{2,6},{3,7},{4,0},{5,1},{6,2},{7,3},{8,12},{9,13},{10,... | collective-permute-start | bytes 589832 | tf_op jit(solution)/shard_map/ppermute | solution.py:46
  191.5 12.8 %collective-permute-start.17 = (bf16[24,4096]{1,0:T(8,128)(2,1)S(1)}, bf16[24,4096]{1,0:T(8,128)(2,1)S(1)}, u32[]{:S(2)}, u32[]{:S(2)}) collective-permute-start(bf16[24,4096]{1,0:T(8,128)(2,1)S(1)} %get-tuple-element.63.near_ref), channel_id=1, source_target_pairs={{0,4},{1,5},{2,6},{3,7},{4,0},{5,1},{6,2},{7,3},{8,12},{9,13},{10,... | collective-permute-start | bytes 589832 | tf_op jit(solution)/shard_map/ppermute | solution.py:46
  201.7 13.9 %collective-permute-start.21 = (bf16[48,4096]{1,0:T(8,128)(2,1)S(1)}, bf16[48,4096]{1,0:T(8,128)(2,1)S(1)}, u32[]{:S(2)}, u32[]{:S(2)}) collective-permute-start(bf16[48,4096]{1,0:T(8,128)(2,1)S(1)} %shard_map.77.refs_6_), channel_id=1, source_target_pairs={{0,2},{1,3},{2,0},{3,1},{4,6},{5,7},{6,4},{7,5},{8,10},{9,11},{10,... | collective-permute-start | bytes 1179656 | tf_op jit(solution)/shard_map/ppermute | solution.py:46
  204.3 19.7 %collective-permute-start.23 = (bf16[48,4096]{1,0:T(8,128)(2,1)S(1)}, bf16[48,4096]{1,0:T(8,128)(2,1)S(1)}, u32[]{:S(2)}, u32[]{:S(2)}) collective-permute-start(bf16[48,4096]{1,0:T(8,128)(2,1)S(1)} %shard_map.80.refs_6_), channel_id=1, source_target_pairs={{0,2},{1,3},{2,0},{3,1},{4,6},{5,7},{6,4},{7,5},{8,10},{9,11},{10,... | collective-permute-start | bytes 1179656 | tf_op jit(solution)/shard_map/ppermute | solution.py:46
  218.7 16.1 %collective-permute-start.22 = (bf16[48,4096]{1,0:T(8,128)(2,1)S(1)}, bf16[48,4096]{1,0:T(8,128)(2,1)S(1)}, u32[]{:S(2)}, u32[]{:S(2)}) collective-permute-start(bf16[48,4096]{1,0:T(8,128)(2,1)S(1)} %get-tuple-element.68), channel_id=1, source_target_pairs={{0,2},{1,3},{2,0},{3,1},{4,6},{5,7},{6,4},{7,5},{8,10},{9,11},{10,... | collective-permute-start | bytes 1179656 | tf_op jit(solution)/shard_map/ppermute | solution.py:46
  227.2 12.9 %collective-permute-start.24 = (bf16[48,4096]{1,0:T(8,128)(2,1)S(1)}, bf16[48,4096]{1,0:T(8,128)(2,1)S(1)}, u32[]{:S(2)}, u32[]{:S(2)}) collective-permute-start(bf16[48,4096]{1,0:T(8,128)(2,1)S(1)} %get-tuple-element.71), channel_id=1, source_target_pairs={{0,2},{1,3},{2,0},{3,1},{4,6},{5,7},{6,4},{7,5},{8,10},{9,11},{10,... | collective-permute-start | bytes 1179656 | tf_op jit(solution)/shard_map/ppermute | solution.py:46
  234.9 15.5 %collective-permute-start.25 = (bf16[24,4096]{1,0:T(8,128)(2,1)S(1)}, bf16[24,4096]{1,0:T(8,128)(2,1)S(1)}, u32[]{:S(2)}, u32[]{:S(2)}) collective-permute-start(bf16[24,4096]{1,0:T(8,128)(2,1)S(1)} %get-tuple-element.73), channel_id=1, source_target_pairs={{0,4},{1,5},{2,6},{3,7},{4,0},{5,1},{6,2},{7,3},{8,12},{9,13},{10,... | collective-permute-start | bytes 589832 | tf_op jit(solution)/shard_map/ppermute | solution.py:46
  240.1 12.6 %collective-permute-start.26 = (bf16[24,4096]{1,0:T(8,128)(2,1)S(1)}, bf16[24,4096]{1,0:T(8,128)(2,1)S(1)}, u32[]{:S(2)}, u32[]{:S(2)}) collective-permute-start(bf16[24,4096]{1,0:T(8,128)(2,1)S(1)} %get-tuple-element.74), channel_id=1, source_target_pairs={{0,4},{1,5},{2,6},{3,7},{4,0},{5,1},{6,2},{7,3},{8,12},{9,13},{10,... | collective-permute-start | bytes 589832 | tf_op jit(solution)/shard_map/ppermute | solution.py:46
  252.7 5.0 %copy-start.10 = (bf16[64,4096]{1,0:T(8,128)(2,1)S(1)}, bf16[64,4096]{1,0:T(8,128)(2,1)}, u32[]{:S(2)}) copy-start(bf16[64,4096]{1,0:T(8,128)(2,1)} %copy-done.9) | copy-start | bytes 1572868
  254.1 11.4 %copy-start.8 = (bf16[64,4096]{1,0:T(8,128)(2,1)S(1)}, bf16[64,4096]{1,0:T(8,128)(2,1)}, u32[]{:S(2)}) copy-start(bf16[64,4096]{1,0:T(8,128)(2,1)} %copy-done.7) | copy-start | bytes 1572868
  254.1 27.4 %all-to-all-start.3 = ((bf16[4,24,2048]{2,1,0:T(8,128)(2,1)}), bf16[4,24,2048]{2,1,0:T(8,128)(2,1)S(1)}, u32[]{:S(2)}, u32[]{:S(2)}) async-start(bf16[4,24,2048]{2,1,0:T(8,128)(2,1)} %bitcast.15), calls=%async_computation.3 | async-start | bytes 786432 | tf_op jit(solution)/shard_map/all_to_all | solution.py:40
  257.7 35.0 %collective-permute-start.18 = (bf16[64,4096]{1,0:T(8,128)(2,1)S(1)}, bf16[64,4096]{1,0:T(8,128)(2,1)S(1)}, u32[]{:S(2)}, u32[]{:S(2)}) collective-permute-start(bf16[64,4096]{1,0:T(8,128)(2,1)S(1)} %copy-done.10), channel_id=1, source_target_pairs={{0,32},{32,64},{64,96},{96,128},{128,160},{160,192},{192,224},{224... | collective-permute-start | bytes 1572872 | tf_op jit(solution)/shard_map/ppermute | solution.py:55
  265.5 27.2 %collective-permute-start.19 = (bf16[64,4096]{1,0:T(8,128)(2,1)S(1)}, bf16[64,4096]{1,0:T(8,128)(2,1)S(1)}, u32[]{:S(2)}, u32[]{:S(2)}) collective-permute-start(bf16[64,4096]{1,0:T(8,128)(2,1)S(1)} %copy-done.8), channel_id=1, source_target_pairs={{0,480},{32,0},{64,32},{96,64},{128,96},{160,128},{192,160},{224,1... | collective-permute-start | bytes 1572872 | tf_op jit(solution)/shard_map/ppermute | solution.py:55
  281.8 12.2 %collective-permute-start.27 = (bf16[48,2048]{1,0:T(8,128)(2,1)S(1)}, bf16[48,2048]{1,0:T(8,128)(2,1)S(1)}, u32[]{:S(2)}, u32[]{:S(2)}) collective-permute-start(bf16[48,2048]{1,0:T(8,128)(2,1)S(1)} %get-tuple-element.75), channel_id=1, source_target_pairs={{0,32},{32,64},{64,96},{96,128},{128,160},{160,192},{192,224},{224... | collective-permute-start | bytes 589832 | tf_op jit(solution)/shard_map/ppermute | solution.py:55
  290.8 9.7 %collective-permute-start.28 = (bf16[48,2048]{1,0:T(8,128)(2,1)S(1)}, bf16[48,2048]{1,0:T(8,128)(2,1)S(1)}, u32[]{:S(2)}, u32[]{:S(2)}) collective-permute-start(bf16[48,2048]{1,0:T(8,128)(2,1)S(1)} %get-tuple-element.76), channel_id=1, source_target_pairs={{0,480},{32,0},{64,32},{96,64},{128,96},{160,128},{192,160},{224,1... | collective-permute-start | bytes 589832 | tf_op jit(solution)/shard_map/ppermute | solution.py:55

commit v4 on v3

--- a/solution.py
+++ b/solution.py
@@ -12,6 +12,7 @@
 CHIPS = 4
 CORES = 2
 PIECES = 2
+SWAPS = ((2, 1), (1, 2))
 DIRS = 2
 FOLD = 2
 EACH = DIRS * MOST
@@ -139,20 +140,23 @@
     far_ref[...] = total[rows:].astype(jnp.bfloat16)
 
 
-def expert_kernel(*refs):
-    pieces = refs[: 3 * PIECES]
-    near_ref, far_ref, done_near_ref, done_far_ref = refs[3 * PIECES :]
-    rows = jnp.concatenate([near_ref[...], far_ref[...]], axis=0)
-    result = jnp.zeros(rows.shape, jnp.float32)
-    for p in range(0, PIECES, 2):
-        gates, ups, downs = ([ref[...] for ref in pieces[3 * p + n : 3 * p + 6 : 3]] for n in range(3))
+def expert_kernel(crossed):
+    def kernel(*refs):
+        pieces = refs[: 3 * PIECES]
+        near_ref, far_ref, done_ref, passed_ref = refs[3 * PIECES :]
+        rows = jnp.concatenate([near_ref[...], far_ref[...]], axis=0)
+        gates, ups, downs = ([ref[...] for ref in pieces[n::3]] for n in range(3))
         both = dot(rows, jnp.concatenate(gates + ups, axis=1))
         half = both.shape[1] // 2
         hidden = (jax.nn.silu(both[:, :half]) * both[:, half:]).astype(jnp.bfloat16)
-        result = result + dot(hidden, jnp.concatenate(downs, axis=0))
-    count = near_ref.shape[0]
-    done_near_ref[...] = result[:count].astype(jnp.bfloat16)
-    done_far_ref[...] = result[count:].astype(jnp.bfloat16)
+        result = dot(hidden, jnp.concatenate(downs, axis=0))
+        parts = [result[n * LISTED : (n + 1) * LISTED] for n in range(CHIPS)]
+        if crossed:
+            parts = [parts[n] for n in (0, 2, 1, 3)]
+        done_ref[...] = jnp.concatenate(parts[:2], axis=0).astype(jnp.bfloat16)
+        passed_ref[...] = jnp.concatenate(parts[2:], axis=0).astype(jnp.bfloat16)
+
+    return kernel
 
 
 def fold_kernel(*refs):
@@ -227,15 +231,15 @@
     (sent,) = local_call(list_kernel, [(GROUPS * PART, width)], ids, *states)
     held, early = lax.optimization_barrier((group_exchange(sent), early))
     near = local_call(unfold_kernel, [(LISTED, model)] * DIRS, held)
-    far = [chip_swap(near[d], 2) for d in range(DIRS)]
+    far = [chip_swap(near[d], SWAPS[d][0]) for d in range(DIRS)]
     _, states = lax.optimization_barrier((far[1], states))
     moved = both_ways(states)
     owns, gots = [], []
     for d in range(DIRS):
         (pair,) = local_call(pair_kernel, [(2 * LISTED, model)], near[d], far[d])
-        other = chip_swap(pair, 1)
+        other = chip_swap(pair, SWAPS[d][1])
         done, sent_back = local_call(
-            expert_kernel, [(2 * LISTED, model)] * 2, *weights, pair, other, vmem=32
+            expert_kernel(SWAPS[d][1] == 2), [(2 * LISTED, model)] * 2, *weights, pair, other, vmem=32
         )
         got = chip_swap(sent_back, 1)
         own, passed = local_call(add_kernel, [(LISTED, model)] * 2, done, got)

time: 305 us -> 303 us (level)
  the two profiles are of different devices: /device:TPU:14 before, /device:TPU:94 now
where the time goes in v4:
time: 303 us; the launch traced here: 302 us
  starting transfers between devices  141 us (47%)
  waiting for transfers between devices  104 us (34%)
  blocking collectives  23.7 us (8%)
  Pallas kernels  23.3 us (8%)
  local copies, waits for them, and re-layouts  7.88 us (3%)
    ppermute x16, starting transfers between devices, chip_swap(): lax.ppermute(value, 'expert', pairs_of(lambda g, m, c: (g, m ^ k, c)))  61.2 us
    ppermute x16, waiting for transfers between devices, chip_swap(): lax.ppermute(value, 'expert', pairs_of(lambda g, m, c: (g, m ^ k, c)))  43 us
    all_to_all x3, waiting for transfers between devices, group_exchange(): lax.all_to_all(value, 'expert', split_axis=0, concat_axis=0, axis_index_g...  39.2 us
    all_to_all x3, starting transfers between devices, group_exchange(): lax.all_to_all(value, 'expert', split_axis=0, concat_axis=0, axis_index_g...  37.4 us
    ppermute x10, starting transfers between devices, section_shift(): lax.ppermute(value, 'section', [(s, (s + steps) % count) for s in range(c...  36.6 us
    all_to_all x1, blocking collectives, group_exchange(): lax.all_to_all(value, 'expert', split_axis=0, concat_axis=0, axis_index_g...  23.7 us
    pallas_call x22, Pallas kernels, local_call(): pl.pallas_call(kernel, out_shape=[jax.ShapeDtypeStruct(shape, jnp.bfloat1...  23.3 us
    ppermute x10, waiting for transfers between devices, section_shift(): lax.ppermute(value, 'section', [(s, (s + steps) % count) for s in range(c...  22.1 us
  transfers between devices with their start and end apart: 32, of which 21 were waited for; matrix products, arithmetic and copies ran while one was open for 1% of the time, Pallas kernels for 5%

profile of v4, /device:TPU:94, one launch (start us, length us, event | category | flops | bytes accessed | tf_op | source)
XLA Modules:
  0.0 301.9 jit_solution(15760775071145947268)
XLA Ops:
  4.5 13.4 %all-to-all-start = ((bf16[4,24,2048]{2,1,0:T(8,128)(2,1)}), bf16[4,24,2048]{2,1,0:T(8,128)(2,1)S(1)}, u32[]{:S(2)}, u32[]{:S(2)}) async-start(bf16[4,24,2048]{2,1,0:T(8,128)(2,1)} %bitcast.38), calls=%async_computation | async-start | bytes 786432 | tf_op jit(solution)/shard_map/all_to_all | solution.py:41
  19.9 2.4 collective-permute-start.6
  22.3 1.9 collective-permute-start.7
  26.3 2.0 collective-permute-start
  29.1 3.8 %collective-permute-start.1 = (f32[2,64,16]{2,1,0:T(8,128)}, f32[2,64,16]{2,1,0:T(8,128)S(1)}, u32[]{:S(2)}, u32[]{:S(2)}) collective-permute-start(f32[2,64,16]{2,1,0:T(8,128)} %bitcast.44), channel_id=1, source_target_pairs={{0,480},{32,0},{64,32},{96,64},{128,96},{160,128},{192,160},{224,1... | collective-permute-start | bytes 24584 | tf_op jit(solution)/shard_map/ppermute | solution.py:56
  33.0 5.8 %collective-permute-done.1.refs_1_ = f32[2,64,16]{2,1,0:T(8,128)S(1)} collective-permute-done((f32[2,64,16]{2,1,0:T(8,128)}, f32[2,64,16]{2,1,0:T(8,128)S(1)}, u32[]{:S(2)}, u32[]{:S(2)}) %collective-permute-start.1) | collective-permute-done | bytes 8224 | tf_op jit(solution)/shard_map/ppermute | solution.py:56
  39.5 4.4 %all-to-all-done = bf16[4,24,2048]{2,1,0:T(8,128)(2,1)S(1)} async-done(((bf16[4,24,2048]{2,1,0:T(8,128)(2,1)}), bf16[4,24,2048]{2,1,0:T(8,128)(2,1)S(1)}, u32[]{:S(2)}, u32[]{:S(2)}) %all-to-all-start) | async-done | bytes 393248 | tf_op jit(solution)/shard_map/all_to_all | solution.py:41
  44.2 1.9 collective-permute-start.8
  46.1 4.4 %collective-permute-start.2 = (bf16[24,4096]{1,0:T(8,128)(2,1)S(1)}, bf16[24,4096]{1,0:T(8,128)(2,1)S(1)}, u32[]{:S(2)}, u32[]{:S(2)}) collective-permute-start(bf16[24,4096]{1,0:T(8,128)(2,1)S(1)} %get-tuple-element.44.near_ref), channel_id=1, source_target_pairs={{0,2},{1,3},{2,0},{3,1},{4,6},{5,7},{6,4},{7,5},{8,10},{9,11},{10,... | collective-permute-start | bytes 589832 | tf_op jit(solution)/shard_map/ppermute | solution.py:47
  50.5 4.0 %collective-permute-done.8.far_ref = bf16[24,4096]{1,0:T(8,128)(2,1)S(1)} collective-permute-done((bf16[24,4096]{1,0:T(8,128)(2,1)S(1)}, bf16[24,4096]{1,0:T(8,128)(2,1)S(1)}, u32[]{:S(2)}, u32[]{:S(2)}) %collective-permute-start.8) | collective-permute-done | bytes 196640 | tf_op jit(solution)/shard_map/ppermute | solution.py:47
  54.5 3.9 %collective-permute-start.9 = (bf16[48,4096]{1,0:T(8,128)(2,1)S(1)}, bf16[48,4096]{1,0:T(8,128)(2,1)S(1)}, u32[]{:S(2)}, u32[]{:S(2)}) collective-permute-start(bf16[48,4096]{1,0:T(8,128)(2,1)S(1)} %shard_map.66.refs_6_), channel_id=1, source_target_pairs={{0,2},{1,3},{2,0},{3,1},{4,6},{5,7},{6,4},{7,5},{8,10},{9,11},{10,... | collective-permute-start | bytes 1179656 | tf_op jit(solution)/shard_map/ppermute | solution.py:47
  58.4 2.4 collective-permute-start.11
  60.9 7.6 %collective-permute-done.9.refs_7_ = bf16[48,4096]{1,0:T(8,128)(2,1)S(1)} collective-permute-done((bf16[48,4096]{1,0:T(8,128)(2,1)S(1)}, bf16[48,4096]{1,0:T(8,128)(2,1)S(1)}, u32[]{:S(2)}, u32[]{:S(2)}) %collective-permute-start.9) | collective-permute-done | bytes 393248 | tf_op jit(solution)/shard_map/ppermute | solution.py:47
  68.5 3.1 %shard_map.67 = (bf16[48,4096]{1,0:T(8,128)(2,1)S(1)}, bf16[48,4096]{1,0:T(8,128)(2,1)S(1)}) custom-call(bf16[4096,128]{1,0:T(8,128)(2,1)S(1)} %bitcast.20, bf16[4096,128]{1,0:T(8,128)(2,1)S(1)} %bitcast.25, bf16[128,4096]{1,0:T(8,128)(2,1)S(1)} %bitcast.30, bf16[4096,128]{1,0:T(8,128)(2,1)} %collective-permute-done.5.refs_3_, ...), custom_call_target="tpu_custom_call" | custom-call | tf_op jit(solution)/shard_map/pallas_call | solution.py:60
  71.6 4.4 %collective-permute-start.10 = (bf16[48,4096]{1,0:T(8,128)(2,1)S(1)}, bf16[48,4096]{1,0:T(8,128)(2,1)S(1)}, u32[]{:S(2)}, u32[]{:S(2)}) collective-permute-start(bf16[48,4096]{1,0:T(8,128)(2,1)S(1)} %get-tuple-element.49), channel_id=1, source_target_pairs={{0,2},{1,3},{2,0},{3,1},{4,6},{5,7},{6,4},{7,5},{8,10},{9,11},{10,... | collective-permute-start | bytes 1179656 | tf_op jit(solution)/shard_map/ppermute | solution.py:47
  77.0 3.1 %shard_map.70 = (bf16[48,4096]{1,0:T(8,128)(2,1)S(1)}, bf16[48,4096]{1,0:T(8,128)(2,1)S(1)}) custom-call(bf16[4096,128]{1,0:T(8,128)(2,1)S(1)} %bitcast.21, bf16[4096,128]{1,0:T(8,128)(2,1)S(1)} %bitcast.26, bf16[128,4096]{1,0:T(8,128)(2,1)S(1)} %bitcast.31, bf16[4096,128]{1,0:T(8,128)(2,1)} %collective-permute-done.5.refs_3_, ...), custom_call_target="tpu_custom_call" | custom-call | tf_op jit(solution)/shard_map/pallas_call | solution.py:60
  80.1 4.0 %collective-permute-start.12 = (bf16[48,4096]{1,0:T(8,128)(2,1)S(1)}, bf16[48,4096]{1,0:T(8,128)(2,1)S(1)}, u32[]{:S(2)}, u32[]{:S(2)}) collective-permute-start(bf16[48,4096]{1,0:T(8,128)(2,1)S(1)} %get-tuple-element.52), channel_id=1, source_target_pairs={{0,2},{1,3},{2,0},{3,1},{4,6},{5,7},{6,4},{7,5},{8,10},{9,11},{10,... | collective-permute-start | bytes 1179656 | tf_op jit(solution)/shard_map/ppermute | solution.py:47
  84.2 2.4 collective-permute-start.13
  86.6 7.4 %collective-permute-done.12.got_ref = bf16[48,4096]{1,0:T(8,128)(2,1)S(1)} collective-permute-done((bf16[48,4096]{1,0:T(8,128)(2,1)S(1)}, bf16[48,4096]{1,0:T(8,128)(2,1)S(1)}, u32[]{:S(2)}, u32[]{:S(2)}) %collective-permute-start.12) | collective-permute-done | bytes 393248 | tf_op jit(solution)/shard_map/ppermute | solution.py:47
  94.1 4.8 %collective-permute-start.14 = (bf16[24,4096]{1,0:T(8,128)(2,1)S(1)}, bf16[24,4096]{1,0:T(8,128)(2,1)S(1)}, u32[]{:S(2)}, u32[]{:S(2)}) collective-permute-start(bf16[24,4096]{1,0:T(8,128)(2,1)S(1)} %get-tuple-element.55), channel_id=1, source_target_pairs={{0,4},{1,5},{2,6},{3,7},{4,0},{5,1},{6,2},{7,3},{8,12},{9,13},{10,... | collective-permute-start | bytes 589832 | tf_op jit(solution)/shard_map/ppermute | solution.py:47
  98.9 4.3 %collective-permute-done.14.refs_3_ = bf16[24,4096]{1,0:T(8,128)(2,1)S(1)} collective-permute-done((bf16[24,4096]{1,0:T(8,128)(2,1)S(1)}, bf16[24,4096]{1,0:T(8,128)(2,1)S(1)}, u32[]{:S(2)}, u32[]{:S(2)}) %collective-permute-start.14) | collective-permute-done | bytes 196640 | tf_op jit(solution)/shard_map/ppermute | solution.py:47
  104.5 15.5 %all-to-all-start.1 = ((bf16[4,24,2048]{2,1,0:T(8,128)(2,1)}), bf16[4,24,2048]{2,1,0:T(8,128)(2,1)S(1)}, u32[]{:S(2)}, u32[]{:S(2)}) async-start(bf16[4,24,2048]{2,1,0:T(8,128)(2,1)} %bitcast.39), calls=%async_computation.1 | async-start | bytes 786432 | tf_op jit(solution)/shard_map/all_to_all | solution.py:41
  122.0 3.9 %collective-permute-start.4 = (bf16[64,4096]{1,0:T(8,128)(2,1)}, bf16[64,4096]{1,0:T(8,128)(2,1)}, u32[]{:S(2)}, u32[]{:S(2)}) collective-permute-start(bf16[64,4096]{1,0:T(8,128)(2,1)} %copy-done.3), channel_id=1, source_target_pairs={{0,480},{32,0},{64,32},{96,64},{128,96},{160,128},{192,160},{224,1... | collective-permute-start | bytes 1572872 | tf_op jit(solution)/shard_map/ppermute | solution.py:56
  125.9 21.2 %all-to-all-done.1 = bf16[4,24,2048]{2,1,0:T(8,128)(2,1)S(1)} async-done(((bf16[4,24,2048]{2,1,0:T(8,128)(2,1)}), bf16[4,24,2048]{2,1,0:T(8,128)(2,1)S(1)}, u32[]{:S(2)}, u32[]{:S(2)}) %all-to-all-start.1) | async-done | bytes 393248 | tf_op jit(solution)/shard_map/all_to_all | solution.py:41
  148.1 2.0 collective-permute-start.15
  150.1 3.9 %collective-permute-start.16 = (bf16[48,2048]{1,0:T(8,128)(2,1)}, bf16[48,2048]{1,0:T(8,128)(2,1)}, u32[]{:S(2)}, u32[]{:S(2)}) collective-permute-start(bf16[48,2048]{1,0:T(8,128)(2,1)} %get-tuple-element.57), channel_id=1, source_target_pairs={{0,480},{32,0},{64,32},{96,64},{128,96},{160,128},{192,160},{224,1... | collective-permute-start | bytes 589832 | tf_op jit(solution)/shard_map/ppermute | solution.py:56
  156.0 5.4 %collective-permute-done.16.refs_5_ = bf16[48,2048]{1,0:T(8,128)(2,1)} collective-permute-done((bf16[48,2048]{1,0:T(8,128)(2,1)}, bf16[48,2048]{1,0:T(8,128)(2,1)}, u32[]{:S(2)}, u32[]{:S(2)}) %collective-permute-start.16) | collective-permute-done | bytes 196640 | tf_op jit(solution)/shard_map/ppermute | solution.py:56
  161.3 2.5 shard_map.74
  164.8 23.7 %all_to_all.46 = bf16[4,24,2048]{2,1,0:T(8,128)(2,1)S(1)} all-to-all(bf16[4,24,2048]{2,1,0:T(8,128)(2,1)S(1)} %bitcast.40), channel_id=1, replica_groups={{0,8,16,24},{1,9,17,25},{2,10,18,26},{3,11,19,27},{4,12,20,28},{5,13,21..., dimensions={0} | all-to-all | bytes 786432 | tf_op jit(solution)/shard_map/all_to_all | solution.py:41
  192.7 6.4 %collective-permute-done.20.far_ref = bf16[24,4096]{1,0:T(8,128)(2,1)S(1)} collective-permute-done((bf16[24,4096]{1,0:T(8,128)(2,1)S(1)}, bf16[24,4096]{1,0:T(8,128)(2,1)S(1)}, u32[]{:S(2)}, u32[]{:S(2)}) %collective-permute-start.20) | collective-permute-done | bytes 196640 | tf_op jit(solution)/shard_map/ppermute | solution.py:47
  199.1 1.9 collective-permute-start.21
  201.1 8.1 %collective-permute-start.23 = (bf16[48,4096]{1,0:T(8,128)(2,1)S(1)}, bf16[48,4096]{1,0:T(8,128)(2,1)S(1)}, u32[]{:S(2)}, u32[]{:S(2)}) collective-permute-start(bf16[48,4096]{1,0:T(8,128)(2,1)S(1)} %shard_map.80.refs_6_), channel_id=1, source_target_pairs={{0,4},{1,5},{2,6},{3,7},{4,0},{5,1},{6,2},{7,3},{8,12},{9,13},{10,... | collective-permute-start | bytes 1179656 | tf_op jit(solution)/shard_map/ppermute | solution.py:47
  209.9 3.1 %shard_map.78 = (bf16[48,4096]{1,0:T(8,128)(2,1)S(1)}, bf16[48,4096]{1,0:T(8,128)(2,1)S(1)}) custom-call(bf16[4096,128]{1,0:T(8,128)(2,1)S(1)} %bitcast.22, bf16[4096,128]{1,0:T(8,128)(2,1)S(1)} %bitcast.27, bf16[128,4096]{1,0:T(8,128)(2,1)S(1)} %bitcast.32, bf16[4096,128]{1,0:T(8,128)(2,1)} %collective-permute-done.5.refs_3_, ...), custom_call_target="tpu_custom_call" | custom-call | tf_op jit(solution)/shard_map/pallas_call | solution.py:60
  213.0 3.9 %collective-permute-start.22 = (bf16[48,4096]{1,0:T(8,128)(2,1)S(1)}, bf16[48,4096]{1,0:T(8,128)(2,1)S(1)}, u32[]{:S(2)}, u32[]{:S(2)}) collective-permute-start(bf16[48,4096]{1,0:T(8,128)(2,1)S(1)} %get-tuple-element.68), channel_id=1, source_target_pairs={{0,2},{1,3},{2,0},{3,1},{4,6},{5,7},{6,4},{7,5},{8,10},{9,11},{10,... | collective-permute-start | bytes 1179656 | tf_op jit(solution)/shard_map/ppermute | solution.py:47
  217.7 3.1 %shard_map.81 = (bf16[48,4096]{1,0:T(8,128)(2,1)S(1)}, bf16[48,4096]{1,0:T(8,128)(2,1)S(1)}) custom-call(bf16[4096,128]{1,0:T(8,128)(2,1)S(1)} %bitcast.23, bf16[4096,128]{1,0:T(8,128)(2,1)S(1)} %bitcast.28, bf16[128,4096]{1,0:T(8,128)(2,1)S(1)} %bitcast.33, bf16[4096,128]{1,0:T(8,128)(2,1)} %collective-permute-done.5.refs_3_, ...), custom_call_target="tpu_custom_call" | custom-call | tf_op jit(solution)/shard_map/pallas_call | solution.py:60
  220.8 4.8 %collective-permute-start.24 = (bf16[48,4096]{1,0:T(8,128)(2,1)S(1)}, bf16[48,4096]{1,0:T(8,128)(2,1)S(1)}, u32[]{:S(2)}, u32[]{:S(2)}) collective-permute-start(bf16[48,4096]{1,0:T(8,128)(2,1)S(1)} %get-tuple-element.71), channel_id=1, source_target_pairs={{0,2},{1,3},{2,0},{3,1},{4,6},{5,7},{6,4},{7,5},{8,10},{9,11},{10,... | collective-permute-start | bytes 1179656 | tf_op jit(solution)/shard_map/ppermute | solution.py:47
  226.7 5.8 %collective-permute-start.25 = (bf16[24,4096]{1,0:T(8,128)(2,1)S(1)}, bf16[24,4096]{1,0:T(8,128)(2,1)S(1)}, u32[]{:S(2)}, u32[]{:S(2)}) collective-permute-start(bf16[24,4096]{1,0:T(8,128)(2,1)S(1)} %get-tuple-element.73), channel_id=1, source_target_pairs={{0,4},{1,5},{2,6},{3,7},{4,0},{5,1},{6,2},{7,3},{8,12},{9,13},{10,... | collective-permute-start | bytes 589832 | tf_op jit(solution)/shard_map/ppermute | solution.py:47
  232.5 2.9 collective-permute-done.24.got_ref
  235.5 4.7 %collective-permute-start.26 = (bf16[24,4096]{1,0:T(8,128)(2,1)S(1)}, bf16[24,4096]{1,0:T(8,128)(2,1)S(1)}, u32[]{:S(2)}, u32[]{:S(2)}) collective-permute-start(bf16[24,4096]{1,0:T(8,128)(2,1)S(1)} %get-tuple-element.74), channel_id=1, source_target_pairs={{0,4},{1,5},{2,6},{3,7},{4,0},{5,1},{6,2},{7,3},{8,12},{9,13},{10,... | collective-permute-start | bytes 589832 | tf_op jit(solution)/shard_map/ppermute | solution.py:47
  240.2 2.8 collective-permute-done.25.refs_2_
  243.0 4.2 %collective-permute-done.26.refs_3_ = bf16[24,4096]{1,0:T(8,128)(2,1)S(1)} collective-permute-done((bf16[24,4096]{1,0:T(8,128)(2,1)S(1)}, bf16[24,4096]{1,0:T(8,128)(2,1)S(1)}, u32[]{:S(2)}, u32[]{:S(2)}) %collective-permute-start.26) | collective-permute-done | bytes 196640 | tf_op jit(solution)/shard_map/ppermute | solution.py:47
  248.5 8.5 %all-to-all-start.3 = ((bf16[4,24,2048]{2,1,0:T(8,128)(2,1)}), bf16[4,24,2048]{2,1,0:T(8,128)(2,1)S(1)}, u32[]{:S(2)}, u32[]{:S(2)}) async-start(bf16[4,24,2048]{2,1,0:T(8,128)(2,1)} %bitcast.15), calls=%async_computation.3 | async-start | bytes 786432 | tf_op jit(solution)/shard_map/all_to_all | solution.py:41
  257.0 3.3 %collective-permute-start.18 = (bf16[64,4096]{1,0:T(8,128)(2,1)S(1)}, bf16[64,4096]{1,0:T(8,128)(2,1)S(1)}, u32[]{:S(2)}, u32[]{:S(2)}) collective-permute-start(bf16[64,4096]{1,0:T(8,128)(2,1)S(1)} %copy-done.10), channel_id=1, source_target_pairs={{0,32},{32,64},{64,96},{96,128},{128,160},{160,192},{192,224},{224... | collective-permute-start | bytes 1572872 | tf_op jit(solution)/shard_map/ppermute | solution.py:56
  260.3 2.5 collective-permute-start.19
  262.9 13.7 %all-to-all-done.3 = bf16[4,24,2048]{2,1,0:T(8,128)(2,1)S(1)} async-done(((bf16[4,24,2048]{2,1,0:T(8,128)(2,1)}), bf16[4,24,2048]{2,1,0:T(8,128)(2,1)S(1)}, u32[]{:S(2)}, u32[]{:S(2)}) %all-to-all-start.3) | async-done | bytes 393248 | tf_op jit(solution)/shard_map/all_to_all | solution.py:41
  276.8 11.2 %collective-permute-start.27 = (bf16[48,2048]{1,0:T(8,128)(2,1)S(1)}, bf16[48,2048]{1,0:T(8,128)(2,1)S(1)}, u32[]{:S(2)}, u32[]{:S(2)}) collective-permute-start(bf16[48,2048]{1,0:T(8,128)(2,1)S(1)} %get-tuple-element.75), channel_id=1, source_target_pairs={{0,32},{32,64},{64,96},{96,128},{128,160},{160,192},{192,224},{224... | collective-permute-start | bytes 589832 | tf_op jit(solution)/shard_map/ppermute | solution.py:56
  291.2 7.7 %collective-permute-done.28.refs_5_ = bf16[48,2048]{1,0:T(8,128)(2,1)S(1)} collective-permute-done((bf16[48,2048]{1,0:T(8,128)(2,1)S(1)}, bf16[48,2048]{1,0:T(8,128)(2,1)S(1)}, u32[]{:S(2)}, u32[]{:S(2)}) %collective-permute-start.28) | collective-permute-done | bytes 196640 | tf_op jit(solution)/shard_map/ppermute | solution.py:56
  298.9 3.0 shard_map.85
  (79 shorter events, 30.3 us)
Async XLA Ops:
  1.4 20.9 %copy-start.2 = (bf16[1,128,4096]{2,1,0:T(8,128)(2,1)S(1)}, bf16[1,128,4096]{2,1,0:T(8,128)(2,1)}, u32[]{:S(2)}) copy-start(bf16[1,128,4096]{2,1,0:T(8,128)(2,1)} %param.11) | copy-start | bytes 3145732
  2.8 0.8 copy-start.3
  2.8 1.0 copy-start.4
  2.8 15.1 %copy-start = (bf16[1,4096,128]{2,1,0:T(8,128)(2,1)S(1)}, bf16[1,4096,128]{2,1,0:T(8,128)(2,1)}, u32[]{:S(2)}) copy-start(bf16[1,4096,128]{2,1,0:T(8,128)(2,1)} %param.9) | copy-start | bytes 3145732
  2.8 17.0 %copy-start.1 = (bf16[1,4096,128]{2,1,0:T(8,128)(2,1)S(1)}, bf16[1,4096,128]{2,1,0:T(8,128)(2,1)}, u32[]{:S(2)}) copy-start(bf16[1,4096,128]{2,1,0:T(8,128)(2,1)} %param.10) | copy-start | bytes 3145732
  3.8 0.8 copy-start.5
  4.5 19.7 %copy-start.13 = (s32[2,2,64,8]{2,3,1,0:T(8,128)S(1)}, s32[2,2,64,8]{2,3,1,0:T(8,128)}, u32[]{:S(2)}) copy-start(s32[2,2,64,8]{2,3,1,0:T(8,128)} %param.7) | copy-start | bytes 24580
  4.5 39.3 %all-to-all-start = ((bf16[4,24,2048]{2,1,0:T(8,128)(2,1)}), bf16[4,24,2048]{2,1,0:T(8,128)(2,1)S(1)}, u32[]{:S(2)}, u32[]{:S(2)}) async-start(bf16[4,24,2048]{2,1,0:T(8,128)(2,1)} %bitcast.38), calls=%async_computation | async-start | bytes 786432 | tf_op jit(solution)/shard_map/all_to_all | solution.py:41
  17.9 42.9 %collective-permute-start.5 = (bf16[4096,128]{1,0:T(8,128)(2,1)S(1)}, bf16[4096,128]{1,0:T(8,128)(2,1)}, u32[]{:S(2)}, u32[]{:S(2)}) collective-permute-start(bf16[4096,128]{1,0:T(8,128)(2,1)S(1)} %bitcast.19), channel_id=1, source_target_pairs={{0,1},{1,0},{2,3},{3,2},{4,5},{5,4},{6,7},{7,6},{8,9},{9,8},{10,11... | collective-permute-start | bytes 3145736 | tf_op jit(solution)/shard_map/ppermute | solution.py:51
  19.9 41.0 %collective-permute-start.6 = (bf16[4096,128]{1,0:T(8,128)(2,1)S(1)}, bf16[4096,128]{1,0:T(8,128)(2,1)}, u32[]{:S(2)}, u32[]{:S(2)}) collective-permute-start(bf16[4096,128]{1,0:T(8,128)(2,1)S(1)} %bitcast.24), channel_id=1, source_target_pairs={{0,1},{1,0},{2,3},{3,2},{4,5},{5,4},{6,7},{7,6},{8,9},{9,8},{10,11... | collective-permute-start | bytes 3145736 | tf_op jit(solution)/shard_map/ppermute | solution.py:51
  22.3 2.0 copy-start.15
  22.3 38.6 %collective-permute-start.7 = (bf16[128,4096]{1,0:T(8,128)(2,1)S(1)}, bf16[128,4096]{1,0:T(8,128)(2,1)}, u32[]{:S(2)}, u32[]{:S(2)}) collective-permute-start(bf16[128,4096]{1,0:T(8,128)(2,1)S(1)} %bitcast.29), channel_id=1, source_target_pairs={{0,1},{1,0},{2,3},{3,2},{4,5},{5,4},{6,7},{7,6},{8,9},{9,8},{10,11... | collective-permute-start | bytes 3145736 | tf_op jit(solution)/shard_map/ppermute | solution.py:51
  26.3 6.7 %collective-permute-start = (f32[2,64,16]{2,1,0:T(8,128)}, f32[2,64,16]{2,1,0:T(8,128)}, u32[]{:S(2)}, u32[]{:S(2)}) collective-permute-start(f32[2,64,16]{2,1,0:T(8,128)} %bitcast.43), channel_id=1, source_target_pairs={{0,32},{32,64},{64,96},{96,128},{128,160},{160,192},{192,224},{224... | collective-permute-start | bytes 24584 | tf_op jit(solution)/shard_map/ppermute | solution.py:56
  29.1 9.8 %collective-permute-start.1 = (f32[2,64,16]{2,1,0:T(8,128)}, f32[2,64,16]{2,1,0:T(8,128)S(1)}, u32[]{:S(2)}, u32[]{:S(2)}) collective-permute-start(f32[2,64,16]{2,1,0:T(8,128)} %bitcast.44), channel_id=1, source_target_pairs={{0,480},{32,0},{64,32},{96,64},{128,96},{160,128},{192,160},{224,1... | collective-permute-start | bytes 24584 | tf_op jit(solution)/shard_map/ppermute | solution.py:56
  38.8 0.6 copy-start.11
  44.2 10.3 %collective-permute-start.8 = (bf16[24,4096]{1,0:T(8,128)(2,1)S(1)}, bf16[24,4096]{1,0:T(8,128)(2,1)S(1)}, u32[]{:S(2)}, u32[]{:S(2)}) collective-permute-start(bf16[24,4096]{1,0:T(8,128)(2,1)S(1)} %get-tuple-element.47.near_ref), channel_id=1, source_target_pairs={{0,4},{1,5},{2,6},{3,7},{4,0},{5,1},{6,2},{7,3},{8,12},{9,13},{10,... | collective-permute-start | bytes 589832 | tf_op jit(solution)/shard_map/ppermute | solution.py:47
  46.1 12.3 %collective-permute-start.2 = (bf16[24,4096]{1,0:T(8,128)(2,1)S(1)}, bf16[24,4096]{1,0:T(8,128)(2,1)S(1)}, u32[]{:S(2)}, u32[]{:S(2)}) collective-permute-start(bf16[24,4096]{1,0:T(8,128)(2,1)S(1)} %get-tuple-element.44.near_ref), channel_id=1, source_target_pairs={{0,2},{1,3},{2,0},{3,1},{4,6},{5,7},{6,4},{7,5},{8,10},{9,11},{10,... | collective-permute-start | bytes 589832 | tf_op jit(solution)/shard_map/ppermute | solution.py:47
  54.5 14.0 %collective-permute-start.9 = (bf16[48,4096]{1,0:T(8,128)(2,1)S(1)}, bf16[48,4096]{1,0:T(8,128)(2,1)S(1)}, u32[]{:S(2)}, u32[]{:S(2)}) collective-permute-start(bf16[48,4096]{1,0:T(8,128)(2,1)S(1)} %shard_map.66.refs_6_), channel_id=1, source_target_pairs={{0,2},{1,3},{2,0},{3,1},{4,6},{5,7},{6,4},{7,5},{8,10},{9,11},{10,... | collective-permute-start | bytes 1179656 | tf_op jit(solution)/shard_map/ppermute | solution.py:47
  58.4 18.5 %collective-permute-start.11 = (bf16[48,4096]{1,0:T(8,128)(2,1)S(1)}, bf16[48,4096]{1,0:T(8,128)(2,1)S(1)}, u32[]{:S(2)}, u32[]{:S(2)}) collective-permute-start(bf16[48,4096]{1,0:T(8,128)(2,1)S(1)} %shard_map.69.refs_6_), channel_id=1, source_target_pairs={{0,4},{1,5},{2,6},{3,7},{4,0},{5,1},{6,2},{7,3},{8,12},{9,13},{10,... | collective-permute-start | bytes 1179656 | tf_op jit(solution)/shard_map/ppermute | solution.py:47
  71.6 12.5 %collective-permute-start.10 = (bf16[48,4096]{1,0:T(8,128)(2,1)S(1)}, bf16[48,4096]{1,0:T(8,128)(2,1)S(1)}, u32[]{:S(2)}, u32[]{:S(2)}) collective-permute-start(bf16[48,4096]{1,0:T(8,128)(2,1)S(1)} %get-tuple-element.49), channel_id=1, source_target_pairs={{0,2},{1,3},{2,0},{3,1},{4,6},{5,7},{6,4},{7,5},{8,10},{9,11},{10,... | collective-permute-start | bytes 1179656 | tf_op jit(solution)/shard_map/ppermute | solution.py:47
  80.1 13.9 %collective-permute-start.12 = (bf16[48,4096]{1,0:T(8,128)(2,1)S(1)}, bf16[48,4096]{1,0:T(8,128)(2,1)S(1)}, u32[]{:S(2)}, u32[]{:S(2)}) collective-permute-start(bf16[48,4096]{1,0:T(8,128)(2,1)S(1)} %get-tuple-element.52), channel_id=1, source_target_pairs={{0,2},{1,3},{2,0},{3,1},{4,6},{5,7},{6,4},{7,5},{8,10},{9,11},{10,... | collective-permute-start | bytes 1179656 | tf_op jit(solution)/shard_map/ppermute | solution.py:47
  84.2 14.7 %collective-permute-start.13 = (bf16[24,4096]{1,0:T(8,128)(2,1)S(1)}, bf16[24,4096]{1,0:T(8,128)(2,1)S(1)}, u32[]{:S(2)}, u32[]{:S(2)}) collective-permute-start(bf16[24,4096]{1,0:T(8,128)(2,1)S(1)} %get-tuple-element.54), channel_id=1, source_target_pairs={{0,4},{1,5},{2,6},{3,7},{4,0},{5,1},{6,2},{7,3},{8,12},{9,13},{10,... | collective-permute-start | bytes 589832 | tf_op jit(solution)/shard_map/ppermute | solution.py:47
  94.1 9.1 %collective-permute-start.14 = (bf16[24,4096]{1,0:T(8,128)(2,1)S(1)}, bf16[24,4096]{1,0:T(8,128)(2,1)S(1)}, u32[]{:S(2)}, u32[]{:S(2)}) collective-permute-start(bf16[24,4096]{1,0:T(8,128)(2,1)S(1)} %get-tuple-element.55), channel_id=1, source_target_pairs={{0,4},{1,5},{2,6},{3,7},{4,0},{5,1},{6,2},{7,3},{8,12},{9,13},{10,... | collective-permute-start | bytes 589832 | tf_op jit(solution)/shard_map/ppermute | solution.py:47
  103.8 0.8 copy-start.6
  104.5 42.6 %all-to-all-start.1 = ((bf16[4,24,2048]{2,1,0:T(8,128)(2,1)}), bf16[4,24,2048]{2,1,0:T(8,128)(2,1)S(1)}, u32[]{:S(2)}, u32[]{:S(2)}) async-start(bf16[4,24,2048]{2,1,0:T(8,128)(2,1)} %bitcast.39), calls=%async_computation.1 | async-start | bytes 786432 | tf_op jit(solution)/shard_map/all_to_all | solution.py:41
  120.1 34.1 %collective-permute-start.3 = (bf16[64,4096]{1,0:T(8,128)(2,1)}, bf16[64,4096]{1,0:T(8,128)(2,1)}, u32[]{:S(2)}, u32[]{:S(2)}) collective-permute-start(bf16[64,4096]{1,0:T(8,128)(2,1)} %copy-done.4), channel_id=1, source_target_pairs={{0,32},{32,64},{64,96},{96,128},{128,160},{160,192},{192,224},{224... | collective-permute-start | bytes 1572872 | tf_op jit(solution)/shard_map/ppermute | solution.py:56
  122.0 32.2 %collective-permute-start.4 = (bf16[64,4096]{1,0:T(8,128)(2,1)}, bf16[64,4096]{1,0:T(8,128)(2,1)}, u32[]{:S(2)}, u32[]{:S(2)}) collective-permute-start(bf16[64,4096]{1,0:T(8,128)(2,1)} %copy-done.3), channel_id=1, source_target_pairs={{0,480},{32,0},{64,32},{96,64},{128,96},{160,128},{192,160},{224,1... | collective-permute-start | bytes 1572872 | tf_op jit(solution)/shard_map/ppermute | solution.py:56
  147.1 6.9 %copy-start.14 = (s32[1,2,64,8]{2,3,1,0:T(8,128)S(1)}, s32[1,2,64,8]{2,3,1,0:T(8,128)}, u32[]{:S(2)}) copy-start(s32[1,2,64,8]{2,3,1,0:T(8,128)} %get-tuple-element.82) | copy-start | bytes 12292
  148.1 13.3 %copy-start.12 = (f32[2,64,16]{2,1,0:T(8,128)S(1)}, f32[2,64,16]{2,1,0:T(8,128)}, u32[]{:S(2)}) copy-start(f32[2,64,16]{2,1,0:T(8,128)} %copy-done.11) | copy-start | bytes 24580
  148.1 7.9 %collective-permute-start.15 = (bf16[48,2048]{1,0:T(8,128)(2,1)}, bf16[48,2048]{1,0:T(8,128)(2,1)S(1)}, u32[]{:S(2)}, u32[]{:S(2)}) collective-permute-start(bf16[48,2048]{1,0:T(8,128)(2,1)} %get-tuple-element.56), channel_id=1, source_target_pairs={{0,32},{32,64},{64,96},{96,128},{128,160},{160,192},{192,224},{224... | collective-permute-start | bytes 589832 | tf_op jit(solution)/shard_map/ppermute | solution.py:56
  150.1 11.2 %collective-permute-start.16 = (bf16[48,2048]{1,0:T(8,128)(2,1)}, bf16[48,2048]{1,0:T(8,128)(2,1)}, u32[]{:S(2)}, u32[]{:S(2)}) collective-permute-start(bf16[48,2048]{1,0:T(8,128)(2,1)} %get-tuple-element.57), channel_id=1, source_target_pairs={{0,480},{32,0},{64,32},{96,64},{128,96},{160,128},{192,160},{224,1... | collective-permute-start | bytes 589832 | tf_op jit(solution)/shard_map/ppermute | solution.py:56
  163.8 0.8 copy-start.7
  163.8 1.0 copy-start.9
  188.8 10.2 %collective-permute-start.20 = (bf16[24,4096]{1,0:T(8,128)(2,1)S(1)}, bf16[24,4096]{1,0:T(8,128)(2,1)S(1)}, u32[]{:S(2)}, u32[]{:S(2)}) collective-permute-start(bf16[24,4096]{1,0:T(8,128)(2,1)S(1)} %get-tuple-element.66.near_ref), channel_id=1, source_target_pairs={{0,4},{1,5},{2,6},{3,7},{4,0},{5,1},{6,2},{7,3},{8,12},{9,13},{10,... | collective-permute-start | bytes 589832 | tf_op jit(solution)/shard_map/ppermute | solution.py:47
  190.7 10.3 %collective-permute-start.17 = (bf16[24,4096]{1,0:T(8,128)(2,1)S(1)}, bf16[24,4096]{1,0:T(8,128)(2,1)S(1)}, u32[]{:S(2)}, u32[]{:S(2)}) collective-permute-start(bf16[24,4096]{1,0:T(8,128)(2,1)S(1)} %get-tuple-element.63.near_ref), channel_id=1, source_target_pairs={{0,2},{1,3},{2,0},{3,1},{4,6},{5,7},{6,4},{7,5},{8,10},{9,11},{10,... | collective-permute-start | bytes 589832 | tf_op jit(solution)/shard_map/ppermute | solution.py:47
  199.1 10.8 %collective-permute-start.21 = (bf16[48,4096]{1,0:T(8,128)(2,1)S(1)}, bf16[48,4096]{1,0:T(8,128)(2,1)S(1)}, u32[]{:S(2)}, u32[]{:S(2)}) collective-permute-start(bf16[48,4096]{1,0:T(8,128)(2,1)S(1)} %shard_map.77.refs_6_), channel_id=1, source_target_pairs={{0,2},{1,3},{2,0},{3,1},{4,6},{5,7},{6,4},{7,5},{8,10},{9,11},{10,... | collective-permute-start | bytes 1179656 | tf_op jit(solution)/shard_map/ppermute | solution.py:47
  201.1 16.7 %collective-permute-start.23 = (bf16[48,4096]{1,0:T(8,128)(2,1)S(1)}, bf16[48,4096]{1,0:T(8,128)(2,1)S(1)}, u32[]{:S(2)}, u32[]{:S(2)}) collective-permute-start(bf16[48,4096]{1,0:T(8,128)(2,1)S(1)} %shard_map.80.refs_6_), channel_id=1, source_target_pairs={{0,4},{1,5},{2,6},{3,7},{4,0},{5,1},{6,2},{7,3},{8,12},{9,13},{10,... | collective-permute-start | bytes 1179656 | tf_op jit(solution)/shard_map/ppermute | solution.py:47
  213.0 13.6 %collective-permute-start.22 = (bf16[48,4096]{1,0:T(8,128)(2,1)S(1)}, bf16[48,4096]{1,0:T(8,128)(2,1)S(1)}, u32[]{:S(2)}, u32[]{:S(2)}) collective-permute-start(bf16[48,4096]{1,0:T(8,128)(2,1)S(1)} %get-tuple-element.68), channel_id=1, source_target_pairs={{0,2},{1,3},{2,0},{3,1},{4,6},{5,7},{6,4},{7,5},{8,10},{9,11},{10,... | collective-permute-start | bytes 1179656 | tf_op jit(solution)/shard_map/ppermute | solution.py:47
  220.8 14.6 %collective-permute-start.24 = (bf16[48,4096]{1,0:T(8,128)(2,1)S(1)}, bf16[48,4096]{1,0:T(8,128)(2,1)S(1)}, u32[]{:S(2)}, u32[]{:S(2)}) collective-permute-start(bf16[48,4096]{1,0:T(8,128)(2,1)S(1)} %get-tuple-element.71), channel_id=1, source_target_pairs={{0,2},{1,3},{2,0},{3,1},{4,6},{5,7},{6,4},{7,5},{8,10},{9,11},{10,... | collective-permute-start | bytes 1179656 | tf_op jit(solution)/shard_map/ppermute | solution.py:47
  226.7 16.3 %collective-permute-start.25 = (bf16[24,4096]{1,0:T(8,128)(2,1)S(1)}, bf16[24,4096]{1,0:T(8,128)(2,1)S(1)}, u32[]{:S(2)}, u32[]{:S(2)}) collective-permute-start(bf16[24,4096]{1,0:T(8,128)(2,1)S(1)} %get-tuple-element.73), channel_id=1, source_target_pairs={{0,4},{1,5},{2,6},{3,7},{4,0},{5,1},{6,2},{7,3},{8,12},{9,13},{10,... | collective-permute-start | bytes 589832 | tf_op jit(solution)/shard_map/ppermute | solution.py:47
  235.5 11.6 %collective-permute-start.26 = (bf16[24,4096]{1,0:T(8,128)(2,1)S(1)}, bf16[24,4096]{1,0:T(8,128)(2,1)S(1)}, u32[]{:S(2)}, u32[]{:S(2)}) collective-permute-start(bf16[24,4096]{1,0:T(8,128)(2,1)S(1)} %get-tuple-element.74), channel_id=1, source_target_pairs={{0,4},{1,5},{2,6},{3,7},{4,0},{5,1},{6,2},{7,3},{8,12},{9,13},{10,... | collective-permute-start | bytes 589832 | tf_op jit(solution)/shard_map/ppermute | solution.py:47
  247.1 9.9 %copy-start.10 = (bf16[64,4096]{1,0:T(8,128)(2,1)S(1)}, bf16[64,4096]{1,0:T(8,128)(2,1)}, u32[]{:S(2)}) copy-start(bf16[64,4096]{1,0:T(8,128)(2,1)} %copy-done.9) | copy-start | bytes 1572868
  248.5 11.8 %copy-start.8 = (bf16[64,4096]{1,0:T(8,128)(2,1)S(1)}, bf16[64,4096]{1,0:T(8,128)(2,1)}, u32[]{:S(2)}) copy-start(bf16[64,4096]{1,0:T(8,128)(2,1)} %copy-done.7) | copy-start | bytes 1572868
  248.5 28.0 %all-to-all-start.3 = ((bf16[4,24,2048]{2,1,0:T(8,128)(2,1)}), bf16[4,24,2048]{2,1,0:T(8,128)(2,1)S(1)}, u32[]{:S(2)}, u32[]{:S(2)}) async-start(bf16[4,24,2048]{2,1,0:T(8,128)(2,1)} %bitcast.15), calls=%async_computation.3 | async-start | bytes 786432 | tf_op jit(solution)/shard_map/all_to_all | solution.py:41
  257.0 32.9 %collective-permute-start.18 = (bf16[64,4096]{1,0:T(8,128)(2,1)S(1)}, bf16[64,4096]{1,0:T(8,128)(2,1)S(1)}, u32[]{:S(2)}, u32[]{:S(2)}) collective-permute-start(bf16[64,4096]{1,0:T(8,128)(2,1)S(1)} %copy-done.10), channel_id=1, source_target_pairs={{0,32},{32,64},{64,96},{96,128},{128,160},{160,192},{192,224},{224... | collective-permute-start | bytes 1572872 | tf_op jit(solution)/shard_map/ppermute | solution.py:56
  260.3 29.6 %collective-permute-start.19 = (bf16[64,4096]{1,0:T(8,128)(2,1)S(1)}, bf16[64,4096]{1,0:T(8,128)(2,1)S(1)}, u32[]{:S(2)}, u32[]{:S(2)}) collective-permute-start(bf16[64,4096]{1,0:T(8,128)(2,1)S(1)} %copy-done.8), channel_id=1, source_target_pairs={{0,480},{32,0},{64,32},{96,64},{128,96},{160,128},{192,160},{224,1... | collective-permute-start | bytes 1572872 | tf_op jit(solution)/shard_map/ppermute | solution.py:56
  276.8 14.4 %collective-permute-start.27 = (bf16[48,2048]{1,0:T(8,128)(2,1)S(1)}, bf16[48,2048]{1,0:T(8,128)(2,1)S(1)}, u32[]{:S(2)}, u32[]{:S(2)}) collective-permute-start(bf16[48,2048]{1,0:T(8,128)(2,1)S(1)} %get-tuple-element.75), channel_id=1, source_target_pairs={{0,32},{32,64},{64,96},{96,128},{128,160},{160,192},{192,224},{224... | collective-permute-start | bytes 589832 | tf_op jit(solution)/shard_map/ppermute | solution.py:56
  288.0 10.9 %collective-permute-start.28 = (bf16[48,2048]{1,0:T(8,128)(2,1)S(1)}, bf16[48,2048]{1,0:T(8,128)(2,1)S(1)}, u32[]{:S(2)}, u32[]{:S(2)}) collective-permute-start(bf16[48,2048]{1,0:T(8,128)(2,1)S(1)} %get-tuple-element.76), channel_id=1, source_target_pairs={{0,480},{32,0},{64,32},{96,64},{128,96},{160,128},{192,160},{224,1... | collective-permute-start | bytes 589832 | tf_op jit(solution)/shard_map/ppermute | solution.py:56
